TPU v7x, 256 devices: a whole 4x4x8 slice. The times are simulated.
256 devices in a mesh: cplx: 2 (over core), node: 4 (over y), edge: 32 (over z, x).
Axes of the slice: x: 4, y: 4, z: 8, core: 2. Of those that a mesh axis runs over, the one named last changes fastest.
Arguments:
- node_in: bfloat16 [16384, 512], P(('cplx', 'node', 'edge')), parts along dimension 0, may hold values from -6 to 6
- edge_in: bfloat16 [16384, 64, 128], P(('cplx', 'node', 'edge')), parts along dimension 0, may hold values from -6 to 6
- neighbours: int32 [16384, 64], P(('cplx', 'node', 'edge')), parts along dimension 0, may hold values from 0 to 8191
- edge_mask: int32 [16384, 64], P(('cplx', 'node', 'edge')), parts along dimension 0, may hold values 0 or 1
- w_src: bfloat16 [512, 128], replicated, may hold values from -0.25 to 0.25
- w_dst: bfloat16 [512, 128], replicated, may hold values from -0.25 to 0.25
- w_edge_one: bfloat16 [128, 128], replicated, may hold values from -0.5 to 0.5
- w_edge_two: bfloat16 [128, 128], replicated, may hold values from -0.5 to 0.5
- w_edge_three: bfloat16 [128, 128], replicated, may hold values from -0.5 to 0.5
- w_node: bfloat16 [128, 512], replicated, may hold values from -0.5 to 0.5
- node_cot: bfloat16 [16384, 512], P(('cplx', 'node', 'edge')), parts along dimension 0, may hold values from -6 to 6
- edge_cot: bfloat16 [16384, 64, 128], P(('cplx', 'node', 'edge')), parts along dimension 0, may hold values from -6 to 6
Outputs:
- node_out: bfloat16 [16384, 512], P(('cplx', 'node', 'edge')), parts along dimension 0
- edge_out: bfloat16 [16384, 64, 128], P(('cplx', 'node', 'edge')), parts along dimension 0
- grad_node: bfloat16 [16384, 512], P(('cplx', 'node', 'edge')), parts along dimension 0
- grad_edge: bfloat16 [16384, 64, 128], P(('cplx', 'node', 'edge')), parts along dimension 0
- grad_w_src: float32 [1024, 128], P('cplx'), parts along dimension 0
- grad_w_dst: float32 [1024, 128], P('cplx'), parts along dimension 0
- grad_w_edge_one: float32 [256, 128], P('cplx'), parts along dimension 0
- grad_w_edge_two: float32 [256, 128], P('cplx'), parts along dimension 0
- grad_w_edge_three: float32 [256, 128], P('cplx'), parts along dimension 0
- grad_w_node: float32 [256, 512], P('cplx'), parts along dimension 0
There are 2 independent parts, one for each index of `cplx`. A program takes and returns all parts, laid end to end along the dimension named above; an argument that names none is the same for every part. Nothing has to cross between parts.
All inputs are finite; a program needn't handle non-finite values. No bound on the sum of `edge_mask` on one device may be relied on, other than what follows from the above.
Results may differ from a plain program's by a relative error of at most 0.015.
Values may be sent and summed in bfloat16 or wider, within the bound.
No kernel may reach another device: no remote copies, remote signals or barrier semaphores. Data moves between devices by JAX's collectives and lax.ppermute only.
A program may use at most 64 MiB of HBM per device.

v0:
```python
import math

import jax
import jax.numpy as jnp
from jax import lax
from jax.sharding import PartitionSpec as P


def silu_parts(value):
    sigma_val = jax.nn.sigmoid(value)
    return (value * sigma_val, sigma_val * (1.0 + value * (1.0 - sigma_val)))


def shards(
    node_in,
    edge_in,
    neighbours,
    edge_mask,
    w_src,
    w_dst,
    w_edge_one,
    w_edge_two,
    w_edge_three,
    w_node,
    node_cot,
    edge_cot,
):
    row_count, nbr_count, edge_width = edge_in.shape
    agg_scale = 1.0 / math.sqrt(nbr_count)
    src_proj = jnp.dot(node_in, w_src, preferred_element_type=jnp.float32).astype(jnp.bfloat16)
    targets = jnp.dot(
        lax.all_gather(node_in, ("node", "edge"), axis=0, tiled=True),
        w_dst,
        preferred_element_type=jnp.float32,
    ).astype(jnp.bfloat16)
    total = targets.shape[0]
    node_scale = 1.0 / math.sqrt(total)
    edge_scale = 1.0 / math.sqrt(total * nbr_count)
    flat_nbr = neighbours.reshape(-1)
    pulled = jnp.take(targets, flat_nbr, axis=0).reshape(row_count, nbr_count, edge_width)
    flat_edges = edge_in.reshape(row_count * nbr_count, edge_width)
    masked = edge_mask.astype(jnp.float32)[:, :, None]
    pre_one = jnp.dot(flat_edges, w_edge_one, preferred_element_type=jnp.float32).reshape(
        row_count, nbr_count, edge_width
    )
    pre_one = (
        pre_one + src_proj[:, None, :].astype(jnp.float32) + pulled.astype(jnp.float32)
    ).reshape(-1, edge_width)
    act_one_f, deriv_one = silu_parts(pre_one)
    act_one = act_one_f.astype(jnp.bfloat16)
    pre_two = jnp.dot(act_one, w_edge_two, preferred_element_type=jnp.float32)
    act_two_f, deriv_two = silu_parts(pre_two)
    act_two = act_two_f.astype(jnp.bfloat16)
    update = jnp.dot(act_two, w_edge_three, preferred_element_type=jnp.float32).reshape(
        row_count, nbr_count, edge_width
    )
    edge_new = edge_in.astype(jnp.float32) + masked * update
    edge_out = edge_new.astype(jnp.bfloat16)
    aggregate = (jnp.sum(masked * edge_new, axis=1) * agg_scale).astype(jnp.bfloat16)
    node_out = (
        node_in.astype(jnp.float32) + jnp.dot(aggregate, w_node, preferred_element_type=jnp.float32)
    ).astype(jnp.bfloat16)
    node_term = jnp.dot(aggregate.T, node_cot, preferred_element_type=jnp.float32)
    grad_agg = jnp.dot(node_cot, w_node.T, preferred_element_type=jnp.float32)
    grad_new = edge_cot.astype(jnp.float32) + masked * grad_agg[:, None, :] * agg_scale
    grad_upd = (masked * grad_new).astype(jnp.bfloat16).reshape(-1, edge_width)
    grad_pre_two = (
        jnp.dot(grad_upd, w_edge_three.T, preferred_element_type=jnp.float32) * deriv_two
    ).astype(jnp.bfloat16)
    grad_pre_one = (
        jnp.dot(grad_pre_two, w_edge_two.T, preferred_element_type=jnp.float32) * deriv_one
    ).astype(jnp.bfloat16)
    accumulated = (
        jnp.zeros((total, edge_width), jnp.float32)
        .at[flat_nbr]
        .add(grad_pre_one.astype(jnp.float32))
    )
    grad_dst = lax.psum_scatter(
        accumulated, ("node", "edge"), scatter_dimension=0, tiled=True
    ).astype(jnp.bfloat16)
    back_edge = jnp.dot(grad_pre_one, w_edge_one.T, preferred_element_type=jnp.float32).reshape(
        row_count, nbr_count, edge_width
    )
    grad_edge = (grad_new + back_edge).astype(jnp.bfloat16)
    grad_src = jnp.sum(
        grad_pre_one.reshape(row_count, nbr_count, edge_width).astype(jnp.float32), axis=1
    ).astype(jnp.bfloat16)
    term_one = jnp.dot(flat_edges.T, grad_pre_one, preferred_element_type=jnp.float32)
    term_two = jnp.dot(act_one.T, grad_pre_two, preferred_element_type=jnp.float32)
    term_three = jnp.dot(act_two.T, grad_upd, preferred_element_type=jnp.float32)
    term_src = jnp.dot(node_in.T, grad_src, preferred_element_type=jnp.float32)
    term_dst = jnp.dot(node_in.T, grad_dst, preferred_element_type=jnp.float32)
    grad_node = node_cot.astype(jnp.float32) + jnp.dot(
        grad_src, w_src.T, preferred_element_type=jnp.float32
    )
    grad_node = (grad_node + jnp.dot(grad_dst, w_dst.T, preferred_element_type=jnp.float32)).astype(
        jnp.bfloat16
    )
    sum_src, sum_dst, sum_one, sum_two, sum_three, grad_w_node = lax.psum(
        (term_src, term_dst, term_one, term_two, term_three, node_term), ("node", "edge")
    )
    return (
        node_out,
        edge_out,
        grad_node,
        grad_edge,
        sum_src * node_scale,
        sum_dst * node_scale,
        sum_one * edge_scale,
        sum_two * edge_scale,
        sum_three * edge_scale,
        grad_w_node * node_scale,
    )


def solution(mesh):
    in_specs = (
        P(("cplx", "node", "edge"), None),
        P(("cplx", "node", "edge"), None, None),
        P(("cplx", "node", "edge"), None),
        P(("cplx", "node", "edge"), None),
        P(),
        P(),
        P(),
        P(),
        P(),
        P(),
        P(("cplx", "node", "edge"), None),
        P(("cplx", "node", "edge"), None, None),
    )
    out_specs = (
        P(("cplx", "node", "edge"), None),
        P(("cplx", "node", "edge"), None, None),
        P(("cplx", "node", "edge"), None),
        P(("cplx", "node", "edge"), None, None),
        P("cplx", None),
        P("cplx", None),
        P("cplx", None),
        P("cplx", None),
        P("cplx", None),
        P("cplx", None),
    )
    return jax.shard_map(shards, mesh=mesh, in_specs=in_specs, out_specs=out_specs, check_vma=False)
```

profile of v0, /device:TPU:8, one launch (start us, length us, event | category | flops | bytes accessed | tf_op | source)
XLA Modules:
  0.0 1125.9 jit_solution(9651398476849360758)
XLA Ops:
  7.2 0.0 copy-start
  7.2 0.0 all-gather.2.cloned.1.call-start
  7.2 0.7 all-gather.2.cloned.1.call-update
  7.9 0.0 reduce-scatter.2.cloned.1.call-start
  8.0 0.8 reshape.88
  8.8 0.8 convert_element_type.67
  9.6 0.8 compare_and_fusion
  10.4 1.1 fusion.14
  11.5 1.1 fusion.21
  12.6 2.6 multiply_convert_fusion
  15.2 123.1 %all-gather.2.cloned.1.call-done = bf16[8192,512]{1,0:T(8,128)(2,1)} async-done(((bf16[64,512]{1,0:T(8,128)(2,1)}), bf16[8192,512]{1,0:T(8,128)(2,1)}) %all-gather.2.cloned.1.call-update) | async-done | bytes 8388624 | tf_op jit(solution)/shard_map/all_gather | solution.py:32
  138.3 5.7 convolution_convert_fusion
  144.0 0.0 copy-start.1
  144.0 15.0 %gather_fusion = bf16[4096,128]{1,0:T(8,128)(2,1)} fusion(bf16[8192,128]{1,0:T(8,128)(2,1)S(1)} %convolution_convert_fusion, s32[4096]{0:T(1024)S(1)} %broadcast_clamp_fusion), kind=kCustom, calls=%fused_computation | custom fusion | bytes 2113536 | tf_op jit(solution)/shard_map/jit(_take)/gather | solution.py:40
  159.0 1.8 convert_add_fusion
  160.9 0.9 fusion.7
  161.8 1.7 multiply_convert_fusion.1
  163.5 0.9 fusion
  164.5 0.5 bitcast_reduce_fusion
  164.9 0.5 copy-done.8
  165.5 24.6 %scatter_custom_fusion = f32[8192,128]{1,0:T(8,128)} fusion(s32[4096]{0:T(1024)S(1)} %bitcast.76, bf16[4096,128]{1,0:T(8,128)(2,1)S(1)} %get-tuple-element.34, f32[]{:T(128)} %constant.15.clone.1), kind=kCustom, calls=%fused_computation.17 | custom fusion | flops 1048576 | bytes 5242884 | tf_op jit(solution)/shard_map/scatter-add | solution.py:76
  190.0 0.0 reduce-scatter.2.cloned.1.call-update
  190.1 0.0 all-reduce.3.cloned.1.call-start
  190.1 0.4 fusion.22
  190.6 0.7 copy-done.2
  191.3 0.3 copy-done.5
  191.6 2.2 fusion.11
  193.8 0.9 convolution_bitcast_fusion.1
  194.7 0.9 fusion.18
  195.6 1.1 fusion.23
  196.7 1.1 fusion.24
  197.9 1.1 convolution_bitcast_fusion.2
  199.0 612.9 %reduce-scatter.2.cloned.1.call-done = f32[64,128]{1,0:T(8,128)} async-done(((f32[8192,128]{1,0:T(8,128)}), f32[64,128]{1,0:T(8,128)}) %reduce-scatter.2.cloned.1.call-update) | async-done | bytes 32784 | tf_op jit(solution)/shard_map/reduce_scatter | solution.py:78
  811.9 1.7 convolution_bitcast_fusion
  813.5 0.0 all-reduce.3.cloned.1.call-update
  813.6 0.8 fusion.12
  814.3 0.2 convolution_add_fusion.1
  814.5 1.6 fusion.13
  816.1 295.8 %all-reduce.3.cloned.1.call-done = (f32[512,128]{0,1:T(8,128)}, f32[512,128]{0,1:T(8,128)}, f32[128,128]{0,1:T(8,128)}, f32[128,128]{0,1:T(8,128)}, f32[128,128]{0,1:T(8,128)}, /*index=5*/f32[128,512]{1,0:T(8,128)}) async-done(((f32[512,128]{0,1:T(8,128)}, f32[512,128]{0,1:T(8,128)}, f32[128,128]{0,1:T(8,128)}, f32[128,128]{0,1:T(8,128)}, f32[128,128]{0,1:T(8,128)}, /*index=5*/f32[128,512]{1,0:T(8,128)}), ...) | async-done | bytes 983056 | tf_op jit(solution)/shard_map/psum | solution.py:99
  1111.9 1.1 broadcast_multiply_fusion.1
  1113.1 0.8 copy.25
  1113.9 0.8 broadcast_multiply_fusion.5
  1114.7 0.7 copy.26
  1115.5 0.9 broadcast_multiply_fusion.3
  1116.4 0.7 copy.28
  1117.1 0.7 copy.27
  1117.8 0.8 copy.24
  1118.7 0.7 broadcast_multiply_fusion
  (33 shorter events, 0.1 us)
Async XLA Ops:
  7.2 131.1 %copy-start = (bf16[512,128]{1,0:T(8,128)(2,1)S(1)}, bf16[512,128]{1,0:T(8,128)(2,1)}, u32[]{:S(2)}) copy-start(bf16[512,128]{1,0:T(8,128)(2,1)} %param.17) | copy-start | bytes 393220
  7.2 131.1 %all-gather.2.cloned.1.call-start = ((), (), s32[]{:S(2)}) async-start(), calls=%async_computation.1 | async-start | bytes 8454144 | tf_op jit(solution)/shard_map/all_gather | solution.py:32
  7.9 803.9 %reduce-scatter.2.cloned.1.call-start = ((), (), s32[]{:S(2)}) async-start(), calls=%async_computation.2 | async-start | bytes 4227072 | tf_op jit(solution)/shard_map/reduce_scatter | solution.py:78
  144.0 15.1 %copy-start.1 = (bf16[64,64,128]{2,1,0:T(8,128)(2,1)S(1)}, bf16[64,64,128]{2,1,0:T(8,128)(2,1)}, u32[]{:S(2)}) copy-start(bf16[64,64,128]{2,1,0:T(8,128)(2,1)} %param.13) | copy-start | bytes 3145732
  144.0 15.1 %copy-start.15 = (bf16[128,128]{1,0:T(8,128)(2,1)S(1)}, bf16[128,128]{1,0:T(8,128)(2,1)}, u32[]{:S(2)}) copy-start(bf16[128,128]{1,0:T(8,128)(2,1)} %param.18) | copy-start | bytes 98308
  160.9 0.9 copy-start.16
  161.8 1.7 copy-start.3
  161.8 1.7 copy-start.6
  161.8 1.7 copy-start.17
  164.5 1.0 copy-start.8
  190.0 1.2 copy-start.2
  190.1 921.9 %all-reduce.3.cloned.1.call-start = ((), (), s32[]{:S(2)}) async-start(), calls=%async_computation.3 | async-start | bytes 1966080 | tf_op jit(solution)/shard_map/psum | solution.py:99
  190.1 1.5 copy-start.5
  191.6 2.2 copy-start.10
  191.6 3.1 copy-start.11
  191.6 4.0 copy-start.4
  191.6 4.0 copy-start.9
  193.8 3.0 copy-start.7
  197.9 615.7 %copy-start.12 = (bf16[128,512]{1,0:T(8,128)(2,1)S(1)}, bf16[128,512]{1,0:T(8,128)(2,1)}, u32[]{:S(2)}) copy-start(bf16[128,512]{1,0:T(8,128)(2,1)} %param.21) | copy-start | bytes 393220
  197.9 616.5 %copy-start.13 = (bf16[512,128]{1,0:T(8,128)(2,1)S(1)}, bf16[512,128]{1,0:T(8,128)(2,1)}, u32[]{:S(2)}) copy-start(bf16[512,128]{1,0:T(8,128)(2,1)} %param.16) | copy-start | bytes 393220
  1111.9 6.7 copy-start.14
Sparse Core Ops, SparseCore 0:
  11.6 126.5 all-gather.1
  190.2 621.6 reduce-scatter.1
  820.4 291.4 all-reduce.2
where the time goes:
time: 1130 us
  waiting for transfers between devices  1030 us (91%)
  other arithmetic  33.2 us (3%)
  matrix products  24.8 us (2%)
  local copies, waits for them, and re-layouts  21.4 us (2%)
  between operations  13.9 us (1%)
    reduce_scatter x1, waiting for transfers between devices, shards(): lax.psum_scatter(accumulated, ('node', 'edge'), scatter_dimension=0, tile...  613 us
    psum x1, waiting for transfers between devices, shards(): lax.psum((term_src, term_dst, term_one, term_two, term_three, node_term),...  296 us
    all_gather x1, waiting for transfers between devices, shards(): lax.all_gather(node_in, ('node', 'edge'), axis=0, tiled=True)  123 us
    scatter-add x1, other arithmetic, shards(): accumulated = jnp.zeros((total, edge_width), jnp.float32).at[flat_nbr].ad...  24.6 us
  transfers between devices with their start and end apart: 3, of which 3 were waited for; matrix products, arithmetic and copies ran while one was open for 2% of the time, Pallas kernels for 0%

commit v1 on v0

--- a/solution.py
+++ b/solution.py
@@ -3,7 +3,46 @@
 import jax
 import jax.numpy as jnp
 from jax import lax
+from jax.sharding import Mesh
 from jax.sharding import PartitionSpec as P
+
+RING = "z"
+PLANE = ("y", "x")
+ALL = ("y", "z", "x")
+
+
+def exchange(value, axes):
+    return lax.all_to_all(value, axes, 0, 0, tiled=True)
+
+
+def gather_rows(rows):
+    count, width = rows.shape
+    long = lax.axis_size(RING)
+    plane = lax.axis_size("y"), lax.axis_size("x")
+    column = exchange(jnp.broadcast_to(rows[None], (long, count, width)), RING)
+    whole = exchange(jnp.broadcast_to(column[None], (plane[0] * plane[1], *column.shape)), PLANE)
+    whole = whole.reshape(plane[0], plane[1], long, count, width)
+    return whole.transpose(0, 2, 1, 3, 4).reshape(-1, width)
+
+
+def scatter_rows(partial):
+    long = lax.axis_size(RING)
+    plane = lax.axis_size("y"), lax.axis_size("x")
+    width = partial.shape[-1]
+    blocks = partial.astype(jnp.bfloat16).reshape(plane[0], long, plane[1], -1, width)
+    blocks = blocks.transpose(0, 2, 1, 3, 4).reshape(plane[0] * plane[1], -1, width)
+    summed = jnp.sum(exchange(blocks, PLANE).astype(jnp.float32), axis=0)
+    summed = summed.astype(jnp.bfloat16).reshape(long, -1, width)
+    return jnp.sum(exchange(summed, RING).astype(jnp.float32), axis=0)
+
+
+def sum_everywhere(value, parts):
+    rows, width = value.shape
+    height = -(-rows // (parts * 16)) * 16
+    value = jnp.pad(value.astype(jnp.bfloat16), ((0, parts * height - rows), (0, 0)))
+    own = jnp.sum(exchange(value.reshape(parts, height, width), ALL).astype(jnp.float32), axis=0)
+    own = jnp.broadcast_to(own.astype(jnp.bfloat16)[None], (parts, height, width))
+    return exchange(own, ALL).reshape(-1, width)[:rows].astype(jnp.float32)
 
 
 def silu_parts(value):
@@ -28,11 +67,9 @@
     row_count, nbr_count, edge_width = edge_in.shape
     agg_scale = 1.0 / math.sqrt(nbr_count)
     src_proj = jnp.dot(node_in, w_src, preferred_element_type=jnp.float32).astype(jnp.bfloat16)
-    targets = jnp.dot(
-        lax.all_gather(node_in, ("node", "edge"), axis=0, tiled=True),
-        w_dst,
-        preferred_element_type=jnp.float32,
-    ).astype(jnp.bfloat16)
+    targets = gather_rows(
+        jnp.dot(node_in, w_dst, preferred_element_type=jnp.float32).astype(jnp.bfloat16)
+    )
     total = targets.shape[0]
     node_scale = 1.0 / math.sqrt(total)
     edge_scale = 1.0 / math.sqrt(total * nbr_count)
@@ -75,9 +112,7 @@
         .at[flat_nbr]
         .add(grad_pre_one.astype(jnp.float32))
     )
-    grad_dst = lax.psum_scatter(
-        accumulated, ("node", "edge"), scatter_dimension=0, tiled=True
-    ).astype(jnp.bfloat16)
+    grad_dst = scatter_rows(accumulated).astype(jnp.bfloat16)
     back_edge = jnp.dot(grad_pre_one, w_edge_one.T, preferred_element_type=jnp.float32).reshape(
         row_count, nbr_count, edge_width
     )
@@ -96,9 +131,15 @@
     grad_node = (grad_node + jnp.dot(grad_dst, w_dst.T, preferred_element_type=jnp.float32)).astype(
         jnp.bfloat16
     )
-    sum_src, sum_dst, sum_one, sum_two, sum_three, grad_w_node = lax.psum(
-        (term_src, term_dst, term_one, term_two, term_three, node_term), ("node", "edge")
+    terms = (term_src, term_dst, term_one, term_two, term_three, node_term.reshape(-1, edge_width))
+    sums = sum_everywhere(jnp.concatenate(terms, axis=0), total // row_count)
+    starts = [0]
+    for term in terms:
+        starts.append(starts[-1] + term.shape[0])
+    sum_src, sum_dst, sum_one, sum_two, sum_three, grad_w_node = (
+        sums[low:high] for low, high in zip(starts[:-1], starts[1:])
     )
+    grad_w_node = grad_w_node.reshape(node_term.shape)
     return (
         node_out,
         edge_out,
@@ -114,25 +155,30 @@
 
 
 def solution(mesh):
+    shape = mesh.shape
+    outer = shape["node"]
+    inner = outer
+    devices = mesh.devices.reshape(shape["cplx"], outer, shape["edge"] // inner, inner)
+    mesh = Mesh(devices, ("cplx", *ALL))
     in_specs = (
-        P(("cplx", "node", "edge"), None),
-        P(("cplx", "node", "edge"), None, None),
-        P(("cplx", "node", "edge"), None),
-        P(("cplx", "node", "edge"), None),
+        P(("cplx", *ALL), None),
+        P(("cplx", *ALL), None, None),
+        P(("cplx", *ALL), None),
+        P(("cplx", *ALL), None),
         P(),
         P(),
         P(),
         P(),
         P(),
         P(),
-        P(("cplx", "node", "edge"), None),
-        P(("cplx", "node", "edge"), None, None),
+        P(("cplx", *ALL), None),
+        P(("cplx", *ALL), None, None),
     )
     out_specs = (
-        P(("cplx", "node", "edge"), None),
-        P(("cplx", "node", "edge"), None, None),
-        P(("cplx", "node", "edge"), None),
-        P(("cplx", "node", "edge"), None, None),
+        P(("cplx", *ALL), None),
+        P(("cplx", *ALL), None, None),
+        P(("cplx", *ALL), None),
+        P(("cplx", *ALL), None, None),
         P("cplx", None),
         P("cplx", None),
         P("cplx", None),

time: 1130 us -> 222 us (0.20)
  waiting for transfers between devices: 1030 us -> 70.9 us
  starting transfers between devices: 0.12 us -> 34.7 us
  blocking collectives: 0 us -> 24.8 us
  between operations: 13.9 us -> 0.98 us
  local copies, waits for them, and re-layouts: 21.4 us -> 32.8 us
    reduce_scatter x1 -> x0, waiting for transfers between devices: 613 us -> none  [shards(): lax.psum_scatter(accumulated, ('node', 'edge'), scatter_dimension=0, tile...]
    psum x1 -> x0, waiting for transfers between devices: 296 us -> none  [shards(): lax.psum((term_src, term_dst, term_one, term_two, term_three, node_term),...]
    all_gather x1 -> x0, waiting for transfers between devices: 123 us -> none  [shards(): lax.all_gather(node_in, ('node', 'edge'), axis=0, tiled=True)]
    all_to_all x0 -> x5, waiting for transfers between devices: none -> 70.9 us  [exchange(): return lax.all_to_all(value, axes, 0, 0, tiled=True)]
    all_to_all x0 -> x5, starting transfers between devices: none -> 34.7 us  [exchange(): return lax.all_to_all(value, axes, 0, 0, tiled=True)]
    all_to_all x0 -> x1, blocking collectives: none -> 24.8 us  [exchange(): return lax.all_to_all(value, axes, 0, 0, tiled=True)]
  transfers between devices with their start and end apart: 3 -> 5, of which waited for: 3 -> 5; matrix products, arithmetic and copies ran while one was open for 2% -> 8% of each run, Pallas kernels for 0% -> 0%
where the time goes in v1:
time: 222 us; the launch traced here: 221 us
  waiting for transfers between devices  70.9 us (32%)
  other arithmetic  38.8 us (17%)
  starting transfers between devices  34.7 us (16%)
  local copies, waits for them, and re-layouts  32.8 us (15%)
  blocking collectives  24.8 us (11%)
  matrix products  18 us (8%)
    all_to_all x5, waiting for transfers between devices, exchange(): return lax.all_to_all(value, axes, 0, 0, tiled=True)  70.9 us
    all_to_all x5, starting transfers between devices, exchange(): return lax.all_to_all(value, axes, 0, 0, tiled=True)  34.7 us
    all_to_all x1, blocking collectives, exchange(): return lax.all_to_all(value, axes, 0, 0, tiled=True)  24.8 us
    scatter-add x1, other arithmetic, shards(): accumulated = jnp.zeros((total, edge_width), jnp.float32).at[flat_nbr].ad...  24.7 us
    gather x1, local copies, waits for them, and re-layouts, shards(): jnp.take(targets, flat_nbr, axis=0)  15 us
    unnamed x53, local copies, waits for them, and re-layouts  5.33 us
  transfers between devices with their start and end apart: 5, of which 5 were waited for; matrix products, arithmetic and copies ran while one was open for 8% of the time, Pallas kernels for 0%

profile of v1, /device:TPU:8, one launch (start us, length us, event | category | flops | bytes accessed | tf_op | source)
XLA Modules:
  0.0 221.1 jit_solution(12767801599728168162)
XLA Ops:
  0.7 1.1 convolution_convert_fusion.6
  1.8 0.7 broadcast_in_dim.19
  2.5 8.5 %all-to-all-start = ((bf16[8,64,128]{2,1,0:T(8,128)(2,1)}), bf16[8,64,128]{2,1,0:T(8,128)(2,1)S(1)}, u32[]{:S(2)}, u32[]{:S(2)}) async-start(bf16[8,64,128]{2,1,0:T(8,128)(2,1)} %broadcast_in_dim.19), calls=%async_computation | async-start | bytes 262144 | tf_op jit(solution)/shard_map/all_to_all | solution.py:15
  10.9 0.8 reshape.140
  11.8 1.4 convert_element_type.80
  13.2 6.9 %all-to-all-done = bf16[8,64,128]{2,1,0:T(8,128)(2,1)S(1)} async-done(((bf16[8,64,128]{2,1,0:T(8,128)(2,1)}), bf16[8,64,128]{2,1,0:T(8,128)(2,1)S(1)}, u32[]{:S(2)}, u32[]{:S(2)}) %all-to-all-start) | async-done | bytes 131104 | tf_op jit(solution)/shard_map/all_to_all | solution.py:15
  20.0 1.9 broadcast_in_dim.20
  21.9 7.5 %all-to-all-start.1 = ((bf16[16,8,64,128]{3,2,1,0:T(8,128)(2,1)}), bf16[16,8,64,128]{3,2,1,0:T(8,128)(2,1)S(1)}, u32[]{:S(2)}, u32[]{:S(2)}) async-start(bf16[16,8,64,128]{3,2,1,0:T(8,128)(2,1)} %broadcast_in_dim.20), calls=%async_computation.1 | async-start | bytes 4194304 | tf_op jit(solution)/shard_map/all_to_all | solution.py:15
  29.5 1.4 compare_and_fusion
  30.9 0.8 fusion.22
  32.4 2.2 %multiply_convert_fusion = bf16[64,64,128]{2,1,0:T(8,128)(2,1)} fusion(bf16[64,64,128]{2,1,0:T(8,128)(2,1)S(1)} %copy-done.3, f32[64,128]{1,0:T(8,128)S(1)} %fusion.26, f32[64,64]{1,0:T(8,128)} %convert_element_type.80), kind=kLoop, calls=%fused_computation.19 | loop fusion | flops 3145728 | bytes 2146304 | tf_op jit(solution)/shard_map/convert_element_type | solution.py:103
  34.7 21.0 %all-to-all-done.1 = bf16[16,8,64,128]{3,2,1,0:T(8,128)(2,1)S(1)} async-done(((bf16[16,8,64,128]{3,2,1,0:T(8,128)(2,1)}), bf16[16,8,64,128]{3,2,1,0:T(8,128)(2,1)S(1)}, u32[]{:S(2)}, u32[]{:S(2)}) %all-to-all-start.1) | async-done | bytes 2097184 | tf_op jit(solution)/shard_map/all_to_all | solution.py:15
  55.7 1.3 copy-done.2
  57.1 1.8 copy.38
  58.9 15.0 %gather_fusion = bf16[4096,128]{1,0:T(8,128)(2,1)} fusion(bf16[8192,128]{1,0:T(8,128)(2,1)S(1)} %bitcast.93, s32[4096]{0:T(1024)S(1)} %broadcast_clamp_fusion), kind=kCustom, calls=%fused_computation | custom fusion | bytes 2113536 | tf_op jit(solution)/shard_map/jit(_take)/gather | solution.py:77
  74.0 1.9 convert_add_fusion
  75.8 0.9 fusion.7
  76.8 0.7 multiply_convert_fusion.1
  78.4 0.9 fusion
  80.3 24.7 %scatter_custom_fusion = f32[8192,128]{1,0:T(8,128)} fusion(s32[4096]{0:T(1024)} %bitcast.106, bf16[4096,128]{1,0:T(8,128)(2,1)S(1)} %get-tuple-element.24, f32[]{:T(128)} %constant.16.clone.1), kind=kCustom, calls=%fused_computation.16 | custom fusion | flops 1048576 | bytes 5243392 | tf_op jit(solution)/shard_map/scatter-add | solution.py:113
  105.0 2.4 %convert_element_type.97 = bf16[8192,128]{1,0:T(8,128)(2,1)S(1)} convert(f32[8192,128]{1,0:T(8,128)} %scatter_custom_fusion) | non-fusion elementwise | flops 1048576 | bytes 6291456 | tf_op jit(solution)/shard_map/convert_element_type | solution.py:32
  107.4 1.6 copy.39
  108.9 6.7 %all-to-all-start.2 = ((bf16[16,512,128]{2,1,0:T(8,128)(2,1)}), bf16[16,512,128]{2,1,0:T(8,128)(2,1)}, u32[]{:S(2)}, u32[]{:S(2)}) async-start(bf16[16,512,128]{2,1,0:T(8,128)(2,1)} %bitcast.97), calls=%async_computation.2 | async-start | bytes 4194304 | tf_op jit(solution)/shard_map/all_to_all | solution.py:15
  115.7 1.3 fusion.27
  117.0 2.2 fusion.11
  119.8 0.9 convolution_convert_fusion
  120.6 1.6 reshape.150
  122.3 1.7 copy.43
  123.9 19.2 %all-to-all-done.2 = bf16[16,512,128]{2,1,0:T(8,128)(2,1)} async-done(((bf16[16,512,128]{2,1,0:T(8,128)(2,1)}), bf16[16,512,128]{2,1,0:T(8,128)(2,1)}, u32[]{:S(2)}, u32[]{:S(2)}) %all-to-all-start.2) | async-done | bytes 2097184 | tf_op jit(solution)/shard_map/all_to_all | solution.py:15
  143.2 2.6 %reduce_sum.59 = bf16[512,128]{1,0:T(8,128)(2,1)} reduce(bf16[16,512,128]{2,1,0:T(8,128)(2,1)} %all-to-all-done.2, bf16[]{:T(256)} %constant.35.clone.1), dimensions={0}, to_apply=%region_3.4 | reduce | flops 983040 | bytes 2228226 | tf_op jit(solution)/shard_map/reduce_sum | solution.py:34
  145.7 4.0 %all-to-all-start.3 = ((bf16[8,64,128]{2,1,0:T(8,128)(2,1)}), bf16[8,64,128]{2,1,0:T(8,128)(2,1)}, u32[]{:S(2)}, u32[]{:S(2)}) async-start(bf16[8,64,128]{2,1,0:T(8,128)(2,1)} %bitcast.13), calls=%async_computation.3 | async-start | bytes 262144 | tf_op jit(solution)/shard_map/all_to_all | solution.py:15
  149.7 0.9 fusion.13
  150.6 8.2 %all-to-all-done.3 = bf16[8,64,128]{2,1,0:T(8,128)(2,1)} async-done(((bf16[8,64,128]{2,1,0:T(8,128)(2,1)}), bf16[8,64,128]{2,1,0:T(8,128)(2,1)}, u32[]{:S(2)}, u32[]{:S(2)}) %all-to-all-start.3) | async-done | bytes 131104 | tf_op jit(solution)/shard_map/all_to_all | solution.py:15
  158.8 1.5 reduce_sum.60
  160.3 1.7 fusion.15
  162.1 1.1 fusion.21
  163.2 1.1 fusion.19
  164.3 1.1 fusion.18
  165.4 0.7 constant_dynamic-update-slice_fusion
  166.2 1.3 copy.48
  167.5 24.8 %all_to_all.30 = bf16[128,16,128]{2,1,0:T(8,128)(2,1)S(1)} all-to-all(bf16[128,16,128]{2,1,0:T(8,128)(2,1)S(1)} %bitcast.102), channel_id=1, replica_groups=mesh['cplx'=2,'y'=4,'z'=8,'x'=4] {'y','z','x'}, dimensions={0} | all-to-all | bytes 1048576 | tf_op jit(solution)/shard_map/all_to_all | solution.py:15
  192.5 0.9 broadcast_in_dim.40
  193.4 8.0 %all-to-all-start.5 = ((bf16[128,16,128]{2,1,0:T(8,128)(2,1)}), bf16[128,16,128]{2,1,0:T(8,128)(2,1)S(1)}, u32[]{:S(2)}, u32[]{:S(2)}) async-start(bf16[128,16,128]{2,1,0:T(8,128)(2,1)} %broadcast_in_dim.40), calls=%async_computation.5 | async-start | bytes 1048576 | tf_op jit(solution)/shard_map/all_to_all | solution.py:15
  201.5 0.8 fusion.16
  202.4 0.8 fusion.17
  203.2 15.5 %all-to-all-done.5 = bf16[128,16,128]{2,1,0:T(8,128)(2,1)S(1)} async-done(((bf16[128,16,128]{2,1,0:T(8,128)(2,1)}), bf16[128,16,128]{2,1,0:T(8,128)(2,1)S(1)}, u32[]{:S(2)}, u32[]{:S(2)}) %all-to-all-start.5) | async-done | bytes 524320 | tf_op jit(solution)/shard_map/all_to_all | solution.py:15
  218.8 0.9 slice_multiply_fusion
  220.3 0.7 mul.134
  (60 shorter events, 4.4 us)
Async XLA Ops:
  0.6 31.0 %copy-start = (bf16[128,512]{1,0:T(8,128)(2,1)S(1)}, bf16[128,512]{1,0:T(8,128)(2,1)}, u32[]{:S(2)}) copy-start(bf16[128,512]{1,0:T(8,128)(2,1)} %param.21) | copy-start | bytes 393220
  2.5 17.6 %all-to-all-start = ((bf16[8,64,128]{2,1,0:T(8,128)(2,1)}), bf16[8,64,128]{2,1,0:T(8,128)(2,1)S(1)}, u32[]{:S(2)}, u32[]{:S(2)}) async-start(bf16[8,64,128]{2,1,0:T(8,128)(2,1)} %broadcast_in_dim.19), calls=%async_computation | async-start | bytes 262144 | tf_op jit(solution)/shard_map/all_to_all | solution.py:15
  21.9 9.0 %copy-start.11 = (bf16[64,512]{1,0:T(8,128)(2,1)S(1)}, bf16[64,512]{1,0:T(8,128)(2,1)}, u32[]{:S(2)}) copy-start(bf16[64,512]{1,0:T(8,128)(2,1)} %param.12) | copy-start | bytes 196612
  21.9 9.0 %copy-start.13 = (bf16[512,128]{1,0:T(8,128)(2,1)S(1)}, bf16[512,128]{1,0:T(8,128)(2,1)}, u32[]{:S(2)}) copy-start(bf16[512,128]{1,0:T(8,128)(2,1)} %param.16) | copy-start | bytes 393220
  21.9 9.8 %copy-start.12 = (bf16[64,512]{1,0:T(8,128)(2,1)S(1)}, bf16[64,512]{1,0:T(8,128)(2,1)}, u32[]{:S(2)}) copy-start(bf16[64,512]{1,0:T(8,128)(2,1)} %param.22) | copy-start | bytes 196612
  21.9 10.5 %copy-start.3 = (bf16[64,64,128]{2,1,0:T(8,128)(2,1)S(1)}, bf16[64,64,128]{2,1,0:T(8,128)(2,1)}, u32[]{:S(2)}) copy-start(bf16[64,64,128]{2,1,0:T(8,128)(2,1)} %param.23) | copy-start | bytes 3145732
  21.9 33.8 %all-to-all-start.1 = ((bf16[16,8,64,128]{3,2,1,0:T(8,128)(2,1)}), bf16[16,8,64,128]{3,2,1,0:T(8,128)(2,1)S(1)}, u32[]{:S(2)}, u32[]{:S(2)}) async-start(bf16[16,8,64,128]{3,2,1,0:T(8,128)(2,1)} %broadcast_in_dim.20), calls=%async_computation.1 | async-start | bytes 4194304 | tf_op jit(solution)/shard_map/all_to_all | solution.py:15
  29.5 1.4 copy-start.22
  31.8 0.6 copy-start.16
  55.7 1.3 copy-start.2
  58.9 15.0 %copy-start.1 = (bf16[64,64,128]{2,1,0:T(8,128)(2,1)S(1)}, bf16[64,64,128]{2,1,0:T(8,128)(2,1)}, u32[]{:S(2)}) copy-start(bf16[64,64,128]{2,1,0:T(8,128)(2,1)} %param.13) | copy-start | bytes 3145732
  75.8 0.9 copy-start.23
  76.7 1.0 copy-start.5
  76.8 1.6 copy-start.7
  76.8 1.6 copy-start.24
  79.3 1.0 copy-start.9
  108.9 34.2 %all-to-all-start.2 = ((bf16[16,512,128]{2,1,0:T(8,128)(2,1)}), bf16[16,512,128]{2,1,0:T(8,128)(2,1)}, u32[]{:S(2)}, u32[]{:S(2)}) async-start(bf16[16,512,128]{2,1,0:T(8,128)(2,1)} %bitcast.97), calls=%async_computation.2 | async-start | bytes 4194304 | tf_op jit(solution)/shard_map/all_to_all | solution.py:15
  115.6 1.3 copy-start.4
  115.6 1.3 copy-start.17
  115.6 1.3 copy-start.18
  115.6 1.3 copy-start.25
  119.1 0.6 copy-start.19
  145.7 13.1 %all-to-all-start.3 = ((bf16[8,64,128]{2,1,0:T(8,128)(2,1)}), bf16[8,64,128]{2,1,0:T(8,128)(2,1)}, u32[]{:S(2)}, u32[]{:S(2)}) async-start(bf16[8,64,128]{2,1,0:T(8,128)(2,1)} %bitcast.13), calls=%async_computation.3 | async-start | bytes 262144 | tf_op jit(solution)/shard_map/all_to_all | solution.py:15
  160.3 2.9 %copy-start.6 = (bf16[4096,128]{1,0:T(8,128)(2,1)S(1)}, bf16[4096,128]{1,0:T(8,128)(2,1)}, u32[]{:S(2)}) copy-start(bf16[4096,128]{1,0:T(8,128)(2,1)} %copy-done.5) | copy-start | bytes 3145732
  160.3 2.9 %copy-start.10 = (bf16[4096,128]{1,0:T(8,128)(2,1)S(1)}, bf16[4096,128]{1,0:T(8,128)(2,1)}, u32[]{:S(2)}) copy-start(bf16[4096,128]{1,0:T(8,128)(2,1)} %copy-done.9) | copy-start | bytes 3145732
  162.1 2.2 %copy-start.8 = (bf16[64,64,128]{2,1,0:T(8,128)(2,1)S(1)}, bf16[64,64,128]{2,1,0:T(8,128)(2,1)}, u32[]{:S(2)}) copy-start(bf16[64,64,128]{2,1,0:T(8,128)(2,1)} %multiply_convert_fusion) | copy-start | bytes 3145732
  163.2 2.2 %copy-start.15 = (bf16[512,128]{0,1:T(8,128)(2,1)S(1)}, bf16[512,128]{0,1:T(8,128)(2,1)}, u32[]{:S(2)}) copy-start(bf16[512,128]{0,1:T(8,128)(2,1)} %copy.43) | copy-start | bytes 393220
  167.5 34.0 %copy-start.20 = (f32[64,128]{1,0:T(8,128)S(1)}, f32[64,128]{1,0:T(8,128)}, u32[]{:S(2)}) copy-start(f32[64,128]{1,0:T(8,128)} %copy-done.19) | copy-start | bytes 98308
  167.5 34.9 %copy-start.14 = (bf16[512,128]{1,0:T(8,128)(2,1)S(1)}, bf16[512,128]{1,0:T(8,128)(2,1)}, u32[]{:S(2)}) copy-start(bf16[512,128]{1,0:T(8,128)(2,1)} %param.17) | copy-start | bytes 393220
  167.5 34.9 %copy-start.21 = (bf16[64,128]{1,0:T(8,128)(2,1)S(1)}, bf16[64,128]{1,0:T(8,128)(2,1)}, u32[]{:S(2)}) copy-start(bf16[64,128]{1,0:T(8,128)(2,1)} %reduce_sum.60) | copy-start | bytes 49156
  193.4 25.3 %all-to-all-start.5 = ((bf16[128,16,128]{2,1,0:T(8,128)(2,1)}), bf16[128,16,128]{2,1,0:T(8,128)(2,1)S(1)}, u32[]{:S(2)}, u32[]{:S(2)}) async-start(bf16[128,16,128]{2,1,0:T(8,128)(2,1)} %broadcast_in_dim.40), calls=%async_computation.5 | async-start | bytes 1048576 | tf_op jit(solution)/shard_map/all_to_all | solution.py:15

commit v2 on v1

v2 whole, which is shorter than its diff:
```python
import functools
import math

import jax
import jax.numpy as jnp
from jax import lax
from jax.experimental import pallas as pl
from jax.experimental.pallas import tpu as pltpu
from jax.sharding import Mesh
from jax.sharding import PartitionSpec as P

RING = "z"
PLANE = ("y", "x")
ALL = ("y", "z", "x")
SUMS = 4
UNROLL = 32
BLOCK = 512
PIECE = 512


def exchange(value, axes):
    return lax.all_to_all(value, axes, 0, 0, tiled=True)


def spread(value, axes):
    count = math.prod(lax.axis_size(axis) for axis in axes)
    return exchange(jnp.broadcast_to(value[None], (count, *value.shape)), axes)


def sum_first(value):
    return jnp.sum(value.astype(jnp.float32), axis=0)


def deriv(value, sigma_val):
    return sigma_val * (1.0 + value * (1.0 - sigma_val))


def edge_chain_body(
    place_ref,
    table_ref,
    base_ref,
    up_ref,
    weight_ref,
    act_one_ref,
    act_two_ref,
    grad_two_ref,
    grad_one_ref,
    total_ref,
    table,
    pulled,
    grads,
    *sums,
):
    step = pl.program_id(0)
    block = pulled.shape[0]
    count, width = table.shape

    @pl.when(step == 0)
    def _():
        def fill(at, carry):
            rows = pl.ds(pl.multiple_of(at * PIECE, PIECE), PIECE)
            table[rows, :] = table_ref[rows, :].astype(jnp.float32)
            for one in sums:
                one[rows, :] = jnp.zeros((PIECE, width), jnp.float32)
            return carry

        lax.fori_loop(0, count // PIECE, fill, 0)

    first = step * block

    def pull(at, carry):
        low = at * UNROLL
        for k in range(UNROLL):
            place = place_ref[first + low + k]
            pulled[pl.ds(low + k, 1), :] = table[pl.ds(place, 1), :]
        return carry

    lax.fori_loop(0, block // UNROLL, pull, 0)

    pre_one = base_ref[...] + pulled[...]
    sigma_one = jax.nn.sigmoid(pre_one)
    act_one = (pre_one * sigma_one).astype(jnp.bfloat16)
    act_one_ref[...] = act_one
    pre_two = jnp.dot(act_one, weight_ref[...], preferred_element_type=jnp.float32)
    sigma_two = jax.nn.sigmoid(pre_two)
    act_two_ref[...] = (pre_two * sigma_two).astype(jnp.bfloat16)
    grad_two = (up_ref[...] * deriv(pre_two, sigma_two)).astype(jnp.bfloat16)
    grad_two_ref[...] = grad_two
    back = lax.dot_general(
        grad_two,
        weight_ref[...],
        (((1,), (1,)), ((), ())),
        preferred_element_type=jnp.float32,
    )
    grad_one = (back * deriv(pre_one, sigma_one)).astype(jnp.bfloat16)
    grad_one_ref[...] = grad_one
    grads[...] = grad_one.astype(jnp.float32)

    def push(at, carry):
        low = at * UNROLL
        for k in range(UNROLL):
            one = sums[k % SUMS]
            row = pl.ds(place_ref[first + low + k], 1)
            one[row, :] += grads[pl.ds(low + k, 1), :]
        return carry

    lax.fori_loop(0, block // UNROLL, push, 0)

    @pl.when(step == pl.num_programs(0) - 1)
    def _():
        def merge(at, carry):
            rows = pl.ds(pl.multiple_of(at * PIECE, PIECE), PIECE)
            value = sums[0][rows, :]
            for one in sums[1:]:
                value = value + one[rows, :]
            total_ref[rows, :] = value.astype(jnp.bfloat16)
            return carry

        lax.fori_loop(0, count // PIECE, merge, 0)


def edge_chain(places, table, base, up, weight):
    count, width = table.shape
    edges = places.shape[0]
    rows = pl.BlockSpec((BLOCK, width), lambda i, places: (i, 0))

    def whole(shape):
        return pl.BlockSpec(shape, lambda i, places: (0, 0))

    held = pltpu.VMEM((count, width), jnp.float32)
    part = pltpu.VMEM((BLOCK, width), jnp.float32)
    return pl.pallas_call(
        edge_chain_body,
        grid_spec=pltpu.PrefetchScalarGridSpec(
            num_scalar_prefetch=1,
            grid=(edges // BLOCK,),
            in_specs=[whole((count, width)), rows, rows, whole((width, width))],
            out_specs=[rows, rows, rows, rows, whole((count, width))],
            scratch_shapes=[held, part, part] + [held] * SUMS,
        ),
        out_shape=[jax.ShapeDtypeStruct((edges, width), jnp.bfloat16)] * 4
        + [jax.ShapeDtypeStruct((count, width), jnp.bfloat16)],
        compiler_params=pltpu.CompilerParams(vmem_limit_bytes=40 * 1024 * 1024),
        cost_estimate=pl.CostEstimate(
            flops=20 * edges * width * width, bytes_accessed=60 * 2**20, transcendentals=0
        ),
        name="edge_chain",
    )(places, table, base, up, weight)


def shards(
    node_in,
    edge_in,
    neighbours,
    edge_mask,
    w_src,
    w_dst,
    w_edge_one,
    w_edge_two,
    w_edge_three,
    w_node,
    node_cot,
    edge_cot,
):
    row_count, nbr_count, edge_width = edge_in.shape
    bf16, f32 = jnp.bfloat16, jnp.float32
    dot = functools.partial(jnp.dot, preferred_element_type=f32)
    long, deep, wide = lax.axis_size(RING), lax.axis_size("y"), lax.axis_size("x")
    parts = long * deep * wide
    total = parts * row_count
    agg_scale = 1.0 / math.sqrt(nbr_count)
    node_scale = 1.0 / math.sqrt(total)
    edge_scale = 1.0 / math.sqrt(total * nbr_count)

    column = spread(dot(node_in, w_dst).astype(bf16), (RING,)).reshape(-1, edge_width)
    table = spread(column, PLANE).reshape(total, edge_width)
    own_row, rest = neighbours % row_count, neighbours // row_count
    at_x, rest = rest % wide, rest // wide
    at_z, at_y = rest % long, rest // long
    places = (((at_y * wide + at_x) * long + at_z) * row_count + own_row).reshape(-1)

    src_proj = dot(node_in, w_src).astype(bf16)
    flat_edges = edge_in.reshape(row_count * nbr_count, edge_width)
    masked = edge_mask.astype(f32)[:, :, None]
    base = dot(flat_edges, w_edge_one).reshape(row_count, nbr_count, edge_width)
    base = (base + src_proj[:, None, :].astype(f32)).reshape(-1, edge_width)
    grad_agg = dot(node_cot, w_node.T)
    grad_new = edge_cot.astype(f32) + masked * grad_agg[:, None, :] * agg_scale
    grad_upd = (masked * grad_new).astype(bf16).reshape(-1, edge_width)
    grad_up = dot(grad_upd, w_edge_three.T)

    table, base, grad_up, node_late = lax.optimization_barrier((table, base, grad_up, node_in))
    node_column = spread(node_late, (RING,)).reshape(-1, node_in.shape[1])
    act_one, act_two, grad_pre_two, grad_pre_one, partial = edge_chain(
        places, table, base, grad_up, w_edge_two
    )
    act_one, act_two, grad_pre_two, grad_pre_one, node_column, partial = lax.optimization_barrier(
        (act_one, act_two, grad_pre_two, grad_pre_one, node_column, partial)
    )
    arriving = exchange(partial.reshape(deep * wide, -1, edge_width), PLANE)

    update = dot(act_two, w_edge_three).reshape(row_count, nbr_count, edge_width)
    edge_new = edge_in.astype(f32) + masked * update
    edge_out = edge_new.astype(bf16)
    aggregate = (jnp.sum(masked * edge_new, axis=1) * agg_scale).astype(bf16)
    node_out = (node_in.astype(f32) + dot(aggregate, w_node)).astype(bf16)
    back_edge = dot(grad_pre_one, w_edge_one.T).reshape(row_count, nbr_count, edge_width)
    grad_edge = (grad_new + back_edge).astype(bf16)
    grad_src = jnp.sum(
        grad_pre_one.reshape(row_count, nbr_count, edge_width).astype(f32), axis=1
    ).astype(bf16)
    grad_node = node_cot.astype(f32) + dot(grad_src, w_src.T)

    term_node = dot(aggregate.T, node_cot)
    terms = [
        dot(node_in.T, grad_src),
        dot(flat_edges.T, grad_pre_one),
        dot(act_one.T, grad_pre_two),
        dot(act_two.T, grad_upd),
    ]
    terms += [term_node[:, at : at + edge_width] for at in range(0, term_node.shape[1], edge_width)]
    early = jnp.concatenate([term.astype(bf16) for term in terms], axis=0)
    done = (node_out, edge_out, grad_edge, grad_node, early, arriving)
    node_out, edge_out, grad_edge, grad_node, early, arriving = lax.optimization_barrier(done)

    partial = sum_first(arriving).astype(bf16)
    grad_dst = sum_first(exchange(partial.reshape(long, row_count, edge_width), (RING,)))
    grad_dst = grad_dst.astype(bf16)
    terms.append(dot(node_column.T, partial))
    starts = [0]
    for term in terms:
        starts.append(starts[-1] + term.shape[0])
    height = -(-starts[-1] // (parts * 16)) * 16
    blank = jnp.zeros((parts * height - starts[-1], edge_width), bf16)
    packed = jnp.concatenate([early, terms[-1].astype(bf16), blank], axis=0)
    own = sum_first(exchange(packed.reshape(parts, height, edge_width), ALL)).astype(bf16)
    sums = spread(own, ALL).reshape(-1, edge_width).astype(f32)
    sums = [sums[low:high] for low, high in zip(starts[:-1], starts[1:])]

    grad_node = (grad_node + dot(grad_dst, w_dst.T)).astype(bf16)
    return (
        node_out,
        edge_out,
        grad_node,
        grad_edge,
        sums[0] * node_scale,
        sums[-1] * node_scale,
        sums[1] * edge_scale,
        sums[2] * edge_scale,
        sums[3] * edge_scale,
        jnp.concatenate(sums[4:-1], axis=1) * node_scale,
    )


def solution(mesh):
    shape = mesh.shape
    outer = shape["node"]
    inner = outer
    devices = mesh.devices.reshape(shape["cplx"], outer, shape["edge"] // inner, inner)
    mesh = Mesh(devices, ("cplx", *ALL))
    in_specs = (
        P(("cplx", *ALL), None),
        P(("cplx", *ALL), None, None),
        P(("cplx", *ALL), None),
        P(("cplx", *ALL), None),
        P(),
        P(),
        P(),
        P(),
        P(),
        P(),
        P(("cplx", *ALL), None),
        P(("cplx", *ALL), None, None),
    )
    out_specs = (
        P(("cplx", *ALL), None),
        P(("cplx", *ALL), None, None),
        P(("cplx", *ALL), None),
        P(("cplx", *ALL), None, None),
        P("cplx", None),
        P("cplx", None),
        P("cplx", None),
        P("cplx", None),
        P("cplx", None),
        P("cplx", None),
    )
    return jax.shard_map(shards, mesh=mesh, in_specs=in_specs, out_specs=out_specs, check_vma=False)
```

time: 222 us -> 196 us (0.88)
  other arithmetic: 38.8 us -> 8.05 us
  blocking collectives: 24.8 us -> 47 us
  local copies, waits for them, and re-layouts: 32.8 us -> 11.9 us
  Pallas kernels: 0 us -> 16.4 us
  waiting for transfers between devices: 70.9 us -> 64.8 us
  starting transfers between devices: 34.7 us -> 29.2 us
    scatter-add x1 -> x0, other arithmetic: 24.7 us -> none  [shards(): accumulated = jnp.zeros((total, edge_width), jnp.float32).at[flat_nbr].ad...]
    all_to_all x1 -> x2, blocking collectives: 24.8 us -> 47 us  [exchange(): return lax.all_to_all(value, axes, 0, 0, tiled=True)]
    pallas_call x0 -> x1, Pallas kernels: none -> 16.4 us  [edge_chain(): pl.pallas_call(edge_chain_body, grid_spec=pltpu.PrefetchScalarGridSpec(nu...]
    gather x1 -> x0, local copies, waits for them, and re-layouts: 15 us -> none  [shards(): jnp.take(targets, flat_nbr, axis=0)]
    all_to_all x5, waiting for transfers between devices: 70.9 us -> 64.8 us  [exchange(): return lax.all_to_all(value, axes, 0, 0, tiled=True)]
    all_to_all x5, starting transfers between devices: 34.7 us -> 29.2 us  [exchange(): return lax.all_to_all(value, axes, 0, 0, tiled=True)]
    convert_element_type x4 -> x3, other arithmetic: 6.07 us -> 1.84 us  [the longest x1 1.77 us: shards(): grad_upd = (masked * grad_new).astype(bf16).reshape(-1, edge_width)]
    reshape x3 -> x1, local copies, waits for them, and re-layouts: 4.15 us -> 0.07 us  [shards(): (((at_y * wide + at_x) * long + at_z) * row_count + own_row).reshape(-1)]
  transfers between devices with their start and end apart: 5 -> 5, of which waited for: 5 -> 4; matrix products, arithmetic and copies ran while one was open for 8% -> 8% of each run, Pallas kernels for 0% -> 8%
where the time goes in v2:
time: 196 us; the launch traced here: 195 us
  waiting for transfers between devices  64.8 us (33%)
  blocking collectives  47 us (24%)
  starting transfers between devices  29.2 us (15%)
  matrix products  16.5 us (8%)
  Pallas kernels  16.4 us (8%)
  local copies, waits for them, and re-layouts  11.9 us (6%)
  other arithmetic  8.05 us (4%)
    all_to_all x5, waiting for transfers between devices, exchange(): return lax.all_to_all(value, axes, 0, 0, tiled=True)  64.8 us
    all_to_all x2, blocking collectives, exchange(): return lax.all_to_all(value, axes, 0, 0, tiled=True)  47 us
    all_to_all x5, starting transfers between devices, exchange(): return lax.all_to_all(value, axes, 0, 0, tiled=True)  29.2 us
    pallas_call x1, Pallas kernels, edge_chain(): pl.pallas_call(edge_chain_body, grid_spec=pltpu.PrefetchScalarGridSpec(nu...  16.4 us
    unnamed x55, local copies, waits for them, and re-layouts  7.49 us
  transfers between devices with their start and end apart: 5, of which 4 were waited for; matrix products, arithmetic and copies ran while one was open for 8% of the time, Pallas kernels for 8%

profile of v2, /device:TPU:8, one launch (start us, length us, event | category | flops | bytes accessed | tf_op | source)
XLA Modules:
  0.0 194.9 jit_solution(13962286713437355026)
XLA Ops:
  0.7 1.1 convolution_convert_fusion.7
  1.8 17.4 %all_to_all.35 = bf16[8,64,128]{2,1,0:T(8,128)(2,1)S(1)} all-to-all(bf16[8,64,128]{2,1,0:T(8,128)(2,1)S(1)} %broadcast_in_dim.12), channel_id=1, replica_groups=mesh['cplx'=2,'y'=4,'z'=8,'x'=4] {'z'}, dimensions={0} | all-to-all | bytes 262144 | tf_op jit(solution)/shard_map/all_to_all | solution.py:22
  19.2 1.7 broadcast_in_dim.14
  20.9 7.5 %all-to-all-start.1 = ((bf16[16,512,128]{2,1,0:T(8,128)(2,1)}), bf16[16,512,128]{2,1,0:T(8,128)(2,1)S(1)}, u32[]{:S(2)}, u32[]{:S(2)}) async-start(bf16[16,512,128]{2,1,0:T(8,128)(2,1)} %broadcast_in_dim.14), calls=%async_computation.1 | async-start | bytes 4194304 | tf_op jit(solution)/shard_map/all_to_all | solution.py:22
  28.5 0.2 fusion.9
  28.7 0.2 fusion.27
  28.8 1.8 multiply_convert_fusion
  30.7 1.8 fusion.28.up_ref
  32.5 0.2 copy-done.10
  32.6 1.7 convolution_add_fusion
  34.4 20.4 %all-to-all-done.1 = bf16[16,512,128]{2,1,0:T(8,128)(2,1)S(1)} async-done(((bf16[16,512,128]{2,1,0:T(8,128)(2,1)}), bf16[16,512,128]{2,1,0:T(8,128)(2,1)S(1)}, u32[]{:S(2)}, u32[]{:S(2)}) %all-to-all-start.1) | async-done | bytes 2097184 | tf_op jit(solution)/shard_map/all_to_all | solution.py:22
  54.8 0.8 broadcast_in_dim.15
  55.6 4.2 %all-to-all-start.2 = ((bf16[8,64,512]{2,1,0:T(8,128)(2,1)}), bf16[8,64,512]{2,1,0:T(8,128)(2,1)}, u32[]{:S(2)}, u32[]{:S(2)}) async-start(bf16[8,64,512]{2,1,0:T(8,128)(2,1)} %broadcast_in_dim.15), calls=%async_computation.2 | async-start | bytes 1048576 | tf_op jit(solution)/shard_map/all_to_all | solution.py:22
  59.8 0.9 fusion.15
  60.7 0.6 pad.6.clone
  61.3 1.6 copy-done.1
  62.9 1.6 copy-done.2
  64.5 16.4 %edge_chain.1 = (bf16[4096,128]{1,0:T(8,128)(2,1)S(1)}, bf16[4096,128]{1,0:T(8,128)(2,1)S(1)}, bf16[4096,128]{1,0:T(8,128)(2,1)S(1)}, bf16[4096,128]{1,0:T(8,128)(2,1)S(1)}, bf16[8192,128]{1,0:T(8,128)(2,1)}) custom-call(s32[4096]{0:T(1024)S(1)} %reshape.88.place_ref, bf16[8192,128]{1,0:T(8,128)(2,1)S(1)} %bitcast.64, f32[4096,128]{1,0:T(8,128)S(1)} %bitcast.65, ...), custom_call_target="tpu_custom_call" | custom-call | flops 1342177280 | bytes 62914560 | tf_op jit(solution)/shard_map/edge_chain/pallas_call | solution.py:132
  80.9 1.0 copy-done.3
  81.8 1.1 copy-done.5
  82.9 1.1 copy-done.7
  84.0 0.3 bitcast_reduce_fusion
  84.3 1.8 fusion.29
  86.0 0.9 fusion.2
  86.9 6.8 %all-to-all-start.3 = ((bf16[16,512,128]{2,1,0:T(8,128)(2,1)}), bf16[16,512,128]{2,1,0:T(8,128)(2,1)}, u32[]{:S(2)}, u32[]{:S(2)}) async-start(bf16[16,512,128]{2,1,0:T(8,128)(2,1)} %bitcast.12), calls=%async_computation.3 | async-start | bytes 4194304 | tf_op jit(solution)/shard_map/all_to_all | solution.py:22
  93.8 1.1 fusion.8
  95.0 0.3 copy-done.14
  95.3 3.5 %fusion = (bf16[64,64,128]{2,1,0:T(8,128)(2,1)}, f32[64,128]{1,0:T(8,128)S(1)}, bf16[64,64,128]{2,1,0:T(8,128)(2,1)}) fusion(bf16[64,64,128]{2,1,0:T(8,128)(2,1)S(1)} %copy-done.11, f32[64,64]{1,0:T(8,128)S(1)} %convert_element_type.81, f32[64,64,128]{2,1,0:T(8,128)} %bitcast.69, f32[64,128]{1,0:T(8,128)S(1)} %fusion.27, ...), kind=kOutput, calls=%fused_computation.6 | convolution fusion | flops 140500992 | bytes 7454720 | tf_op jit(solution)/shard_map/dot_general | solution.py:202
  98.8 0.2 convolution_convert_fusion.1
  99.1 0.5 fusion.6
  99.6 0.4 copy-done.13
  100.1 0.5 fusion.5
  100.6 0.8 fusion.3
  101.4 0.2 convolution_add_fusion.2
  101.6 19.7 %all-to-all-done.3 = bf16[16,512,128]{2,1,0:T(8,128)(2,1)} async-done(((bf16[16,512,128]{2,1,0:T(8,128)(2,1)}), bf16[16,512,128]{2,1,0:T(8,128)(2,1)}, u32[]{:S(2)}, u32[]{:S(2)}) %all-to-all-start.3) | async-done | bytes 2097184 | tf_op jit(solution)/shard_map/all_to_all | solution.py:22
  121.3 2.6 %reduce_sum.59 = bf16[512,128]{1,0:T(8,128)(2,1)} reduce(bf16[16,512,128]{2,1,0:T(8,128)(2,1)} %all-to-all-done.3, bf16[]{:T(256)} %constant.83.clone.1), dimensions={0}, to_apply=%region_2.3 | reduce | flops 983040 | bytes 2228226 | tf_op jit(solution)/shard_map/reduce_sum | solution.py:31
  123.8 1.3 convolution_convert_fusion
  125.3 0.3 copy.38
  125.6 29.7 %all_to_all.36 = bf16[128,16,128]{2,1,0:T(8,128)(2,1)S(1)} all-to-all(bf16[128,16,128]{2,1,0:T(8,128)(2,1)S(1)} %bitcast.70), channel_id=1, replica_groups=mesh['cplx'=2,'y'=4,'z'=8,'x'=4] {'y','z','x'}, dimensions={0} | all-to-all | bytes 1048576 | tf_op jit(solution)/shard_map/all_to_all | solution.py:22
  155.2 3.8 %all-to-all-start.4 = ((bf16[8,64,128]{2,1,0:T(8,128)(2,1)}), bf16[8,64,128]{2,1,0:T(8,128)(2,1)S(1)}, u32[]{:S(2)}, u32[]{:S(2)}) async-start(bf16[8,64,128]{2,1,0:T(8,128)(2,1)} %bitcast.13), calls=%async_computation.4 | async-start | bytes 262144 | tf_op jit(solution)/shard_map/all_to_all | solution.py:22
  159.2 8.9 %all-to-all-done.4 = bf16[8,64,128]{2,1,0:T(8,128)(2,1)S(1)} async-done(((bf16[8,64,128]{2,1,0:T(8,128)(2,1)}), bf16[8,64,128]{2,1,0:T(8,128)(2,1)S(1)}, u32[]{:S(2)}, u32[]{:S(2)}) %all-to-all-start.4) | async-done | bytes 131104 | tf_op jit(solution)/shard_map/all_to_all | solution.py:22
  168.1 0.9 broadcast_in_dim.17
  169.0 6.9 %all-to-all-start.6 = ((bf16[128,16,128]{2,1,0:T(8,128)(2,1)}), bf16[128,16,128]{2,1,0:T(8,128)(2,1)S(1)}, u32[]{:S(2)}, u32[]{:S(2)}) async-start(bf16[128,16,128]{2,1,0:T(8,128)(2,1)} %broadcast_in_dim.17), calls=%async_computation.6 | async-start | bytes 1048576 | tf_op jit(solution)/shard_map/all_to_all | solution.py:22
  175.9 0.8 fusion.4
  176.7 15.8 %all-to-all-done.6 = bf16[128,16,128]{2,1,0:T(8,128)(2,1)S(1)} async-done(((bf16[128,16,128]{2,1,0:T(8,128)(2,1)}), bf16[128,16,128]{2,1,0:T(8,128)(2,1)S(1)}, u32[]{:S(2)}, u32[]{:S(2)}) %all-to-all-start.6) | async-done | bytes 524320 | tf_op jit(solution)/shard_map/all_to_all | solution.py:22
  192.6 0.8 slice_multiply_fusion
  193.5 0.7 slice_multiply_fusion.2
  194.2 0.7 maximum_multiply_fusion
  (58 shorter events, 0.7 us)
Async XLA Ops:
  0.6 28.0 %copy-start = (bf16[128,512]{1,0:T(8,128)(2,1)S(1)}, bf16[128,512]{1,0:T(8,128)(2,1)}, u32[]{:S(2)}) copy-start(bf16[128,512]{1,0:T(8,128)(2,1)} %param.21) | copy-start | bytes 393220
  20.9 7.6 %copy-start.24 = (s32[64,64]{1,0:T(8,128)S(1)}, s32[64,64]{1,0:T(8,128)}, u32[]{:S(2)}) copy-start(s32[64,64]{1,0:T(8,128)} %param.15) | copy-start | bytes 49156
  20.9 7.6 %copy-start.15 = (bf16[64,512]{1,0:T(8,128)(2,1)S(1)}, bf16[64,512]{1,0:T(8,128)(2,1)}, u32[]{:S(2)}) copy-start(bf16[64,512]{1,0:T(8,128)(2,1)} %param.12) | copy-start | bytes 196612
  20.9 7.6 %copy-start.18 = (bf16[512,128]{1,0:T(8,128)(2,1)S(1)}, bf16[512,128]{1,0:T(8,128)(2,1)}, u32[]{:S(2)}) copy-start(bf16[512,128]{1,0:T(8,128)(2,1)} %param.16) | copy-start | bytes 393220
  20.9 7.8 %copy-start.17 = (bf16[64,512]{1,0:T(8,128)(2,1)S(1)}, bf16[64,512]{1,0:T(8,128)(2,1)}, u32[]{:S(2)}) copy-start(bf16[64,512]{1,0:T(8,128)(2,1)} %param.22) | copy-start | bytes 196612
  20.9 33.8 %all-to-all-start.1 = ((bf16[16,512,128]{2,1,0:T(8,128)(2,1)}), bf16[16,512,128]{2,1,0:T(8,128)(2,1)S(1)}, u32[]{:S(2)}, u32[]{:S(2)}) async-start(bf16[16,512,128]{2,1,0:T(8,128)(2,1)} %broadcast_in_dim.14), calls=%async_computation.1 | async-start | bytes 4194304 | tf_op jit(solution)/shard_map/all_to_all | solution.py:22
  28.5 2.2 %copy-start.22 = (bf16[128,128]{1,0:T(8,128)(2,1)S(1)}, bf16[128,128]{1,0:T(8,128)(2,1)}, u32[]{:S(2)}) copy-start(bf16[128,128]{1,0:T(8,128)(2,1)} %param.20) | copy-start | bytes 98308
  30.6 1.8 copy-start.12
  30.6 2.0 %copy-start.10 = (bf16[64,64,128]{2,1,0:T(8,128)(2,1)S(1)}, bf16[64,64,128]{2,1,0:T(8,128)(2,1)}, u32[]{:S(2)}) copy-start(bf16[64,64,128]{2,1,0:T(8,128)(2,1)} %param.13) | copy-start | bytes 3145732
  30.6 2.0 %copy-start.21 = (bf16[128,128]{1,0:T(8,128)(2,1)S(1)}, bf16[128,128]{1,0:T(8,128)(2,1)}, u32[]{:S(2)}) copy-start(bf16[128,128]{1,0:T(8,128)(2,1)} %param.18) | copy-start | bytes 98308
  32.6 28.7 %copy-start.9 = (bf16[128,128]{1,0:T(8,128)(2,1)S(1)}, bf16[128,128]{1,0:T(8,128)(2,1)}, u32[]{:S(2)}) copy-start(bf16[128,128]{1,0:T(8,128)(2,1)} %weight_ref.1) | copy-start | bytes 98308
  55.6 28.4 %all-to-all-start.2 = ((bf16[8,64,512]{2,1,0:T(8,128)(2,1)}), bf16[8,64,512]{2,1,0:T(8,128)(2,1)}, u32[]{:S(2)}, u32[]{:S(2)}) async-start(bf16[8,64,512]{2,1,0:T(8,128)(2,1)} %broadcast_in_dim.15), calls=%async_computation.2 | async-start | bytes 1048576 | tf_op jit(solution)/shard_map/all_to_all | solution.py:22
  61.3 1.6 copy-start.1
  62.9 1.6 copy-start.2
  80.9 1.0 copy-start.3
  81.8 1.1 copy-start.5
  82.9 1.1 copy-start.7
  86.9 6.9 %copy-start.11 = (bf16[64,64,128]{2,1,0:T(8,128)(2,1)S(1)}, bf16[64,64,128]{2,1,0:T(8,128)(2,1)}, u32[]{:S(2)}) copy-start(bf16[64,64,128]{2,1,0:T(8,128)(2,1)} %param.13) | copy-start | bytes 3145732
  86.9 34.3 %all-to-all-start.3 = ((bf16[16,512,128]{2,1,0:T(8,128)(2,1)}), bf16[16,512,128]{2,1,0:T(8,128)(2,1)}, u32[]{:S(2)}, u32[]{:S(2)}) async-start(bf16[16,512,128]{2,1,0:T(8,128)(2,1)} %bitcast.12), calls=%async_computation.3 | async-start | bytes 4194304 | tf_op jit(solution)/shard_map/all_to_all | solution.py:22
  93.7 1.2 copy-start.4
  93.8 1.5 copy-start.14
  93.8 1.5 copy-start.23
  95.3 3.8 %copy-start.6 = (bf16[4096,128]{1,0:T(8,128)(2,1)S(1)}, bf16[4096,128]{1,0:T(8,128)(2,1)}, u32[]{:S(2)}) copy-start(bf16[4096,128]{1,0:T(8,128)(2,1)} %copy-done.5) | copy-start | bytes 3145732
  95.3 3.8 %copy-start.8 = (bf16[4096,128]{1,0:T(8,128)(2,1)S(1)}, bf16[4096,128]{1,0:T(8,128)(2,1)}, u32[]{:S(2)}) copy-start(bf16[4096,128]{1,0:T(8,128)(2,1)} %copy-done.7) | copy-start | bytes 3145732
  95.3 3.8 %copy-start.16 = (bf16[1408,128]{0,1:T(8,128)(2,1)S(1)}, bf16[1408,128]{0,1:T(8,128)(2,1)}, u32[]{:S(2)}) copy-start(bf16[1408,128]{0,1:T(8,128)(2,1)} %fusion.8) | copy-start | bytes 1081348
  98.8 1.2 copy-start.13
  99.1 2.3 %copy-start.19 = (bf16[512,128]{1,0:T(8,128)(2,1)S(1)}, bf16[512,128]{1,0:T(8,128)(2,1)}, u32[]{:S(2)}) copy-start(bf16[512,128]{1,0:T(8,128)(2,1)} %param.16) | copy-start | bytes 393220
  100.6 24.6 %copy-start.25 = (bf16[2048]{0:T(1024)(128)(2,1)S(1)}, bf16[2048]{0:T(1024)(128)(2,1)}, u32[]{:S(2)}) copy-start(bf16[2048]{0:T(1024)(128)(2,1)} %pad.6.clone) | copy-start | bytes 12292
  125.3 50.6 %copy-start.20 = (bf16[512,128]{1,0:T(8,128)(2,1)S(1)}, bf16[512,128]{1,0:T(8,128)(2,1)}, u32[]{:S(2)}) copy-start(bf16[512,128]{1,0:T(8,128)(2,1)} %param.17) | copy-start | bytes 393220
  155.2 12.9 %all-to-all-start.4 = ((bf16[8,64,128]{2,1,0:T(8,128)(2,1)}), bf16[8,64,128]{2,1,0:T(8,128)(2,1)S(1)}, u32[]{:S(2)}, u32[]{:S(2)}) async-start(bf16[8,64,128]{2,1,0:T(8,128)(2,1)} %bitcast.13), calls=%async_computation.4 | async-start | bytes 262144 | tf_op jit(solution)/shard_map/all_to_all | solution.py:22
  169.0 23.5 %all-to-all-start.6 = ((bf16[128,16,128]{2,1,0:T(8,128)(2,1)}), bf16[128,16,128]{2,1,0:T(8,128)(2,1)S(1)}, u32[]{:S(2)}, u32[]{:S(2)}) async-start(bf16[128,16,128]{2,1,0:T(8,128)(2,1)} %broadcast_in_dim.17), calls=%async_computation.6 | async-start | bytes 1048576 | tf_op jit(solution)/shard_map/all_to_all | solution.py:22

commit v3 on v2

v3 whole, which is shorter than its diff:
```python
import functools
import math

import jax
import jax.numpy as jnp
from jax import lax
from jax.experimental import pallas as pl
from jax.experimental.pallas import tpu as pltpu
from jax.sharding import Mesh
from jax.sharding import PartitionSpec as P

RING = ("z",)
COLUMN = ("y", "z")
PLANE = ("x", "y")
ALL = ("y", "z", "x")
SUMS = 4
UNROLL = 32
BLOCK = 1024
CHUNK = 1024
PIECE = 512


def exchange(value, axes):
    return lax.all_to_all(value, axes, 0, 0, tiled=True)


def spread(value, axes):
    count = math.prod(lax.axis_size(axis) for axis in axes)
    return exchange(jnp.broadcast_to(value[None], (count, *value.shape)), axes)


def sum_first(value):
    return jnp.sum(value.astype(jnp.float32), axis=0)


def deriv(value, sigma_val):
    return sigma_val * (1.0 + value * (1.0 - sigma_val))

def sigmoid(v):
    return 0.5 * jnp.tanh(0.5 * v) + 0.5

def dot(left, right):
    return jnp.dot(left, right, preferred_element_type=jnp.float32)

def dot_turned(left, right):
    return lax.dot_general(left, right, (((1,), (1,)), ((), ())), preferred_element_type=jnp.float32)

def dot_rows(left, right):
    return lax.dot_general(left, right, (((0,), (0,)), ((), ())), preferred_element_type=jnp.float32)

def edge_layer_body(agg_scale,
    place_ref, table_ref, edge_ref, cot_ref, mask_ref, node_ref, node_cot_ref, w_src_ref, one_ref, two_ref, three_ref, w_node_ref,
    edge_out_ref, grad_edge_ref, message_ref, node_out_ref, grad_node_ref,
    table, pulled, grads, src_proj, grad_agg, aggregate, grad_src, early, *sums):
    step = pl.program_id(0)
    block = pulled.shape[0]
    count, width = table.shape
    nodes, deep = node_ref.shape
    nbrs = mask_ref.shape[1]
    groups = block // nbrs
    bf16, f32 = jnp.bfloat16, jnp.float32

    @pl.when(step == 0)
    def _():
        def fill(at, carry):
            rows = pl.ds(pl.multiple_of(at * PIECE, PIECE), PIECE)
            table[rows, :] = table_ref[rows, :].astype(f32)
            for one in sums:
                one[rows, :] = jnp.zeros((PIECE, width), f32)
            return carry
        lax.fori_loop(0, count // PIECE, fill, 0)
        early[...] = jnp.zeros(early.shape, f32)
        src_proj[...] = dot(node_ref[...], w_src_ref[...]).astype(bf16).astype(f32)
        grad_agg[...] = dot_turned(node_cot_ref[...], w_node_ref[...])

    first = step * block

    def pull(at, carry):
        low = at * UNROLL
        for k in range(UNROLL):
            pulled[pl.ds(low + k, 1), :] = table[pl.ds(place_ref[first + low + k], 1), :]
        return carry

    lax.fori_loop(0, block // UNROLL, pull, 0)

    row = pl.multiple_of(step * groups, groups)
    src_rows = src_proj[pl.ds(row, groups), :]
    agg_rows = grad_agg[pl.ds(row, groups), :]
    mask = mask_ref[...].astype(f32).T
    added, grouped = [], []
    per = CHUNK // nbrs
    for low in range(0, block, CHUNK):
        span = pl.ds(low, CHUNK)
        own = range(low // nbrs, low // nbrs + per)
        lay = lambda rows: jnp.concatenate([jnp.broadcast_to(rows[j : j + 1, :], (nbrs, width)) for j in own], axis=0)
        masked = jnp.concatenate([jnp.broadcast_to(mask[:, j : j + 1], (nbrs, width)) for j in own], axis=0)
        edges = edge_ref[span, :]
        grad_new = cot_ref[span, :].astype(f32) + masked * lay(agg_rows) * agg_scale
        grad_upd = (masked * grad_new).astype(bf16)
        pre_one = dot(edges, one_ref[...]) + lay(src_rows) + pulled[span, :]
        sigma_one = sigmoid(pre_one)
        act_one = (pre_one * sigma_one).astype(bf16)
        pre_two = dot(act_one, two_ref[...])
        sigma_two = sigmoid(pre_two)
        act_two = (pre_two * sigma_two).astype(bf16)
        edge_new = edges.astype(f32) + masked * dot(act_two, three_ref[...])
        edge_out_ref[span, :] = edge_new.astype(bf16)
        kept = masked * edge_new
        grad_two = (dot_turned(grad_upd, three_ref[...]) * deriv(pre_two, sigma_two)).astype(bf16)
        grad_one = (dot_turned(grad_two, two_ref[...]) * deriv(pre_one, sigma_one)).astype(bf16)
        grad_wide = grad_one.astype(f32)
        grads[span, :] = grad_wide
        grad_edge_ref[span, :] = (grad_new + dot_turned(grad_one, one_ref[...])).astype(bf16)
        for j in range(per):
            part = slice(j * nbrs, (j + 1) * nbrs)
            added.append(jnp.sum(kept[part], axis=0, keepdims=True))
            grouped.append(jnp.sum(grad_wide[part], axis=0, keepdims=True))
        for at, left, right in ((0, edges, grad_one), (1, act_one, grad_two), (2, act_two, grad_upd)):
            place = pl.ds(deep + at * width, width)
            early[place, :] += dot_rows(left, right)
    aggregate[pl.ds(row, groups), :] = jnp.concatenate(added, axis=0) * agg_scale
    grad_src[pl.ds(row, groups), :] = jnp.concatenate(grouped, axis=0)

    def push(at, carry):
        low = at * UNROLL
        for k in range(UNROLL):
            one = sums[k % len(sums)]
            place = pl.ds(place_ref[first + low + k], 1)
            one[place, :] += grads[pl.ds(low + k, 1), :]
        return carry

    lax.fori_loop(0, block // UNROLL, push, 0)

    @pl.when(step == pl.num_programs(0) - 1)
    def _():
        agg = aggregate[...].astype(bf16)
        node_out_ref[...] = (node_ref[...].astype(f32) + dot(agg, w_node_ref[...])).astype(bf16)
        src = grad_src[...].astype(bf16)
        grad_node_ref[...] = node_cot_ref[...].astype(f32) + dot_turned(src, w_src_ref[...])
        early[pl.ds(0, deep), :] = dot_rows(node_ref[...], src)
        for at in range(0, deep, width):
            early[pl.ds(deep + 3 * width + at, width), :] = dot_rows(agg, node_cot_ref[:, pl.ds(at, width)])
        blocks, height, _ = message_ref.shape
        share = count // blocks
        extra = height - share

        def merge(at, carry):
            rows = pl.ds(pl.multiple_of(at * share, share), share)
            value = sums[0][rows, :]
            for one in sums[1:]:
                value = value + one[rows, :]
            message_ref[at, pl.ds(0, share), :] = value.astype(bf16)
            rows = pl.ds(pl.multiple_of(at * extra, extra), extra)
            message_ref[at, pl.ds(share, extra), :] = early[rows, :].astype(bf16)
            return carry

        lax.fori_loop(0, blocks, merge, 0)


def edge_layer(places, table, edges, cots, mask, node_in, node_cot, w_src, w_one, w_two, w_three, w_node, blocks):
    count, width = table.shape
    total = places.shape[0]
    nodes, nbrs = mask.shape
    deep = node_in.shape[1]
    groups = BLOCK // nbrs
    extra = -(-(2 * deep + 3 * width) // (blocks * 16)) * 16
    f32, bf16 = jnp.float32, jnp.bfloat16
    rows = pl.BlockSpec((BLOCK, width), lambda i, places: (i, 0))
    def whole(*shape):
        return pl.BlockSpec(shape, lambda i, places: (0,) * len(shape))
    held = pltpu.VMEM((count, width), f32)
    part = pltpu.VMEM((BLOCK, width), f32)
    small = pltpu.VMEM((nodes, width), f32)
    return pl.pallas_call(
        functools.partial(edge_layer_body, 1.0 / math.sqrt(nbrs)),
        grid_spec=pltpu.PrefetchScalarGridSpec(
            num_scalar_prefetch=1,
            grid=(total // BLOCK,),
            in_specs=[whole(count, width), rows, rows, pl.BlockSpec((groups, nbrs), lambda i, places: (i, 0)),
              whole(nodes, deep), whole(nodes, deep), whole(deep, width), whole(width, width), whole(width, width), whole(width, width), whole(width, deep)],
            out_specs=[rows, rows, whole(blocks, count // blocks + extra, width), whole(nodes, deep), whole(nodes, deep)],
            scratch_shapes=[held, part, part, small, small, small, small, pltpu.VMEM((blocks * extra, width), f32)] + [held] * SUMS,
        ),
        out_shape=[jax.ShapeDtypeStruct((total, width), bf16)] * 2 + [jax.ShapeDtypeStruct((blocks, count // blocks + extra, width), bf16),
            jax.ShapeDtypeStruct((nodes, deep), bf16), jax.ShapeDtypeStruct((nodes, deep), f32)],
        compiler_params=pltpu.CompilerParams(vmem_limit_bytes=48 * 1024 * 1024),
        name="edge_layer",
    )(places, table, edges, cots, mask, node_in, node_cot, w_src, w_one, w_two, w_three, w_node)


def shards(
    node_in,
    edge_in,
    neighbours,
    edge_mask,
    w_src,
    w_dst,
    w_edge_one,
    w_edge_two,
    w_edge_three,
    w_node,
    node_cot,
    edge_cot,
):
    row_count, nbr_count, width = edge_in.shape
    deep = node_in.shape[1]
    bf16, f32 = jnp.bfloat16, jnp.float32
    long, tall, wide = lax.axis_size("z"), lax.axis_size("y"), lax.axis_size("x")
    blocks = wide * tall
    total = blocks * long * row_count
    node_scale = 1.0 / math.sqrt(total)
    edge_scale = 1.0 / math.sqrt(total * nbr_count)

    column = spread(dot(node_in, w_dst).astype(bf16), COLUMN)
    own_row, rest = neighbours % row_count, neighbours // row_count
    at_x, rest = rest % wide, rest // wide
    places = ((at_x * (tall * long) + rest) * row_count + own_row).reshape(-1)
    column, places, node_late = lax.optimization_barrier((column, places, jnp.concatenate([node_in, node_cot], axis=1)))
    table = spread(column.reshape(-1, width), ("x",)).reshape(total, width)
    node_column = lax.all_gather(node_late, "z", axis=0, tiled=True)

    edge_out, grad_edge, message, node_out, grad_node = edge_layer(
        places,
        table,
        edge_in.reshape(row_count * nbr_count, width),
        edge_cot.reshape(row_count * nbr_count, width),
        edge_mask,
        node_in,
        node_cot,
        w_src,
        w_edge_one,
        w_edge_two,
        w_edge_three,
        w_node,
        blocks,
    )
    share = long * row_count
    arriving = exchange(message, PLANE)
    partial = sum_first(arriving[:, :share]).astype(bf16)
    early = sum_first(arriving[:, share:]).astype(bf16)
    late = dot_rows(node_column[:, :deep], partial).astype(bf16)
    late = sum_first(exchange(late.reshape(blocks, -1, width), PLANE)).astype(bf16)
    extra, rest = early.shape[0], late.shape[0]
    weights = jnp.broadcast_to(jnp.concatenate([early, late])[None], (long, extra + rest, width))
    packed = jnp.concatenate([partial.reshape(long, row_count, width), weights], axis=1)
    own = sum_first(exchange(packed, RING)).astype(bf16)
    grad_node = (grad_node + dot_turned(own[:row_count], w_dst)).astype(bf16)
    sums = spread(own[row_count:], PLANE).astype(f32)
    early = sums[:, :extra].reshape(-1, width)
    late = sums[:, extra:].reshape(-1, width)
    ones = [early[at : at + width] * edge_scale for at in range(deep, deep + 3 * width, width)]
    slabs = [early[at : at + width] for at in range(deep + 3 * width, 2 * deep + 3 * width, width)]
    return (
        node_out,
        edge_out.reshape(edge_in.shape),
        grad_node,
        grad_edge.reshape(edge_in.shape),
        early[:deep] * node_scale,
        late * node_scale,
        *ones,
        jnp.concatenate(slabs, axis=1) * node_scale,
    )


def solution(mesh):
    shape = mesh.shape
    outer = shape["node"]
    inner = outer
    devices = mesh.devices.reshape(shape["cplx"], outer, shape["edge"] // inner, inner)
    mesh = Mesh(devices, ("cplx", *ALL))
    in_specs = (
        P(("cplx", *ALL), None),
        P(("cplx", *ALL), None, None),
        P(("cplx", *ALL), None),
        P(("cplx", *ALL), None),
        P(),
        P(),
        P(),
        P(),
        P(),
        P(),
        P(("cplx", *ALL), None),
        P(("cplx", *ALL), None, None),
    )
    out_specs = (
        P(("cplx", *ALL), None),
        P(("cplx", *ALL), None, None),
        P(("cplx", *ALL), None),
        P(("cplx", *ALL), None, None),
        P("cplx", None),
        P("cplx", None),
        P("cplx", None),
        P("cplx", None),
        P("cplx", None),
        P("cplx", None),
    )
    return jax.shard_map(shards, mesh=mesh, in_specs=in_specs, out_specs=out_specs, check_vma=False)
```

time: 196 us -> 189 us (0.964)
  between operations: 0.97 us -> 14.3 us
  matrix products: 16.5 us -> 3.84 us
  local copies, waits for them, and re-layouts: 11.9 us -> 3.25 us
  waiting for transfers between devices: 64.8 us -> 69.1 us
  blocking collectives: 47 us -> 43.4 us
  Pallas kernels: 16.4 us -> 19.1 us
  other arithmetic: 8.05 us -> 5.78 us
    dot_general x16 -> x3, matrix products: 16.5 us -> 3.84 us  [the longest x1 2.05 us: dot_rows(): lax.dot_general(left, right, (((0,), (0,)), ((), ())), preferred_element_...]
    all_gather x0 -> x1, waiting for transfers between devices: none -> 12.6 us  [shards(): node_column = lax.all_gather(node_late, 'z', axis=0, tiled=True)]
    all_to_all x5 -> x4, waiting for transfers between devices: 64.8 us -> 55.8 us  [exchange(): return lax.all_to_all(value, axes, 0, 0, tiled=True)]
    unnamed x55 -> x22, local copies, waits for them, and re-layouts: 7.49 us -> 0.97 us
    all_to_all x2, blocking collectives: 47 us -> 43.4 us  [exchange(): return lax.all_to_all(value, axes, 0, 0, tiled=True)]
    pallas_call x1, Pallas kernels: 16.4 us -> 19.1 us  [edge_layer(): pl.pallas_call(functools.partial(edge_layer_body, 1.0 / math.sqrt(nbrs)),...]
    reduce_sum x3 -> x4, other arithmetic: 2.73 us -> 0.41 us  [sum_first(): return jnp.sum(value.astype(jnp.float32), axis=0)]
    all_to_all x5 -> x4, starting transfers between devices: 29.2 us -> 29.7 us  [exchange(): return lax.all_to_all(value, axes, 0, 0, tiled=True)]
  transfers between devices with their start and end apart: 5 -> 5, of which waited for: 4 -> 5; matrix products, arithmetic and copies ran while one was open for 8% -> 2% of each run, Pallas kernels for 8% -> 0%
where the time goes in v3:
time: 189 us
  waiting for transfers between devices  69.1 us (37%)
  blocking collectives  43.4 us (23%)
  starting transfers between devices  29.8 us (16%)
  Pallas kernels  19.1 us (10%)
  between operations  14.3 us (8%)
  other arithmetic  5.78 us (3%)
  matrix products  3.84 us (2%)
  local copies, waits for them, and re-layouts  3.25 us (2%)
    all_to_all x4, waiting for transfers between devices, exchange(): return lax.all_to_all(value, axes, 0, 0, tiled=True)  55.8 us
    all_to_all x2, blocking collectives, exchange(): return lax.all_to_all(value, axes, 0, 0, tiled=True)  43.4 us
    all_to_all x4, starting transfers between devices, exchange(): return lax.all_to_all(value, axes, 0, 0, tiled=True)  29.7 us
    pallas_call x1, Pallas kernels, edge_layer(): pl.pallas_call(functools.partial(edge_layer_body, 1.0 / math.sqrt(nbrs)),...  19.1 us
    all_gather x1, waiting for transfers between devices, shards(): node_column = lax.all_gather(node_late, 'z', axis=0, tiled=True)  12.6 us
  transfers between devices with their start and end apart: 5, of which 5 were waited for; matrix products, arithmetic and copies ran while one was open for 2% of the time, Pallas kernels for 0%

profile of v3, /device:TPU:8, one launch (start us, length us, event | category | flops | bytes accessed | tf_op | source)
XLA Modules:
  0.0 188.6 jit_solution(17010344474513541009)
XLA Ops:
  7.2 0.0 copy-start
  7.2 0.9 copy-done
  8.1 1.0 convolution_convert_fusion.1
  9.1 0.9 broadcast_in_dim.10
  10.0 11.7 %all-to-all-start = ((bf16[32,64,128]{2,1,0:T(8,128)(2,1)}), bf16[32,64,128]{2,1,0:T(8,128)(2,1)S(1)}, u32[]{:S(2)}, u32[]{:S(2)}) async-start(bf16[32,64,128]{2,1,0:T(8,128)(2,1)} %broadcast_in_dim.10), calls=%async_computation | async-start | bytes 1048576 | tf_op jit(solution)/shard_map/all_to_all | solution.py:24
  21.7 0.8 fusion.5
  22.5 0.1 reshape.54.place_ref
  22.6 1.5 pad_maximum_fusion.1
  24.1 13.1 %all-to-all-done = bf16[32,64,128]{2,1,0:T(8,128)(2,1)S(1)} async-done(((bf16[32,64,128]{2,1,0:T(8,128)(2,1)}), bf16[32,64,128]{2,1,0:T(8,128)(2,1)S(1)}, u32[]{:S(2)}, u32[]{:S(2)}) %all-to-all-start) | async-done | bytes 524320 | tf_op jit(solution)/shard_map/all_to_all | solution.py:24
  37.2 0.3 broadcast_in_dim.12
  37.5 0.0 copy-start.1
  37.5 0.0 copy-start.2
  37.5 0.0 copy-start.3
  37.5 0.0 copy-start.4
  37.6 0.0 copy-start.5
  37.6 0.0 copy-start.6
  37.6 0.0 copy-start.7
  37.6 0.0 copy-start.8
  37.6 0.0 copy-start.9
  37.6 0.0 copy-start.10
  37.6 27.4 %all_to_all.30 = bf16[4,2048,128]{2,1,0:T(8,128)(2,1)S(1)} all-to-all(bf16[4,2048,128]{2,1,0:T(8,128)(2,1)S(1)} %broadcast_in_dim.12), channel_id=1, replica_groups=mesh['cplx'=2,'y'=4,'z'=8,'x'=4] {'x'}, dimensions={0} | all-to-all | bytes 4194304 | tf_op jit(solution)/shard_map/all_to_all | solution.py:24
  65.0 0.0 copy-done.1
  65.0 0.0 copy-done.2
  65.0 0.0 copy-done.3
  65.0 0.0 copy-done.4
  65.1 19.1 %edge_layer.1 = (bf16[4096,128]{1,0:T(8,128)(2,1)}, bf16[4096,128]{1,0:T(8,128)(2,1)}, bf16[16,608,128]{2,1,0:T(8,128)(2,1)}, bf16[64,512]{1,0:T(8,128)(2,1)}, f32[64,512]{1,0:T(8,128)S(1)}) custom-call(s32[4096]{0:T(1024)S(1)} %reshape.54.place_ref, bf16[8192,128]{1,0:T(8,128)(2,1)S(1)} %bitcast.14, bf16[4096,128]{1,0:T(8,128)(2,1)S(1)} %bitcast.15, ...), custom_call_target="tpu_custom_call" | custom-call | tf_op jit(solution)/shard_map/edge_layer/pallas_call | solution.py:174
  84.2 5.7 %all-to-all-start.2 = ((bf16[16,608,128]{2,1,0:T(8,128)(2,1)}), bf16[16,608,128]{2,1,0:T(8,128)(2,1)S(1)}, u32[]{:S(2)}, u32[]{:S(2)}) async-start(bf16[16,608,128]{2,1,0:T(8,128)(2,1)} %get-tuple-element.23), calls=%async_computation.2 | async-start | bytes 4980736 | tf_op jit(solution)/shard_map/all_to_all | solution.py:24
  89.9 0.0 all-gather.2.cloned.1.call-start
  90.0 0.7 all-gather.2.cloned.1.call-update
  90.7 28.4 %all-to-all-done.2 = bf16[16,608,128]{2,1,0:T(8,128)(2,1)S(1)} async-done(((bf16[16,608,128]{2,1,0:T(8,128)(2,1)}), bf16[16,608,128]{2,1,0:T(8,128)(2,1)S(1)}, u32[]{:S(2)}, u32[]{:S(2)}) %all-to-all-start.2) | async-done | bytes 2490400 | tf_op jit(solution)/shard_map/all_to_all | solution.py:24
  119.1 0.3 slice_reduce_fusion
  119.4 12.6 %all-gather.2.cloned.1.call-done = bf16[512,1024]{1,0:T(8,128)(2,1)} async-done(((bf16[64,1024]{1,0:T(8,128)(2,1)}), bf16[512,1024]{1,0:T(8,128)(2,1)}) %all-gather.2.cloned.1.call-update) | async-done | bytes 1048592 | tf_op jit(solution)/shard_map/all_gather | solution.py:220
  132.0 2.0 %convolution_convert_fusion = bf16[512,128]{1,0:T(8,128)(2,1)} fusion(bf16[512,128]{1,0:T(8,128)(2,1)S(1)} %slice_reduce_fusion, bf16[512,1024]{1,0:T(8,128)(2,1)} %all-gather.2.cloned.1.call-done), kind=kOutput, calls=%fused_computation.1 | convolution fusion | flops 67174400 | bytes 786432 | tf_op jit(solution)/shard_map/dot_general | solution.py:49
  134.1 7.3 %all-to-all-start.3 = ((bf16[16,32,128]{2,1,0:T(8,128)(2,1)}), bf16[16,32,128]{2,1,0:T(8,128)(2,1)S(1)}, u32[]{:S(2)}, u32[]{:S(2)}) async-start(bf16[16,32,128]{2,1,0:T(8,128)(2,1)} %bitcast.6), calls=%async_computation.3 | async-start | bytes 262144 | tf_op jit(solution)/shard_map/all_to_all | solution.py:24
  141.3 0.1 slice_reduce_fusion.1
  141.4 6.3 %all-to-all-done.3 = bf16[16,32,128]{2,1,0:T(8,128)(2,1)S(1)} async-done(((bf16[16,32,128]{2,1,0:T(8,128)(2,1)}), bf16[16,32,128]{2,1,0:T(8,128)(2,1)S(1)}, u32[]{:S(2)}, u32[]{:S(2)}) %all-to-all-start.3) | async-done | bytes 131104 | tf_op jit(solution)/shard_map/all_to_all | solution.py:24
  147.8 16.0 %all_to_all.31 = bf16[8,192,128]{2,1,0:T(8,128)(2,1)S(1)} all-to-all(bf16[8,192,128]{2,1,0:T(8,128)(2,1)S(1)} %pad_maximum_fusion), channel_id=1, replica_groups=mesh['cplx'=2,'y'=4,'z'=8,'x'=4] {'z'}, dimensions={0} | all-to-all | bytes 786432 | tf_op jit(solution)/shard_map/all_to_all | solution.py:24
  163.9 0.1 reduce_sum.51
  164.0 0.9 broadcast_in_dim.14
  164.9 5.1 %all-to-all-start.5 = ((bf16[16,128,128]{2,1,0:T(8,128)(2,1)}), bf16[16,128,128]{2,1,0:T(8,128)(2,1)S(1)}, u32[]{:S(2)}, u32[]{:S(2)}) async-start(bf16[16,128,128]{2,1,0:T(8,128)(2,1)} %broadcast_in_dim.14), calls=%async_computation.5 | async-start | bytes 1048576 | tf_op jit(solution)/shard_map/all_to_all | solution.py:24
  169.9 0.8 fusion
  170.7 7.9 %all-to-all-done.5 = bf16[16,128,128]{2,1,0:T(8,128)(2,1)S(1)} async-done(((bf16[16,128,128]{2,1,0:T(8,128)(2,1)}), bf16[16,128,128]{2,1,0:T(8,128)(2,1)S(1)}, u32[]{:S(2)}, u32[]{:S(2)}) %all-to-all-start.5) | async-done | bytes 524320 | tf_op jit(solution)/shard_map/all_to_all | solution.py:24
  178.7 0.1 slice.65
  178.7 0.7 fusion.13
  179.4 0.7 slice_multiply_fusion.1
  180.1 0.1 convert_element_type.11
  180.2 0.7 slice_multiply_fusion
  181.0 0.7 maximum_multiply_fusion
  (11 shorter events, 0.1 us)
Async XLA Ops:
  7.2 0.9 copy-start
  10.0 27.2 %all-to-all-start = ((bf16[32,64,128]{2,1,0:T(8,128)(2,1)}), bf16[32,64,128]{2,1,0:T(8,128)(2,1)S(1)}, u32[]{:S(2)}, u32[]{:S(2)}) async-start(bf16[32,64,128]{2,1,0:T(8,128)(2,1)} %broadcast_in_dim.10), calls=%async_computation | async-start | bytes 1048576 | tf_op jit(solution)/shard_map/all_to_all | solution.py:24
  37.5 27.5 %copy-start.1 = (bf16[64,64,128]{2,1,0:T(8,128)(2,1)S(1)}, bf16[64,64,128]{2,1,0:T(8,128)(2,1)}, u32[]{:S(2)}) copy-start(bf16[64,64,128]{2,1,0:T(8,128)(2,1)} %param.13) | copy-start | bytes 3145732
  37.5 27.5 %copy-start.2 = (bf16[64,64,128]{2,1,0:T(8,128)(2,1)S(1)}, bf16[64,64,128]{2,1,0:T(8,128)(2,1)}, u32[]{:S(2)}) copy-start(bf16[64,64,128]{2,1,0:T(8,128)(2,1)} %param.23) | copy-start | bytes 3145732
  37.5 27.5 %copy-start.3 = (bf16[64,512]{1,0:T(8,128)(2,1)S(1)}, bf16[64,512]{1,0:T(8,128)(2,1)}, u32[]{:S(2)}) copy-start(bf16[64,512]{1,0:T(8,128)(2,1)} %node_ref.1) | copy-start | bytes 196612
  37.5 27.5 %copy-start.4 = (bf16[64,512]{1,0:T(8,128)(2,1)S(1)}, bf16[64,512]{1,0:T(8,128)(2,1)}, u32[]{:S(2)}) copy-start(bf16[64,512]{1,0:T(8,128)(2,1)} %node_cot_ref.1) | copy-start | bytes 196612
  37.6 27.5 %copy-start.5 = (bf16[512,128]{1,0:T(8,128)(2,1)S(1)}, bf16[512,128]{1,0:T(8,128)(2,1)}, u32[]{:S(2)}) copy-start(bf16[512,128]{1,0:T(8,128)(2,1)} %w_src_ref.1) | copy-start | bytes 393220
  37.6 27.5 %copy-start.6 = (bf16[128,512]{1,0:T(8,128)(2,1)S(1)}, bf16[128,512]{1,0:T(8,128)(2,1)}, u32[]{:S(2)}) copy-start(bf16[128,512]{1,0:T(8,128)(2,1)} %w_node_ref.1) | copy-start | bytes 393220
  37.6 27.5 %copy-start.7 = (s32[64,64]{1,0:T(8,128)S(1)}, s32[64,64]{1,0:T(8,128)}, u32[]{:S(2)}) copy-start(s32[64,64]{1,0:T(8,128)} %mask_ref.1) | copy-start | bytes 49156
  37.6 27.5 %copy-start.8 = (bf16[128,128]{1,0:T(8,128)(2,1)S(1)}, bf16[128,128]{1,0:T(8,128)(2,1)}, u32[]{:S(2)}) copy-start(bf16[128,128]{1,0:T(8,128)(2,1)} %one_ref.1) | copy-start | bytes 98308
  37.6 27.5 %copy-start.9 = (bf16[128,128]{1,0:T(8,128)(2,1)S(1)}, bf16[128,128]{1,0:T(8,128)(2,1)}, u32[]{:S(2)}) copy-start(bf16[128,128]{1,0:T(8,128)(2,1)} %two_ref.1) | copy-start | bytes 98308
  37.6 27.5 %copy-start.10 = (bf16[128,128]{1,0:T(8,128)(2,1)S(1)}, bf16[128,128]{1,0:T(8,128)(2,1)}, u32[]{:S(2)}) copy-start(bf16[128,128]{1,0:T(8,128)(2,1)} %three_ref.1) | copy-start | bytes 98308
  84.2 34.9 %all-to-all-start.2 = ((bf16[16,608,128]{2,1,0:T(8,128)(2,1)}), bf16[16,608,128]{2,1,0:T(8,128)(2,1)S(1)}, u32[]{:S(2)}, u32[]{:S(2)}) async-start(bf16[16,608,128]{2,1,0:T(8,128)(2,1)} %get-tuple-element.23), calls=%async_computation.2 | async-start | bytes 4980736 | tf_op jit(solution)/shard_map/all_to_all | solution.py:24
  89.9 42.1 %all-gather.2.cloned.1.call-start = ((), (), s32[]{:S(2)}) async-start(), calls=%async_computation.6 | async-start | bytes 1179648 | tf_op jit(solution)/shard_map/all_gather | solution.py:220
  134.1 13.6 %all-to-all-start.3 = ((bf16[16,32,128]{2,1,0:T(8,128)(2,1)}), bf16[16,32,128]{2,1,0:T(8,128)(2,1)S(1)}, u32[]{:S(2)}, u32[]{:S(2)}) async-start(bf16[16,32,128]{2,1,0:T(8,128)(2,1)} %bitcast.6), calls=%async_computation.3 | async-start | bytes 262144 | tf_op jit(solution)/shard_map/all_to_all | solution.py:24
  164.9 13.8 %all-to-all-start.5 = ((bf16[16,128,128]{2,1,0:T(8,128)(2,1)}), bf16[16,128,128]{2,1,0:T(8,128)(2,1)S(1)}, u32[]{:S(2)}, u32[]{:S(2)}) async-start(bf16[16,128,128]{2,1,0:T(8,128)(2,1)} %broadcast_in_dim.14), calls=%async_computation.5 | async-start | bytes 1048576 | tf_op jit(solution)/shard_map/all_to_all | solution.py:24
Sparse Core Ops, SparseCore 0:
  93.1 38.8 all-gather.1

commit v4 on v3

v4 whole, which is shorter than its diff:
```python
import functools
import math

import jax
import jax.numpy as jnp
from jax import lax
from jax.experimental import pallas as pl
from jax.experimental.pallas import tpu as pltpu
from jax.sharding import Mesh
from jax.sharding import PartitionSpec as P

RING = ("z",)
COLUMN = ("y", "z")
PLANE = ("x", "y")
ALL = ("y", "z", "x")
SUMS = 4
UNROLL = 32
BLOCK = 1024
SIDE_BLOCK = 1024
PIECE = 512


def exchange(value, axes):
    return lax.all_to_all(value, axes, 0, 0, tiled=True)


def spread(value, axes):
    count = math.prod(lax.axis_size(axis) for axis in axes)
    return exchange(jnp.broadcast_to(value[None], (count, *value.shape)), axes)


def sum_first(value):
    return jnp.sum(value.astype(jnp.float32), axis=0)


def sigmoid(value):
    return 0.5 * jnp.tanh(0.5 * value) + 0.5


def deriv(value, sigma_val):
    return sigma_val * (1.0 + value * (1.0 - sigma_val))


def dot(left, right):
    return jnp.dot(left, right, preferred_element_type=jnp.float32)


def dot_turned(left, right):
    return lax.dot_general(
        left, right, (((1,), (1,)), ((), ())), preferred_element_type=jnp.float32
    )


def dot_rows(left, right):
    return lax.dot_general(
        left, right, (((0,), (0,)), ((), ())), preferred_element_type=jnp.float32
    )


def rows_of(values, count):
    width = values.shape[1]
    rows = [jnp.broadcast_to(values[j : j + 1, :], (count, width)) for j in range(values.shape[0])]
    return jnp.concatenate(rows, axis=0)


def mask_of(mask, width):
    turned = mask.astype(jnp.float32).T
    count = turned.shape[0]
    columns = [jnp.broadcast_to(turned[:, j : j + 1], (count, width)) for j in range(mask.shape[0])]
    return jnp.concatenate(columns, axis=0)


def chain_body(
    agg_scale,
    place_ref,
    table_ref,
    edge_ref,
    cot_ref,
    mask_ref,
    node_ref,
    node_cot_ref,
    w_src_ref,
    one_ref,
    two_ref,
    three_ref,
    w_node_ref,
    act_one_ref,
    act_two_ref,
    grad_two_ref,
    grad_one_ref,
    message_ref,
    table,
    pulled,
    grads,
    src_proj,
    grad_agg,
    *sums,
):
    step = pl.program_id(0)
    block = pulled.shape[0]
    count, width = table.shape
    groups, nbrs = mask_ref.shape
    bf16, f32 = jnp.bfloat16, jnp.float32

    @pl.when(step == 0)
    def _():
        def fill(at, carry):
            rows = pl.ds(pl.multiple_of(at * PIECE, PIECE), PIECE)
            table[rows, :] = table_ref[rows, :].astype(f32)
            for one in sums:
                one[rows, :] = jnp.zeros((PIECE, width), f32)
            return carry

        lax.fori_loop(0, count // PIECE, fill, 0)
        src_proj[...] = dot(node_ref[...], w_src_ref[...]).astype(bf16).astype(f32)
        grad_agg[...] = dot_turned(node_cot_ref[...], w_node_ref[...]) * agg_scale

    first = step * block

    def pull(at, carry):
        low = at * UNROLL
        for k in range(UNROLL):
            pulled[pl.ds(low + k, 1), :] = table[pl.ds(place_ref[first + low + k], 1), :]
        return carry

    lax.fori_loop(0, block // UNROLL, pull, 0)

    row = pl.multiple_of(step * groups, groups)
    masked = mask_of(mask_ref[...], width)
    agg_rows = rows_of(grad_agg[pl.ds(row, groups), :], nbrs)
    grad_upd = (masked * (cot_ref[...].astype(f32) + masked * agg_rows)).astype(bf16)
    pre_one = dot(edge_ref[...], one_ref[...]) + rows_of(src_proj[pl.ds(row, groups), :], nbrs)
    pre_one = pre_one + pulled[...]
    sigma_one = sigmoid(pre_one)
    act_one = (pre_one * sigma_one).astype(bf16)
    act_one_ref[...] = act_one
    pre_two = dot(act_one, two_ref[...])
    sigma_two = sigmoid(pre_two)
    act_two_ref[...] = (pre_two * sigma_two).astype(bf16)
    grad_two = (dot_turned(grad_upd, three_ref[...]) * deriv(pre_two, sigma_two)).astype(bf16)
    grad_two_ref[...] = grad_two
    grad_one = (dot_turned(grad_two, two_ref[...]) * deriv(pre_one, sigma_one)).astype(bf16)
    grad_one_ref[...] = grad_one
    grads[...] = grad_one.astype(f32)

    def push(at, carry):
        low = at * UNROLL
        for k in range(UNROLL):
            one = sums[k % len(sums)]
            place = pl.ds(place_ref[first + low + k], 1)
            one[place, :] += grads[pl.ds(low + k, 1), :]
        return carry

    lax.fori_loop(0, block // UNROLL, push, 0)

    @pl.when(step == pl.num_programs(0) - 1)
    def _():
        def merge(at, carry):
            rows = pl.ds(pl.multiple_of(at * PIECE, PIECE), PIECE)
            value = sums[0][rows, :]
            for one in sums[1:]:
                value = value + one[rows, :]
            message_ref[rows, :] = value.astype(bf16)
            return carry

        lax.fori_loop(0, count // PIECE, merge, 0)


def whole(*shape):
    return pl.BlockSpec(shape, lambda i, *places: (0,) * len(shape))


def edge_chain(
    places, table, edges, cots, mask, node_in, node_cot, w_src, w_one, w_two, w_three, w_node
):
    count, width = table.shape
    total = places.shape[0]
    nodes, nbrs = mask.shape
    deep = node_in.shape[1]
    f32, bf16 = jnp.float32, jnp.bfloat16
    rows = pl.BlockSpec((BLOCK, width), lambda i, places: (i, 0))
    masks = pl.BlockSpec((BLOCK // nbrs, nbrs), lambda i, places: (i, 0))
    square = whole(width, width)
    held = pltpu.VMEM((count, width), f32)
    part = pltpu.VMEM((BLOCK, width), f32)
    small = pltpu.VMEM((nodes, width), f32)
    return pl.pallas_call(
        functools.partial(chain_body, 1.0 / math.sqrt(nbrs)),
        grid_spec=pltpu.PrefetchScalarGridSpec(
            num_scalar_prefetch=1,
            grid=(total // BLOCK,),
            in_specs=[whole(count, width), rows, rows, masks, whole(nodes, deep)]
            + [whole(nodes, deep), whole(deep, width), square, square, square, whole(width, deep)],
            out_specs=[rows] * 4 + [whole(count, width)],
            scratch_shapes=[held, part, part, small, small] + [held] * SUMS,
        ),
        out_shape=[jax.ShapeDtypeStruct((total, width), bf16)] * 4
        + [jax.ShapeDtypeStruct((count, width), bf16)],
        compiler_params=pltpu.CompilerParams(vmem_limit_bytes=44 * 1024 * 1024),
        cost_estimate=pl.CostEstimate(
            flops=8 * total * width * width, bytes_accessed=12 * 2**20, transcendentals=0
        ),
        name="edge_chain",
    )(places, table, edges, cots, mask, node_in, node_cot, w_src, w_one, w_two, w_three, w_node)


def side_body(
    agg_scale,
    edge_ref,
    cot_ref,
    mask_ref,
    act_one_ref,
    act_two_ref,
    grad_two_ref,
    grad_one_ref,
    node_ref,
    node_cot_ref,
    w_src_ref,
    one_ref,
    three_ref,
    w_node_ref,
    edge_out_ref,
    grad_edge_ref,
    early_ref,
    node_out_ref,
    grad_node_ref,
    grad_agg,
    aggregate,
    grad_src,
    terms,
):
    step = pl.program_id(0)
    groups, nbrs = mask_ref.shape
    width = edge_ref.shape[1]
    deep = node_ref.shape[1]
    bf16, f32 = jnp.bfloat16, jnp.float32

    @pl.when(step == 0)
    def _():
        terms[...] = jnp.zeros(terms.shape, f32)
        grad_agg[...] = dot_turned(node_cot_ref[...], w_node_ref[...]) * agg_scale

    row = pl.multiple_of(step * groups, groups)
    masked = mask_of(mask_ref[...], width)
    grad_new = cot_ref[...].astype(f32) + masked * rows_of(grad_agg[pl.ds(row, groups), :], nbrs)
    grad_upd = (masked * grad_new).astype(bf16)
    grad_one = grad_one_ref[...]
    grad_edge_ref[...] = (grad_new + dot_turned(grad_one, one_ref[...])).astype(bf16)
    edges = edge_ref[...]
    act_two = act_two_ref[...]
    edge_new = edges.astype(f32) + masked * dot(act_two, three_ref[...])
    edge_out_ref[...] = edge_new.astype(bf16)
    kept = masked * edge_new
    grad_wide = grad_one.astype(f32)
    added, grouped = [], []
    for j in range(groups):
        part = slice(j * nbrs, (j + 1) * nbrs)
        added.append(jnp.sum(kept[part], axis=0, keepdims=True))
        grouped.append(jnp.sum(grad_wide[part], axis=0, keepdims=True))
    aggregate[pl.ds(row, groups), :] = jnp.concatenate(added, axis=0) * agg_scale
    grad_src[pl.ds(row, groups), :] = jnp.concatenate(grouped, axis=0)
    pairs = ((edges, grad_one), (act_one_ref[...], grad_two_ref[...]), (act_two, grad_upd))
    for at, (left, right) in enumerate(pairs):
        terms[pl.ds(at * width, width), :] += dot_rows(left, right)

    @pl.when(step == pl.num_programs(0) - 1)
    def _():
        agg = aggregate[...].astype(bf16)
        node_out_ref[...] = (node_ref[...].astype(f32) + dot(agg, w_node_ref[...])).astype(bf16)
        src = grad_src[...].astype(bf16)
        grad_node_ref[...] = node_cot_ref[...].astype(f32) + dot_turned(src, w_src_ref[...])
        early_ref[pl.ds(0, deep), :] = dot_rows(node_ref[...], src).astype(bf16)
        early_ref[pl.ds(deep, 3 * width), :] = terms[...].astype(bf16)
        low = deep + 3 * width
        for at in range(0, deep, width):
            slab = dot_rows(agg, node_cot_ref[:, pl.ds(at, width)])
            early_ref[pl.ds(low + at, width), :] = slab.astype(bf16)
        low = low + deep
        rest = early_ref.shape[0] - low
        early_ref[pl.ds(low, rest), :] = jnp.zeros((rest, width), bf16)


def edge_side(
    edges, cots, mask, chain, node_in, node_cot, w_src, w_one, w_three, w_node, early_rows
):
    total, width = edges.shape
    nodes, nbrs = mask.shape
    deep = node_in.shape[1]
    f32, bf16 = jnp.float32, jnp.bfloat16
    rows = pl.BlockSpec((SIDE_BLOCK, width), lambda i: (i, 0))
    masks = pl.BlockSpec((SIDE_BLOCK // nbrs, nbrs), lambda i: (i, 0))
    square = whole(width, width)
    small = pltpu.VMEM((nodes, width), f32)
    return pl.pallas_call(
        functools.partial(side_body, 1.0 / math.sqrt(nbrs)),
        grid=(total // SIDE_BLOCK,),
        in_specs=[rows, rows, masks] + [rows] * 4 + [whole(nodes, deep), whole(nodes, deep)]
        + [whole(deep, width), square, square, whole(width, deep)],
        out_specs=[rows, rows, whole(early_rows, width), whole(nodes, deep), whole(nodes, deep)],
        scratch_shapes=[small, small, small, pltpu.VMEM((3 * width, width), f32)],
        out_shape=[jax.ShapeDtypeStruct((total, width), bf16)] * 2
        + [jax.ShapeDtypeStruct((early_rows, width), bf16)]
        + [jax.ShapeDtypeStruct((nodes, deep), bf16), jax.ShapeDtypeStruct((nodes, deep), f32)],
        compiler_params=pltpu.CompilerParams(vmem_limit_bytes=24 * 1024 * 1024),
        cost_estimate=pl.CostEstimate(
            flops=10 * total * width * width, bytes_accessed=24 * 2**20, transcendentals=0
        ),
        name="edge_side",
    )(edges, cots, mask, *chain, node_in, node_cot, w_src, w_one, w_three, w_node)


def meet_body(arriving_ref, node_ref, early_ref, partial_ref, message_ref):
    blocks, share, width = arriving_ref.shape
    bf16, f32 = jnp.bfloat16, jnp.float32
    value = arriving_ref[0].astype(f32)
    for at in range(1, blocks):
        value = value + arriving_ref[at].astype(f32)
    partial = value.astype(bf16)
    partial_ref[...] = partial
    late = dot_rows(node_ref[...], partial).astype(bf16)
    rest = late.shape[0] // blocks
    extra = early_ref.shape[0] // blocks
    for at in range(blocks):
        message_ref[at, pl.ds(0, extra), :] = early_ref[pl.ds(at * extra, extra), :]
        message_ref[at, pl.ds(extra, rest), :] = late[at * rest : (at + 1) * rest]


def meet(arriving, node_column, early):
    blocks, share, width = arriving.shape
    deep = node_column.shape[1] // 2
    height = (early.shape[0] + deep) // blocks
    return pl.pallas_call(
        meet_body,
        grid=(1,),
        in_specs=[whole(*arriving.shape), whole(share, deep), whole(*early.shape)],
        out_specs=[whole(share, width), whole(blocks, height, width)],
        out_shape=[
            jax.ShapeDtypeStruct((share, width), jnp.bfloat16),
            jax.ShapeDtypeStruct((blocks, height, width), jnp.bfloat16),
        ],
        compiler_params=pltpu.CompilerParams(vmem_limit_bytes=24 * 1024 * 1024),
        cost_estimate=pl.CostEstimate(
            flops=2 * share * deep * width, bytes_accessed=4 * 2**20, transcendentals=0
        ),
        name="meet",
    )(arriving, node_column, early)


def shards(
    node_in,
    edge_in,
    neighbours,
    edge_mask,
    w_src,
    w_dst,
    w_edge_one,
    w_edge_two,
    w_edge_three,
    w_node,
    node_cot,
    edge_cot,
):
    row_count, nbr_count, width = edge_in.shape
    deep = node_in.shape[1]
    bf16, f32 = jnp.bfloat16, jnp.float32
    long, tall, wide = lax.axis_size("z"), lax.axis_size("y"), lax.axis_size("x")
    blocks = wide * tall
    total = blocks * long * row_count
    node_scale = 1.0 / math.sqrt(total)
    edge_scale = 1.0 / math.sqrt(total * nbr_count)

    column = spread(dot(node_in, w_dst).astype(bf16), COLUMN)
    own_row, rest = neighbours % row_count, neighbours // row_count
    at_x, rest = rest % wide, rest // wide
    places = ((at_x * (tall * long) + rest) * row_count + own_row).reshape(-1)
    column, places, node_late = lax.optimization_barrier((column, places, jnp.concatenate([node_in, node_cot], axis=1)))
    table = spread(column.reshape(-1, width), ("x",)).reshape(total, width)
    node_column = lax.all_gather(node_late, "z", axis=0, tiled=True)

    edges = edge_in.reshape(row_count * nbr_count, width)
    cots = edge_cot.reshape(row_count * nbr_count, width)
    *chain, message = edge_chain(
        places,
        table,
        edges,
        cots,
        edge_mask,
        node_in,
        node_cot,
        w_src,
        w_edge_one,
        w_edge_two,
        w_edge_three,
        w_node,
    )
    *chain, message, node_column = lax.optimization_barrier((*chain, message, node_column))
    arriving = exchange(message.reshape(blocks, -1, width), PLANE)
    extra = -(-(2 * deep + 3 * width) // (blocks * 16)) * 16
    edge_out, grad_edge, early, node_out, grad_node = edge_side(
        edges,
        cots,
        edge_mask,
        chain,
        node_in,
        node_cot,
        w_src,
        w_edge_one,
        w_edge_three,
        w_node,
        blocks * extra,
    )
    partial, message = meet(arriving, node_column, early)
    weights = sum_first(exchange(message, PLANE)).astype(bf16)
    weights = jnp.broadcast_to(weights[None], (long, *weights.shape))
    packed = jnp.concatenate([partial.reshape(long, row_count, width), weights], axis=1)
    own = sum_first(exchange(packed, RING)).astype(bf16)
    grad_node = (grad_node + dot_turned(own[:row_count], w_dst)).astype(bf16)
    sums = spread(own[row_count:], PLANE).astype(f32)
    early = sums[:, :extra].reshape(-1, width)
    late = sums[:, extra:].reshape(-1, width)
    ones = [early[at : at + width] * edge_scale for at in range(deep, deep + 3 * width, width)]
    slabs = [early[at : at + width] for at in range(deep + 3 * width, 2 * deep + 3 * width, width)]
    return (
        node_out,
        edge_out.reshape(edge_in.shape),
        grad_node,
        grad_edge.reshape(edge_in.shape),
        early[:deep] * node_scale,
        late * node_scale,
        *ones,
        jnp.concatenate(slabs, axis=1) * node_scale,
    )


def solution(mesh):
    shape = mesh.shape
    outer = shape["node"]
    inner = outer
    devices = mesh.devices.reshape(shape["cplx"], outer, shape["edge"] // inner, inner)
    mesh = Mesh(devices, ("cplx", *ALL))
    in_specs = (
        P(("cplx", *ALL), None),
        P(("cplx", *ALL), None, None),
        P(("cplx", *ALL), None),
        P(("cplx", *ALL), None),
        P(),
        P(),
        P(),
        P(),
        P(),
        P(),
        P(("cplx", *ALL), None),
        P(("cplx", *ALL), None, None),
    )
    out_specs = (
        P(("cplx", *ALL), None),
        P(("cplx", *ALL), None, None),
        P(("cplx", *ALL), None),
        P(("cplx", *ALL), None, None),
        P("cplx", None),
        P("cplx", None),
        P("cplx", None),
        P("cplx", None),
        P("cplx", None),
        P("cplx", None),
    )
    return jax.shard_map(shards, mesh=mesh, in_specs=in_specs, out_specs=out_specs, check_vma=False)
```

time: 189 us -> 180 us (0.952)
  waiting for transfers between devices: 69.1 us -> 30.2 us
  blocking collectives: 43.4 us -> 62 us
  local copies, waits for them, and re-layouts: 3.25 us -> 21.5 us
  starting transfers between devices: 29.8 us -> 22.3 us
  Pallas kernels: 19.1 us -> 21.5 us
  matrix products: 3.84 us -> 1.79 us
    all_to_all x4 -> x3, waiting for transfers between devices: 55.8 us -> 30.2 us  [exchange(): return lax.all_to_all(value, axes, 0, 0, tiled=True)]
    all_to_all x2 -> x3, blocking collectives: 43.4 us -> 62 us  [exchange(): return lax.all_to_all(value, axes, 0, 0, tiled=True)]
    unnamed x22 -> x60, local copies, waits for them, and re-layouts: 0.97 us -> 19.2 us
    all_gather x1, waiting for transfers between devices: 12.6 us -> 0.01 us  [shards(): node_column = lax.all_gather(node_late, 'z', axis=0, tiled=True)]
    all_to_all x4 -> x3, starting transfers between devices: 29.7 us -> 22.2 us  [exchange(): return lax.all_to_all(value, axes, 0, 0, tiled=True)]
    pallas_call x1 -> x3, Pallas kernels: 19.1 us -> 21.5 us  [the longest x1 16.8 us: edge_chain(): pl.pallas_call(functools.partial(chain_body, 1.0 / math.sqrt(nbrs)), grid...]
    dot_general x1 -> x0, matrix products: 2.05 us -> none  [dot_rows(): lax.dot_general(left, right, (((0,), (0,)), ((), ())), preferred_element_...]
  transfers between devices with their start and end apart: 5 -> 4, of which waited for: 5 -> 3; matrix products, arithmetic and copies ran while one was open for 2% -> 2% of each run, Pallas kernels for 0% -> 12%
where the time goes in v4:
time: 180 us; the launch traced here: 179 us
  blocking collectives  62 us (34%)
  waiting for transfers between devices  30.2 us (17%)
  starting transfers between devices  22.3 us (12%)
  local copies, waits for them, and re-layouts  21.5 us (12%)
  Pallas kernels  21.5 us (12%)
  between operations  14.3 us (8%)
  other arithmetic  5.49 us (3%)
    all_to_all x3, blocking collectives, exchange(): return lax.all_to_all(value, axes, 0, 0, tiled=True)  62 us
    all_to_all x3, waiting for transfers between devices, exchange(): return lax.all_to_all(value, axes, 0, 0, tiled=True)  30.2 us
    all_to_all x3, starting transfers between devices, exchange(): return lax.all_to_all(value, axes, 0, 0, tiled=True)  22.2 us
    unnamed x60, local copies, waits for them, and re-layouts  19.2 us
    pallas_call x1, Pallas kernels, edge_chain(): pl.pallas_call(functools.partial(chain_body, 1.0 / math.sqrt(nbrs)), grid...  16.8 us
    pallas_call x1, Pallas kernels, edge_side(): pl.pallas_call(functools.partial(side_body, 1.0 / math.sqrt(nbrs)), grid=...  4.09 us
  transfers between devices with their start and end apart: 4, of which 3 were waited for; matrix products, arithmetic and copies ran while one was open for 2% of the time, Pallas kernels for 12%

profile of v4, /device:TPU:8, one launch (start us, length us, event | category | flops | bytes accessed | tf_op | source)
XLA Modules:
  0.0 179.1 jit_solution(16912235490510100310)
XLA Ops:
  7.2 0.9 copy-done
  8.1 1.0 convolution_convert_fusion
  9.1 0.9 broadcast_in_dim.10
  10.0 11.7 %all-to-all-start = ((bf16[32,64,128]{2,1,0:T(8,128)(2,1)}), bf16[32,64,128]{2,1,0:T(8,128)(2,1)S(1)}, u32[]{:S(2)}, u32[]{:S(2)}) async-start(bf16[32,64,128]{2,1,0:T(8,128)(2,1)} %broadcast_in_dim.10), calls=%async_computation | async-start | bytes 1048576 | tf_op jit(solution)/shard_map/all_to_all | solution.py:24
  21.7 0.0 all-gather.2.cloned.1.call-start
  21.8 0.8 fusion.4
  22.6 0.1 reshape.56.place_ref
  22.7 1.5 pad_maximum_fusion.1
  24.2 13.0 %all-to-all-done = bf16[32,64,128]{2,1,0:T(8,128)(2,1)S(1)} async-done(((bf16[32,64,128]{2,1,0:T(8,128)(2,1)}), bf16[32,64,128]{2,1,0:T(8,128)(2,1)S(1)}, u32[]{:S(2)}, u32[]{:S(2)}) %all-to-all-start) | async-done | bytes 524320 | tf_op jit(solution)/shard_map/all_to_all | solution.py:24
  37.3 0.3 broadcast_in_dim.12
  37.7 27.5 %all_to_all.30 = bf16[4,2048,128]{2,1,0:T(8,128)(2,1)} all-to-all(bf16[4,2048,128]{2,1,0:T(8,128)(2,1)S(1)} %broadcast_in_dim.12), channel_id=1, replica_groups=mesh['cplx'=2,'y'=4,'z'=8,'x'=4] {'x'}, dimensions={0} | all-to-all | bytes 4194304 | tf_op jit(solution)/shard_map/all_to_all | solution.py:24
  65.2 16.8 %edge_chain.1 = (bf16[4096,128]{1,0:T(8,128)(2,1)S(1)}, bf16[4096,128]{1,0:T(8,128)(2,1)S(1)}, bf16[4096,128]{1,0:T(8,128)(2,1)S(1)}, bf16[4096,128]{1,0:T(8,128)(2,1)S(1)}, bf16[8192,128]{1,0:T(8,128)(2,1)S(1)}) custom-call(s32[4096]{0:T(1024)S(1)} %reshape.56.place_ref, bf16[8192,128]{1,0:T(8,128)(2,1)} %bitcast.19, bf16[4096,128]{1,0:T(8,128)(2,1)S(1)} %bitcast.13, ...), custom_call_target="tpu_custom_call" | custom-call | flops 536870912 | bytes 12582912 | tf_op jit(solution)/shard_map/edge_chain/pallas_call | solution.py:187
  82.1 1.3 copy-done.4
  83.4 1.0 copy-done.7
  84.4 1.0 copy-done.9
  85.4 1.0 copy-done.11
  86.4 1.0 copy-done.13
  87.4 5.7 %all-to-all-start.2 = ((bf16[16,512,128]{2,1,0:T(8,128)(2,1)}), bf16[16,512,128]{2,1,0:T(8,128)(2,1)S(1)}, u32[]{:S(2)}, u32[]{:S(2)}) async-start(bf16[16,512,128]{2,1,0:T(8,128)(2,1)} %bitcast.17), calls=%async_computation.2 | async-start | bytes 4194304 | tf_op jit(solution)/shard_map/all_to_all | solution.py:24
  93.1 1.2 copy-done.3
  94.3 1.2 copy-done.8
  95.5 1.2 copy-done.10
  96.7 1.2 copy-done.12
  98.0 1.2 copy-done.14
  99.2 0.9 copy-done.18
  100.1 0.8 copy-done.22
  100.9 0.8 copy-done.24
  101.6 0.8 copy-done.26
  102.4 4.1 %edge_side.1 = (bf16[4096,128]{1,0:T(8,128)(2,1)}, bf16[4096,128]{1,0:T(8,128)(2,1)}, bf16[1536,128]{1,0:T(8,128)(2,1)S(1)}, bf16[64,512]{1,0:T(8,128)(2,1)}, f32[64,512]{1,0:T(8,128)S(1)}) custom-call(bf16[4096,128]{1,0:T(8,128)(2,1)S(1)} %bitcast.14, bf16[4096,128]{1,0:T(8,128)(2,1)S(1)} %bitcast.16, s32[64,64]{1,0:T(8,128)S(1)} %copy-done.22, ...), custom_call_target="tpu_custom_call" | custom-call | flops 671088640 | bytes 25165824 | tf_op jit(solution)/shard_map/edge_side/pallas_call | solution.py:294
  106.5 0.8 copy-done.19
  107.2 0.7 copy-done.27
  107.9 9.2 %all-to-all-done.2.arriving_ref = bf16[16,512,128]{2,1,0:T(8,128)(2,1)S(1)} async-done(((bf16[16,512,128]{2,1,0:T(8,128)(2,1)}), bf16[16,512,128]{2,1,0:T(8,128)(2,1)S(1)}, u32[]{:S(2)}, u32[]{:S(2)}) %all-to-all-start.2) | async-done | bytes 2097184 | tf_op jit(solution)/shard_map/all_to_all | solution.py:24
  117.1 1.2 copy-done.6
  118.3 1.0 copy-done.20
  119.3 0.6 meet.1
  119.9 13.9 %all_to_all.31 = bf16[16,128,128]{2,1,0:T(8,128)(2,1)S(1)} all-to-all(bf16[16,128,128]{2,1,0:T(8,128)(2,1)S(1)} %get-tuple-element.50), channel_id=1, replica_groups=mesh['cplx'=2,'y'=4,'z'=8,'x'=4] {'x','y'}, dimensions={0} | all-to-all | bytes 1048576 | tf_op jit(solution)/shard_map/all_to_all | solution.py:24
  133.8 0.1 reduce_sum.24
  133.9 20.7 %all_to_all.32 = bf16[8,192,128]{2,1,0:T(8,128)(2,1)S(1)} all-to-all(bf16[8,192,128]{2,1,0:T(8,128)(2,1)S(1)} %pad_maximum_fusion), channel_id=1, replica_groups=mesh['cplx'=2,'y'=4,'z'=8,'x'=4] {'z'}, dimensions={0} | all-to-all | bytes 786432 | tf_op jit(solution)/shard_map/all_to_all | solution.py:24
  154.6 0.1 reduce_sum.25
  154.7 0.9 broadcast_in_dim.14
  155.6 4.8 %all-to-all-start.5 = ((bf16[16,128,128]{2,1,0:T(8,128)(2,1)}), bf16[16,128,128]{2,1,0:T(8,128)(2,1)S(1)}, u32[]{:S(2)}, u32[]{:S(2)}) async-start(bf16[16,128,128]{2,1,0:T(8,128)(2,1)} %broadcast_in_dim.14), calls=%async_computation.5 | async-start | bytes 1048576 | tf_op jit(solution)/shard_map/all_to_all | solution.py:24
  160.4 0.8 fusion
  161.2 8.0 %all-to-all-done.5 = bf16[16,128,128]{2,1,0:T(8,128)(2,1)S(1)} async-done(((bf16[16,128,128]{2,1,0:T(8,128)(2,1)}), bf16[16,128,128]{2,1,0:T(8,128)(2,1)S(1)}, u32[]{:S(2)}, u32[]{:S(2)}) %all-to-all-start.5) | async-done | bytes 524320 | tf_op jit(solution)/shard_map/all_to_all | solution.py:24
  169.2 0.1 slice.50
  169.3 0.7 slice_multiply_fusion.1
  170.0 0.7 fusion.12
  170.7 0.1 convert_element_type.15
  170.8 0.7 slice_multiply_fusion
  171.5 0.7 maximum_multiply_fusion
  (46 shorter events, 0.2 us)
Async XLA Ops:
  7.2 0.9 copy-start
  10.0 27.2 %all-to-all-start = ((bf16[32,64,128]{2,1,0:T(8,128)(2,1)}), bf16[32,64,128]{2,1,0:T(8,128)(2,1)S(1)}, u32[]{:S(2)}, u32[]{:S(2)}) async-start(bf16[32,64,128]{2,1,0:T(8,128)(2,1)} %broadcast_in_dim.10), calls=%async_computation | async-start | bytes 1048576 | tf_op jit(solution)/shard_map/all_to_all | solution.py:24
  21.7 65.7 %all-gather.2.cloned.1.call-start = ((), (), s32[]{:S(2)}) async-start(), calls=%async_computation.6 | async-start | bytes 1179648 | tf_op jit(solution)/shard_map/all_gather | solution.py:378
  37.5 27.6 %copy-start.1 = (bf16[64,64,128]{2,1,0:T(8,128)(2,1)S(1)}, bf16[64,64,128]{2,1,0:T(8,128)(2,1)}, u32[]{:S(2)}) copy-start(bf16[64,64,128]{2,1,0:T(8,128)(2,1)} %param.13) | copy-start | bytes 3145732
  37.6 27.6 %copy-start.2 = (bf16[64,64,128]{2,1,0:T(8,128)(2,1)S(1)}, bf16[64,64,128]{2,1,0:T(8,128)(2,1)}, u32[]{:S(2)}) copy-start(bf16[64,64,128]{2,1,0:T(8,128)(2,1)} %param.23) | copy-start | bytes 3145732
  37.6 27.6 %copy-start.5 = (bf16[64,512]{1,0:T(8,128)(2,1)S(1)}, bf16[64,512]{1,0:T(8,128)(2,1)}, u32[]{:S(2)}) copy-start(bf16[64,512]{1,0:T(8,128)(2,1)} %node_ref.3) | copy-start | bytes 196612
  37.6 27.6 %copy-start.15 = (bf16[64,512]{1,0:T(8,128)(2,1)S(1)}, bf16[64,512]{1,0:T(8,128)(2,1)}, u32[]{:S(2)}) copy-start(bf16[64,512]{1,0:T(8,128)(2,1)} %node_cot_ref.3) | copy-start | bytes 196612
  37.6 27.6 %copy-start.16 = (bf16[512,128]{1,0:T(8,128)(2,1)S(1)}, bf16[512,128]{1,0:T(8,128)(2,1)}, u32[]{:S(2)}) copy-start(bf16[512,128]{1,0:T(8,128)(2,1)} %w_src_ref.3) | copy-start | bytes 393220
  37.6 27.6 %copy-start.17 = (bf16[128,512]{1,0:T(8,128)(2,1)S(1)}, bf16[128,512]{1,0:T(8,128)(2,1)}, u32[]{:S(2)}) copy-start(bf16[128,512]{1,0:T(8,128)(2,1)} %w_node_ref.3) | copy-start | bytes 393220
  37.6 27.6 %copy-start.21 = (s32[64,64]{1,0:T(8,128)S(1)}, s32[64,64]{1,0:T(8,128)}, u32[]{:S(2)}) copy-start(s32[64,64]{1,0:T(8,128)} %mask_ref.3) | copy-start | bytes 49156
  37.6 27.6 %copy-start.23 = (bf16[128,128]{1,0:T(8,128)(2,1)S(1)}, bf16[128,128]{1,0:T(8,128)(2,1)}, u32[]{:S(2)}) copy-start(bf16[128,128]{1,0:T(8,128)(2,1)} %one_ref.3) | copy-start | bytes 98308
  37.6 27.6 %copy-start.25 = (bf16[128,128]{1,0:T(8,128)(2,1)S(1)}, bf16[128,128]{1,0:T(8,128)(2,1)}, u32[]{:S(2)}) copy-start(bf16[128,128]{1,0:T(8,128)(2,1)} %three_ref.3) | copy-start | bytes 98308
  37.6 27.6 %copy-start.29 = (bf16[128,128]{1,0:T(8,128)(2,1)S(1)}, bf16[128,128]{1,0:T(8,128)(2,1)}, u32[]{:S(2)}) copy-start(bf16[128,128]{1,0:T(8,128)(2,1)} %two_ref.1) | copy-start | bytes 98308
  82.1 1.4 copy-start.4
  83.4 1.0 copy-start.7
  84.4 1.0 copy-start.9
  85.4 1.0 copy-start.11
  86.3 1.0 copy-start.13
  87.4 29.7 %all-to-all-start.2 = ((bf16[16,512,128]{2,1,0:T(8,128)(2,1)}), bf16[16,512,128]{2,1,0:T(8,128)(2,1)S(1)}, u32[]{:S(2)}, u32[]{:S(2)}) async-start(bf16[16,512,128]{2,1,0:T(8,128)(2,1)} %bitcast.17), calls=%async_computation.2 | async-start | bytes 4194304 | tf_op jit(solution)/shard_map/all_to_all | solution.py:24
  93.1 1.2 copy-start.3
  94.3 1.2 copy-start.8
  95.5 1.2 copy-start.10
  96.7 1.2 copy-start.12
  98.0 1.2 copy-start.14
  99.2 0.9 copy-start.18
  100.1 0.8 copy-start.22
  100.9 0.8 copy-start.24
  101.6 0.8 copy-start.26
  106.5 0.8 copy-start.19
  107.2 0.7 copy-start.27
  117.1 1.2 copy-start.6
  118.3 1.0 copy-start.20
  133.8 26.5 %copy-start.28 = (f32[64,512]{1,0:T(8,128)S(1)}, f32[64,512]{1,0:T(8,128)}, u32[]{:S(2)}) copy-start(f32[64,512]{1,0:T(8,128)} %copy-done.27) | copy-start | bytes 393220
  155.6 13.6 %all-to-all-start.5 = ((bf16[16,128,128]{2,1,0:T(8,128)(2,1)}), bf16[16,128,128]{2,1,0:T(8,128)(2,1)S(1)}, u32[]{:S(2)}, u32[]{:S(2)}) async-start(bf16[16,128,128]{2,1,0:T(8,128)(2,1)} %broadcast_in_dim.14), calls=%async_computation.5 | async-start | bytes 1048576 | tf_op jit(solution)/shard_map/all_to_all | solution.py:24
Sparse Core Ops, SparseCore 0:
  37.4 36.8 all-gather.1

commit v5 on v4

--- a/solution.py
+++ b/solution.py
@@ -10,7 +10,6 @@
 from jax.sharding import PartitionSpec as P
 
 RING = ("z",)
-COLUMN = ("y", "z")
 PLANE = ("x", "y")
 ALL = ("y", "z", "x")
 SUMS = 4
@@ -170,6 +169,10 @@
     return pl.BlockSpec(shape, lambda i, *places: (0,) * len(shape))
 
 
+def in_hbm(value):
+    return pltpu.with_memory_space_constraint(value, pltpu.HBM)
+
+
 def edge_chain(
     places, table, edges, cots, mask, node_in, node_cot, w_src, w_one, w_two, w_three, w_node
 ):
@@ -178,6 +181,8 @@
     nodes, nbrs = mask.shape
     deep = node_in.shape[1]
     f32, bf16 = jnp.float32, jnp.bfloat16
+    rest = (cots, mask, node_in, node_cot, w_src, w_one, w_two, w_three, w_node)
+    rest = tuple(map(in_hbm, rest))
     rows = pl.BlockSpec((BLOCK, width), lambda i, places: (i, 0))
     masks = pl.BlockSpec((BLOCK // nbrs, nbrs), lambda i, places: (i, 0))
     square = whole(width, width)
@@ -194,14 +199,13 @@
             out_specs=[rows] * 4 + [whole(count, width)],
             scratch_shapes=[held, part, part, small, small] + [held] * SUMS,
         ),
-        out_shape=[jax.ShapeDtypeStruct((total, width), bf16)] * 4
-        + [jax.ShapeDtypeStruct((count, width), bf16)],
+        out_shape=[pltpu.HBM((total, width), bf16)] * 4 + [pltpu.HBM((count, width), bf16)],
         compiler_params=pltpu.CompilerParams(vmem_limit_bytes=44 * 1024 * 1024),
         cost_estimate=pl.CostEstimate(
             flops=8 * total * width * width, bytes_accessed=12 * 2**20, transcendentals=0
         ),
         name="edge_chain",
-    )(places, table, edges, cots, mask, node_in, node_cot, w_src, w_one, w_two, w_three, w_node)
+    )(places, table, edges, *rest)
 
 
 def side_body(
@@ -285,6 +289,7 @@
 ):
     total, width = edges.shape
     nodes, nbrs = mask.shape
+    rest = tuple(map(in_hbm, (node_in, node_cot, w_src, w_one, w_three, w_node)))
     deep = node_in.shape[1]
     f32, bf16 = jnp.float32, jnp.bfloat16
     rows = pl.BlockSpec((SIDE_BLOCK, width), lambda i: (i, 0))
@@ -298,15 +303,15 @@
         + [whole(deep, width), square, square, whole(width, deep)],
         out_specs=[rows, rows, whole(early_rows, width), whole(nodes, deep), whole(nodes, deep)],
         scratch_shapes=[small, small, small, pltpu.VMEM((3 * width, width), f32)],
-        out_shape=[jax.ShapeDtypeStruct((total, width), bf16)] * 2
-        + [jax.ShapeDtypeStruct((early_rows, width), bf16)]
-        + [jax.ShapeDtypeStruct((nodes, deep), bf16), jax.ShapeDtypeStruct((nodes, deep), f32)],
+        out_shape=[pltpu.HBM((total, width), bf16)] * 2
+        + [pltpu.HBM((early_rows, width), bf16)]
+        + [pltpu.HBM((nodes, deep), bf16), pltpu.HBM((nodes, deep), f32)],
         compiler_params=pltpu.CompilerParams(vmem_limit_bytes=24 * 1024 * 1024),
         cost_estimate=pl.CostEstimate(
             flops=10 * total * width * width, bytes_accessed=24 * 2**20, transcendentals=0
         ),
         name="edge_side",
-    )(edges, cots, mask, *chain, node_in, node_cot, w_src, w_one, w_three, w_node)
+    )(*map(in_hbm, (edges, cots)), in_hbm(mask), *map(in_hbm, chain), *rest)
 
 
 def meet_body(arriving_ref, node_ref, early_ref, partial_ref, message_ref):
@@ -343,7 +348,7 @@
             flops=2 * share * deep * width, bytes_accessed=4 * 2**20, transcendentals=0
         ),
         name="meet",
-    )(arriving, node_column, early)
+    )(arriving, in_hbm(node_column), in_hbm(early))
 
 
 def shards(
@@ -369,12 +374,12 @@
     node_scale = 1.0 / math.sqrt(total)
     edge_scale = 1.0 / math.sqrt(total * nbr_count)
 
-    column = spread(dot(node_in, w_dst).astype(bf16), COLUMN)
+    column = spread(dot(node_in, w_dst).astype(bf16), RING)
     own_row, rest = neighbours % row_count, neighbours // row_count
     at_x, rest = rest % wide, rest // wide
     places = ((at_x * (tall * long) + rest) * row_count + own_row).reshape(-1)
     column, places, node_late = lax.optimization_barrier((column, places, jnp.concatenate([node_in, node_cot], axis=1)))
-    table = spread(column.reshape(-1, width), ("x",)).reshape(total, width)
+    table = spread(column.reshape(-1, width), PLANE).reshape(total, width)
     node_column = lax.all_gather(node_late, "z", axis=0, tiled=True)
 
     edges = edge_in.reshape(row_count * nbr_count, width)

time: 180 us -> 169 us (0.939)
  blocking collectives: 62 us -> 28.6 us
  waiting for transfers between devices: 30.2 us -> 60.9 us
  local copies, waits for them, and re-layouts: 21.5 us -> 4.42 us
  Pallas kernels: 21.5 us -> 27 us
  starting transfers between devices: 22.3 us -> 26.1 us
    all_to_all x3 -> x2, blocking collectives: 62 us -> 28.6 us  [exchange(): return lax.all_to_all(value, axes, 0, 0, tiled=True)]
    all_to_all x3 -> x4, waiting for transfers between devices: 30.2 us -> 60.2 us  [exchange(): return lax.all_to_all(value, axes, 0, 0, tiled=True)]
    unnamed x60 -> x6, local copies, waits for them, and re-layouts: 19.2 us -> 0.91 us
    all_to_all x3 -> x4, starting transfers between devices: 22.2 us -> 26.1 us  [exchange(): return lax.all_to_all(value, axes, 0, 0, tiled=True)]
    pallas_call x1, Pallas kernels: 4.09 us -> 6.95 us  [edge_side(): pl.pallas_call(functools.partial(side_body, 1.0 / math.sqrt(nbrs)), grid=...]
  transfers between devices with their start and end apart: 4 -> 5, of which waited for: 3 -> 4; matrix products, arithmetic and copies ran while one was open for 2% -> 2% of each run, Pallas kernels for 12% -> 15%
where the time goes in v5:
time: 169 us; the launch traced here: 168 us
  waiting for transfers between devices  60.9 us (36%)
  blocking collectives  28.6 us (17%)
  Pallas kernels  27 us (16%)
  starting transfers between devices  26.1 us (15%)
  between operations  14.1 us (8%)
  other arithmetic  5.49 us (3%)
  local copies, waits for them, and re-layouts  4.42 us (3%)
  matrix products  1.8 us (1%)
    all_to_all x4, waiting for transfers between devices, exchange(): return lax.all_to_all(value, axes, 0, 0, tiled=True)  60.2 us
    all_to_all x2, blocking collectives, exchange(): return lax.all_to_all(value, axes, 0, 0, tiled=True)  28.6 us
    all_to_all x4, starting transfers between devices, exchange(): return lax.all_to_all(value, axes, 0, 0, tiled=True)  26.1 us
    pallas_call x1, Pallas kernels, edge_chain(): pl.pallas_call(functools.partial(chain_body, 1.0 / math.sqrt(nbrs)), grid...  18.3 us
    pallas_call x1, Pallas kernels, edge_side(): pl.pallas_call(functools.partial(side_body, 1.0 / math.sqrt(nbrs)), grid=...  6.95 us
  transfers between devices with their start and end apart: 5, of which 4 were waited for; matrix products, arithmetic and copies ran while one was open for 2% of the time, Pallas kernels for 15%

profile of v5, /device:TPU:8, one launch (start us, length us, event | category | flops | bytes accessed | tf_op | source)
XLA Modules:
  0.0 168.4 jit_solution(16177370414647076509)
XLA Ops:
  7.2 0.0 copy-start
  7.2 0.9 copy-done
  8.1 1.0 convolution_convert_fusion
  9.1 0.7 broadcast_in_dim.10
  9.8 8.5 %all-to-all-start = ((bf16[8,64,128]{2,1,0:T(8,128)(2,1)}), bf16[8,64,128]{2,1,0:T(8,128)(2,1)S(1)}, u32[]{:S(2)}, u32[]{:S(2)}) async-start(bf16[8,64,128]{2,1,0:T(8,128)(2,1)} %broadcast_in_dim.10), calls=%async_computation | async-start | bytes 262144 | tf_op jit(solution)/shard_map/all_to_all | solution.py:23
  18.2 0.8 fusion.4
  19.0 0.1 reshape.56.place_ref
  19.1 1.5 pad_maximum_fusion.1
  20.7 6.7 %all-to-all-done = bf16[8,64,128]{2,1,0:T(8,128)(2,1)S(1)} async-done(((bf16[8,64,128]{2,1,0:T(8,128)(2,1)}), bf16[8,64,128]{2,1,0:T(8,128)(2,1)S(1)}, u32[]{:S(2)}, u32[]{:S(2)}) %all-to-all-start) | async-done | bytes 131104 | tf_op jit(solution)/shard_map/all_to_all | solution.py:23
  27.3 1.7 %broadcast_in_dim.12 = bf16[16,512,128]{2,1,0:T(8,128)(2,1)} broadcast(bf16[512,128]{1,0:T(8,128)(2,1)S(1)} %bitcast.22), dimensions={1,2} | broadcast | bytes 2228224 | tf_op jit(solution)/shard_map/broadcast_in_dim | solution.py:28
  29.1 0.0 copy-start.1
  29.1 7.5 %all-to-all-start.1 = ((bf16[16,512,128]{2,1,0:T(8,128)(2,1)}), bf16[16,512,128]{2,1,0:T(8,128)(2,1)S(1)}, u32[]{:S(2)}, u32[]{:S(2)}) async-start(bf16[16,512,128]{2,1,0:T(8,128)(2,1)} %broadcast_in_dim.12), calls=%async_computation.1 | async-start | bytes 4194304 | tf_op jit(solution)/shard_map/all_to_all | solution.py:23
  36.6 0.0 all-gather.2.cloned.1.call-start
  36.6 0.7 all-gather.2.cloned.1.call-update
  37.3 26.0 %all-to-all-done.1 = bf16[16,512,128]{2,1,0:T(8,128)(2,1)S(1)} async-done(((bf16[16,512,128]{2,1,0:T(8,128)(2,1)}), bf16[16,512,128]{2,1,0:T(8,128)(2,1)S(1)}, u32[]{:S(2)}, u32[]{:S(2)}) %all-to-all-start.1) | async-done | bytes 2097184 | tf_op jit(solution)/shard_map/all_to_all | solution.py:23
  63.4 0.0 copy-done.1
  63.4 18.3 %edge_chain.1 = (bf16[4096,128]{1,0:T(8,128)(2,1)}, bf16[4096,128]{1,0:T(8,128)(2,1)}, bf16[4096,128]{1,0:T(8,128)(2,1)}, bf16[4096,128]{1,0:T(8,128)(2,1)}, bf16[8192,128]{1,0:T(8,128)(2,1)}) custom-call(s32[4096]{0:T(1024)S(1)} %reshape.56.place_ref, bf16[8192,128]{1,0:T(8,128)(2,1)S(1)} %bitcast.13, bf16[4096,128]{1,0:T(8,128)(2,1)S(1)} %bitcast.15, ...), custom_call_target="tpu_custom_call" | custom-call | flops 536870912 | bytes 12582912 | tf_op jit(solution)/shard_map/edge_chain/pallas_call | solution.py:192
  81.6 0.0 all-gather.2.cloned.1.call-done.node_ref
  81.7 5.3 %all-to-all-start.2 = ((bf16[16,512,128]{2,1,0:T(8,128)(2,1)}), bf16[16,512,128]{2,1,0:T(8,128)(2,1)S(1)}, u32[]{:S(2)}, u32[]{:S(2)}) async-start(bf16[16,512,128]{2,1,0:T(8,128)(2,1)} %bitcast.21), calls=%async_computation.2 | async-start | bytes 4194304 | tf_op jit(solution)/shard_map/all_to_all | solution.py:23
  86.9 7.0 %edge_side.1 = (bf16[4096,128]{1,0:T(8,128)(2,1)}, bf16[4096,128]{1,0:T(8,128)(2,1)}, bf16[1536,128]{1,0:T(8,128)(2,1)}, bf16[64,512]{1,0:T(8,128)(2,1)}, f32[64,512]{1,0:T(8,128)}) custom-call(bf16[4096,128]{1,0:T(8,128)(2,1)} %bitcast.14, bf16[4096,128]{1,0:T(8,128)(2,1)} %bitcast.18, s32[64,64]{1,0:T(8,128)} %mask_ref.3, ...), custom_call_target="tpu_custom_call" | custom-call | flops 671088640 | bytes 25165824 | tf_op jit(solution)/shard_map/edge_side/pallas_call | solution.py:299
  93.9 19.5 %all-to-all-done.2.arriving_ref = bf16[16,512,128]{2,1,0:T(8,128)(2,1)S(1)} async-done(((bf16[16,512,128]{2,1,0:T(8,128)(2,1)}), bf16[16,512,128]{2,1,0:T(8,128)(2,1)S(1)}, u32[]{:S(2)}, u32[]{:S(2)}) %all-to-all-start.2) | async-done | bytes 2097184 | tf_op jit(solution)/shard_map/all_to_all | solution.py:23
  113.4 1.7 %meet.1 = (bf16[512,128]{1,0:T(8,128)(2,1)S(1)}, bf16[16,128,128]{2,1,0:T(8,128)(2,1)S(1)}) custom-call(bf16[16,512,128]{2,1,0:T(8,128)(2,1)S(1)} %all-to-all-done.2.arriving_ref, bf16[512,1024]{1,0:T(8,128)(2,1)} %all-gather.2.cloned.1.call-done.node_ref, bf16[1536,128]{1,0:T(8,128)(2,1)} %get-tuple-element.48.early_ref), custom_call_target="tpu_custom_call" | custom-call | flops 67108864 | bytes 4194304 | tf_op jit(solution)/shard_map/meet/pallas_call | solution.py:337
  115.1 14.3 %all_to_all.30 = bf16[16,128,128]{2,1,0:T(8,128)(2,1)S(1)} all-to-all(bf16[16,128,128]{2,1,0:T(8,128)(2,1)S(1)} %get-tuple-element.50), channel_id=1, replica_groups=mesh['cplx'=2,'y'=4,'z'=8,'x'=4] {'x','y'}, dimensions={0} | all-to-all | bytes 1048576 | tf_op jit(solution)/shard_map/all_to_all | solution.py:23
  129.4 0.1 reduce_sum.24
  129.4 0.0 copy-start.2
  129.5 14.3 %all_to_all.31 = bf16[8,192,128]{2,1,0:T(8,128)(2,1)S(1)} all-to-all(bf16[8,192,128]{2,1,0:T(8,128)(2,1)S(1)} %pad_maximum_fusion), channel_id=1, replica_groups=mesh['cplx'=2,'y'=4,'z'=8,'x'=4] {'z'}, dimensions={0} | all-to-all | bytes 786432 | tf_op jit(solution)/shard_map/all_to_all | solution.py:23
  143.8 0.1 reduce_sum.25
  143.9 0.9 broadcast_in_dim.14
  144.8 4.8 %all-to-all-start.5 = ((bf16[16,128,128]{2,1,0:T(8,128)(2,1)}), bf16[16,128,128]{2,1,0:T(8,128)(2,1)S(1)}, u32[]{:S(2)}, u32[]{:S(2)}) async-start(bf16[16,128,128]{2,1,0:T(8,128)(2,1)} %broadcast_in_dim.14), calls=%async_computation.5 | async-start | bytes 1048576 | tf_op jit(solution)/shard_map/all_to_all | solution.py:23
  149.6 0.0 copy-done.2
  149.6 0.8 fusion
  150.4 8.0 %all-to-all-done.5 = bf16[16,128,128]{2,1,0:T(8,128)(2,1)S(1)} async-done(((bf16[16,128,128]{2,1,0:T(8,128)(2,1)}), bf16[16,128,128]{2,1,0:T(8,128)(2,1)S(1)}, u32[]{:S(2)}, u32[]{:S(2)}) %all-to-all-start.5) | async-done | bytes 524320 | tf_op jit(solution)/shard_map/all_to_all | solution.py:23
  158.5 0.1 slice.50
  158.5 0.7 slice_multiply_fusion.1
  159.3 0.7 fusion.12
  159.9 0.1 convert_element_type.15
  160.0 0.7 slice_multiply_fusion
  160.8 0.7 maximum_multiply_fusion
  (3 shorter events, 0.1 us)
Async XLA Ops:
  7.2 0.9 copy-start
  9.8 17.6 %all-to-all-start = ((bf16[8,64,128]{2,1,0:T(8,128)(2,1)}), bf16[8,64,128]{2,1,0:T(8,128)(2,1)S(1)}, u32[]{:S(2)}, u32[]{:S(2)}) async-start(bf16[8,64,128]{2,1,0:T(8,128)(2,1)} %broadcast_in_dim.10), calls=%async_computation | async-start | bytes 262144 | tf_op jit(solution)/shard_map/all_to_all | solution.py:23
  29.1 34.3 %copy-start.1 = (bf16[64,64,128]{2,1,0:T(8,128)(2,1)S(1)}, bf16[64,64,128]{2,1,0:T(8,128)(2,1)}, u32[]{:S(2)}) copy-start(bf16[64,64,128]{2,1,0:T(8,128)(2,1)} %param.13) | copy-start | bytes 3145732
  29.1 34.3 %all-to-all-start.1 = ((bf16[16,512,128]{2,1,0:T(8,128)(2,1)}), bf16[16,512,128]{2,1,0:T(8,128)(2,1)S(1)}, u32[]{:S(2)}, u32[]{:S(2)}) async-start(bf16[16,512,128]{2,1,0:T(8,128)(2,1)} %broadcast_in_dim.12), calls=%async_computation.1 | async-start | bytes 4194304 | tf_op jit(solution)/shard_map/all_to_all | solution.py:23
  36.6 45.1 %all-gather.2.cloned.1.call-start = ((), (), s32[]{:S(2)}) async-start(), calls=%async_computation.6 | async-start | bytes 1179648 | tf_op jit(solution)/shard_map/all_gather | solution.py:383
  81.7 31.7 %all-to-all-start.2 = ((bf16[16,512,128]{2,1,0:T(8,128)(2,1)}), bf16[16,512,128]{2,1,0:T(8,128)(2,1)S(1)}, u32[]{:S(2)}, u32[]{:S(2)}) async-start(bf16[16,512,128]{2,1,0:T(8,128)(2,1)} %bitcast.21), calls=%async_computation.2 | async-start | bytes 4194304 | tf_op jit(solution)/shard_map/all_to_all | solution.py:23
  129.4 20.2 %copy-start.2 = (f32[64,512]{1,0:T(8,128)S(1)}, f32[64,512]{1,0:T(8,128)}, u32[]{:S(2)}) copy-start(f32[64,512]{1,0:T(8,128)} %get-tuple-element.45) | copy-start | bytes 393220
  144.8 13.6 %all-to-all-start.5 = ((bf16[16,128,128]{2,1,0:T(8,128)(2,1)}), bf16[16,128,128]{2,1,0:T(8,128)(2,1)S(1)}, u32[]{:S(2)}, u32[]{:S(2)}) async-start(bf16[16,128,128]{2,1,0:T(8,128)(2,1)} %broadcast_in_dim.14), calls=%async_computation.5 | async-start | bytes 1048576 | tf_op jit(solution)/shard_map/all_to_all | solution.py:23
Sparse Core Ops, SparseCore 0:
  39.8 34.5 all-gather.1

commit v6 on v5

--- a/solution.py
+++ b/solution.py
@@ -13,8 +13,8 @@
 PLANE = ("x", "y")
 ALL = ("y", "z", "x")
 SUMS = 4
-UNROLL = 32
 BLOCK = 1024
+CHUNKS = 4
 SIDE_BLOCK = 1024
 PIECE = 512
 
@@ -69,10 +69,8 @@
     return jnp.concatenate(columns, axis=0)
 
 
-def chain_body(
+def prep_body(
     agg_scale,
-    place_ref,
-    table_ref,
     edge_ref,
     cot_ref,
     mask_ref,
@@ -80,25 +78,84 @@
     node_cot_ref,
     w_src_ref,
     one_ref,
-    two_ref,
     three_ref,
     w_node_ref,
+    base_ref,
+    up_ref,
+    src_proj,
+    grad_agg,
+):
+    step = pl.program_id(0)
+    groups, nbrs = mask_ref.shape
+    width = edge_ref.shape[1]
+    bf16, f32 = jnp.bfloat16, jnp.float32
+
+    @pl.when(step == 0)
+    def _():
+        src_proj[...] = dot(node_ref[...], w_src_ref[...]).astype(bf16).astype(f32)
+        grad_agg[...] = dot_turned(node_cot_ref[...], w_node_ref[...]) * agg_scale
+
+    row = pl.multiple_of(step * groups, groups)
+    masked = mask_of(mask_ref[...], width)
+    agg_rows = rows_of(grad_agg[pl.ds(row, groups), :], nbrs)
+    grad_upd = (masked * (cot_ref[...].astype(f32) + masked * agg_rows)).astype(bf16)
+    up_ref[...] = dot_turned(grad_upd, three_ref[...])
+    src_rows = rows_of(src_proj[pl.ds(row, groups), :], nbrs)
+    base_ref[...] = dot(edge_ref[...], one_ref[...]) + src_rows
+
+
+def in_hbm(value):
+    return pltpu.with_memory_space_constraint(value, pltpu.HBM)
+
+
+def whole(*shape):
+    return pl.BlockSpec(shape, lambda i, *places: (0,) * len(shape))
+
+
+def edge_prep(edges, cots, mask, node_in, node_cot, w_src, w_one, w_three, w_node):
+    total, width = edges.shape
+    nodes, nbrs = mask.shape
+    deep = node_in.shape[1]
+    rest = (edges, cots, mask, node_in, node_cot, w_src, w_one, w_three, w_node)
+    rows = pl.BlockSpec((SIDE_BLOCK, width), lambda i: (i, 0))
+    masks = pl.BlockSpec((SIDE_BLOCK // nbrs, nbrs), lambda i: (i, 0))
+    square = whole(width, width)
+    small = pltpu.VMEM((nodes, width), jnp.float32)
+    return pl.pallas_call(
+        functools.partial(prep_body, 1.0 / math.sqrt(nbrs)),
+        grid=(total // SIDE_BLOCK,),
+        in_specs=[rows, rows, masks, whole(nodes, deep), whole(nodes, deep), whole(deep, width)]
+        + [square, square, whole(width, deep)],
+        out_specs=[rows, rows],
+        scratch_shapes=[small, small],
+        out_shape=[pltpu.HBM((total, width), jnp.float32)] * 2,
+        compiler_params=pltpu.CompilerParams(vmem_limit_bytes=24 * 1024 * 1024),
+        cost_estimate=pl.CostEstimate(
+            flops=4 * total * width * width, bytes_accessed=12 * 2**20, transcendentals=0
+        ),
+        name="edge_prep",
+    )(*map(in_hbm, rest))
+
+
+def chain_body(
+    place_ref,
+    table_ref,
+    base_ref,
+    up_ref,
+    two_ref,
     act_one_ref,
     act_two_ref,
     grad_two_ref,
     grad_one_ref,
     message_ref,
     table,
-    pulled,
-    grads,
-    src_proj,
-    grad_agg,
-    *sums,
+    *held,
 ):
     step = pl.program_id(0)
-    block = pulled.shape[0]
     count, width = table.shape
-    groups, nbrs = mask_ref.shape
+    block = base_ref.shape[0]
+    chunk = block // CHUNKS
+    sums, pulled, grads = held[:SUMS], held[SUMS : SUMS + CHUNKS], held[SUMS + CHUNKS :]
     bf16, f32 = jnp.bfloat16, jnp.float32
 
     @pl.when(step == 0)
@@ -111,46 +168,43 @@
             return carry
 
         lax.fori_loop(0, count // PIECE, fill, 0)
-        src_proj[...] = dot(node_ref[...], w_src_ref[...]).astype(bf16).astype(f32)
-        grad_agg[...] = dot_turned(node_cot_ref[...], w_node_ref[...]) * agg_scale
 
     first = step * block
 
-    def pull(at, carry):
-        low = at * UNROLL
-        for k in range(UNROLL):
-            pulled[pl.ds(low + k, 1), :] = table[pl.ds(place_ref[first + low + k], 1), :]
-        return carry
-
-    lax.fori_loop(0, block // UNROLL, pull, 0)
-
-    row = pl.multiple_of(step * groups, groups)
-    masked = mask_of(mask_ref[...], width)
-    agg_rows = rows_of(grad_agg[pl.ds(row, groups), :], nbrs)
-    grad_upd = (masked * (cot_ref[...].astype(f32) + masked * agg_rows)).astype(bf16)
-    pre_one = dot(edge_ref[...], one_ref[...]) + rows_of(src_proj[pl.ds(row, groups), :], nbrs)
-    pre_one = pre_one + pulled[...]
-    sigma_one = sigmoid(pre_one)
-    act_one = (pre_one * sigma_one).astype(bf16)
-    act_one_ref[...] = act_one
-    pre_two = dot(act_one, two_ref[...])
-    sigma_two = sigmoid(pre_two)
-    act_two_ref[...] = (pre_two * sigma_two).astype(bf16)
-    grad_two = (dot_turned(grad_upd, three_ref[...]) * deriv(pre_two, sigma_two)).astype(bf16)
-    grad_two_ref[...] = grad_two
-    grad_one = (dot_turned(grad_two, two_ref[...]) * deriv(pre_one, sigma_one)).astype(bf16)
-    grad_one_ref[...] = grad_one
-    grads[...] = grad_one.astype(f32)
-
-    def push(at, carry):
-        low = at * UNROLL
-        for k in range(UNROLL):
-            one = sums[k % len(sums)]
-            place = pl.ds(place_ref[first + low + k], 1)
-            one[place, :] += grads[pl.ds(low + k, 1), :]
-        return carry
-
-    lax.fori_loop(0, block // UNROLL, push, 0)
+    def pull(at):
+        for k in range(chunk):
+            place = place_ref[first + at * chunk + k]
+            pulled[at][pl.ds(k, 1), :] = table[pl.ds(place, 1), :]
+
+    def push(at):
+        for k in range(chunk):
+            one = sums[k % SUMS]
+            place = pl.ds(place_ref[first + at * chunk + k], 1)
+            one[place, :] += grads[at][pl.ds(k, 1), :]
+
+    def work(at):
+        span = pl.ds(at * chunk, chunk)
+        pre_one = base_ref[span, :] + pulled[at][...]
+        sigma_one = sigmoid(pre_one)
+        act_one = (pre_one * sigma_one).astype(bf16)
+        act_one_ref[span, :] = act_one
+        pre_two = dot(act_one, two_ref[...])
+        sigma_two = sigmoid(pre_two)
+        act_two_ref[span, :] = (pre_two * sigma_two).astype(bf16)
+        grad_two = (up_ref[span, :] * deriv(pre_two, sigma_two)).astype(bf16)
+        grad_two_ref[span, :] = grad_two
+        grad_one = (dot_turned(grad_two, two_ref[...]) * deriv(pre_one, sigma_one)).astype(bf16)
+        grad_one_ref[span, :] = grad_one
+        grads[at][...] = grad_one.astype(f32)
+
+    pull(0)
+    for at in range(CHUNKS):
+        if at + 1 < CHUNKS:
+            pull(at + 1)
+        work(at)
+        if at > 0:
+            push(at - 1)
+    push(CHUNKS - 1)
 
     @pl.when(step == pl.num_programs(0) - 1)
     def _():
@@ -165,39 +219,21 @@
         lax.fori_loop(0, count // PIECE, merge, 0)
 
 
-def whole(*shape):
-    return pl.BlockSpec(shape, lambda i, *places: (0,) * len(shape))
-
-
-def in_hbm(value):
-    return pltpu.with_memory_space_constraint(value, pltpu.HBM)
-
-
-def edge_chain(
-    places, table, edges, cots, mask, node_in, node_cot, w_src, w_one, w_two, w_three, w_node
-):
+def edge_chain(places, table, base, up, w_two):
     count, width = table.shape
     total = places.shape[0]
-    nodes, nbrs = mask.shape
-    deep = node_in.shape[1]
     f32, bf16 = jnp.float32, jnp.bfloat16
-    rest = (cots, mask, node_in, node_cot, w_src, w_one, w_two, w_three, w_node)
-    rest = tuple(map(in_hbm, rest))
     rows = pl.BlockSpec((BLOCK, width), lambda i, places: (i, 0))
-    masks = pl.BlockSpec((BLOCK // nbrs, nbrs), lambda i, places: (i, 0))
-    square = whole(width, width)
     held = pltpu.VMEM((count, width), f32)
-    part = pltpu.VMEM((BLOCK, width), f32)
-    small = pltpu.VMEM((nodes, width), f32)
+    part = pltpu.VMEM((BLOCK // CHUNKS, width), f32)
     return pl.pallas_call(
-        functools.partial(chain_body, 1.0 / math.sqrt(nbrs)),
+        chain_body,
         grid_spec=pltpu.PrefetchScalarGridSpec(
             num_scalar_prefetch=1,
             grid=(total // BLOCK,),
-            in_specs=[whole(count, width), rows, rows, masks, whole(nodes, deep)]
-            + [whole(nodes, deep), whole(deep, width), square, square, square, whole(width, deep)],
+            in_specs=[whole(count, width), rows, rows, whole(width, width)],
             out_specs=[rows] * 4 + [whole(count, width)],
-            scratch_shapes=[held, part, part, small, small] + [held] * SUMS,
+            scratch_shapes=[held] + [held] * SUMS + [part] * (2 * CHUNKS),
         ),
         out_shape=[pltpu.HBM((total, width), bf16)] * 4 + [pltpu.HBM((count, width), bf16)],
         compiler_params=pltpu.CompilerParams(vmem_limit_bytes=44 * 1024 * 1024),
@@ -205,7 +241,7 @@
             flops=8 * total * width * width, bytes_accessed=12 * 2**20, transcendentals=0
         ),
         name="edge_chain",
-    )(places, table, edges, *rest)
+    )(places, table, in_hbm(base), in_hbm(up), in_hbm(w_two))
 
 
 def side_body(
@@ -330,9 +366,9 @@
         message_ref[at, pl.ds(extra, rest), :] = late[at * rest : (at + 1) * rest]
 
 
-def meet(arriving, node_column, early):
+def meet(arriving, node_column, early, late_rows):
     blocks, share, width = arriving.shape
-    deep = node_column.shape[1] // 2
+    deep = late_rows
     height = (early.shape[0] + deep) // blocks
     return pl.pallas_call(
         meet_body,
@@ -349,6 +385,41 @@
         ),
         name="meet",
     )(arriving, in_hbm(node_column), in_hbm(early))
+
+
+def finish_body(node_scale, edge_scale, sums_ref, src_ref, dst_ref, one_ref, two_ref, three_ref, node_ref):
+    blocks, height, width = sums_ref.shape
+    deep = src_ref.shape[0]
+    piece = deep // blocks
+    extra = height - piece
+    for at in range(blocks):
+        late = sums_ref[at, pl.ds(extra, piece), :].astype(jnp.float32)
+        dst_ref[pl.ds(at * piece, piece), :] = late * node_scale
+    squares = (one_ref, two_ref, three_ref)
+    for low in range(0, 2 * deep + 3 * width, piece):
+        at, place = low // extra, low % extra
+        value = sums_ref[at, pl.ds(place, piece), :].astype(jnp.float32)
+        if low < deep:
+            src_ref[pl.ds(low, piece), :] = value * node_scale
+        elif low < deep + 3 * width:
+            which, row = (low - deep) // width, (low - deep) % width
+            squares[which][pl.ds(row, piece), :] = value * edge_scale
+        else:
+            slab, row = (low - deep - 3 * width) // width, (low - deep - 3 * width) % width
+            node_ref[pl.ds(row, piece), pl.ds(slab * width, width)] = value * node_scale
+
+
+def finish(sums, deep, node_scale, edge_scale):
+    width = sums.shape[2]
+    shapes = [(deep, width)] * 2 + [(width, width)] * 3 + [(width, deep)]
+    return pl.pallas_call(
+        functools.partial(finish_body, node_scale, edge_scale),
+        grid=(1,),
+        in_specs=[whole(*sums.shape)],
+        out_specs=[whole(*shape) for shape in shapes],
+        out_shape=[jax.ShapeDtypeStruct(shape, jnp.float32) for shape in shapes],
+        name="finish",
+    )(sums)
 
 
 def shards(
@@ -374,31 +445,21 @@
     node_scale = 1.0 / math.sqrt(total)
     edge_scale = 1.0 / math.sqrt(total * nbr_count)
 
-    column = spread(dot(node_in, w_dst).astype(bf16), RING)
+    proj = dot(node_in, w_dst).astype(bf16)
+    column = spread(jnp.concatenate([node_in, proj], axis=1), RING).reshape(-1, deep + width)
     own_row, rest = neighbours % row_count, neighbours // row_count
     at_x, rest = rest % wide, rest // wide
     places = ((at_x * (tall * long) + rest) * row_count + own_row).reshape(-1)
-    column, places, node_late = lax.optimization_barrier((column, places, jnp.concatenate([node_in, node_cot], axis=1)))
-    table = spread(column.reshape(-1, width), PLANE).reshape(total, width)
-    node_column = lax.all_gather(node_late, "z", axis=0, tiled=True)
-
+    column, places = lax.optimization_barrier((column, places))
+    table = spread(column[:, deep:], PLANE).reshape(total, width)
     edges = edge_in.reshape(row_count * nbr_count, width)
     cots = edge_cot.reshape(row_count * nbr_count, width)
-    *chain, message = edge_chain(
-        places,
-        table,
-        edges,
-        cots,
-        edge_mask,
-        node_in,
-        node_cot,
-        w_src,
-        w_edge_one,
-        w_edge_two,
-        w_edge_three,
-        w_node,
-    )
-    *chain, message, node_column = lax.optimization_barrier((*chain, message, node_column))
+    base, up = edge_prep(
+        edges, cots, edge_mask, node_in, node_cot, w_src, w_edge_one, w_edge_three, w_node
+    )
+    table, base, up = lax.optimization_barrier((table, base, up))
+    *chain, message = edge_chain(places, table, base, up, w_edge_two)
+    *chain, message = lax.optimization_barrier((*chain, message))
     arriving = exchange(message.reshape(blocks, -1, width), PLANE)
     extra = -(-(2 * deep + 3 * width) // (blocks * 16)) * 16
     edge_out, grad_edge, early, node_out, grad_node = edge_side(
@@ -414,26 +475,19 @@
         w_node,
         blocks * extra,
     )
-    partial, message = meet(arriving, node_column, early)
+    partial, message = meet(arriving, column, early, deep)
     weights = sum_first(exchange(message, PLANE)).astype(bf16)
     weights = jnp.broadcast_to(weights[None], (long, *weights.shape))
     packed = jnp.concatenate([partial.reshape(long, row_count, width), weights], axis=1)
     own = sum_first(exchange(packed, RING)).astype(bf16)
     grad_node = (grad_node + dot_turned(own[:row_count], w_dst)).astype(bf16)
-    sums = spread(own[row_count:], PLANE).astype(f32)
-    early = sums[:, :extra].reshape(-1, width)
-    late = sums[:, extra:].reshape(-1, width)
-    ones = [early[at : at + width] * edge_scale for at in range(deep, deep + 3 * width, width)]
-    slabs = [early[at : at + width] for at in range(deep + 3 * width, 2 * deep + 3 * width, width)]
+    weights = finish(spread(own[row_count:], PLANE), deep, node_scale, edge_scale)
     return (
         node_out,
         edge_out.reshape(edge_in.shape),
         grad_node,
         grad_edge.reshape(edge_in.shape),
-        early[:deep] * node_scale,
-        late * node_scale,
-        *ones,
-        jnp.concatenate(slabs, axis=1) * node_scale,
+        *weights,
     )
 
 

time: 169 us -> 167 us (0.988)
  between operations: 14.1 us -> 0.74 us
  waiting for transfers between devices: 60.9 us -> 72.1 us
  other arithmetic: 5.49 us -> 1.09 us
  Pallas kernels: 27 us -> 31.3 us
    all_to_all x4, waiting for transfers between devices: 60.2 us -> 72.1 us  [exchange(): return lax.all_to_all(value, axes, 0, 0, tiled=True)]
    pallas_call x1 -> x3, Pallas kernels: 18.3 us -> 22.6 us  [the longest x1 15.2 us: edge_chain(): pl.pallas_call(chain_body, grid_spec=pltpu.PrefetchScalarGridSpec(num_sca...]
    mul x3 -> x0, other arithmetic: 2.19 us -> none  [the longest x1 0.73 us: shards(): jnp.concatenate(slabs, axis=1) * node_scale]
  transfers between devices with their start and end apart: 5 -> 4, of which waited for: 4 -> 4; matrix products, arithmetic and copies ran while one was open for 2% -> 1% of each run, Pallas kernels for 15% -> 7%
where the time goes in v6:
time: 167 us; the launch traced here: 166 us
  waiting for transfers between devices  72.1 us (43%)
  Pallas kernels  31.3 us (19%)
  blocking collectives  27.8 us (17%)
  starting transfers between devices  25.7 us (15%)
  local copies, waits for them, and re-layouts  5.35 us (3%)
  matrix products  1.8 us (1%)
    all_to_all x4, waiting for transfers between devices, exchange(): return lax.all_to_all(value, axes, 0, 0, tiled=True)  72.1 us
    all_to_all x2, blocking collectives, exchange(): return lax.all_to_all(value, axes, 0, 0, tiled=True)  27.8 us
    all_to_all x4, starting transfers between devices, exchange(): return lax.all_to_all(value, axes, 0, 0, tiled=True)  25.7 us
    pallas_call x1, Pallas kernels, edge_chain(): pl.pallas_call(chain_body, grid_spec=pltpu.PrefetchScalarGridSpec(num_sca...  15.2 us
    pallas_call x1, Pallas kernels, edge_side(): pl.pallas_call(functools.partial(side_body, 1.0 / math.sqrt(nbrs)), grid=...  6.95 us
    pallas_call x1, Pallas kernels, edge_prep(): pl.pallas_call(functools.partial(prep_body, 1.0 / math.sqrt(nbrs)), grid=...  5.31 us
    broadcast_in_dim x3, local copies, waits for them, and re-layouts, spread(): return exchange(jnp.broadcast_to(value[None], (count, *value.shape)), axes)  3.52 us
  transfers between devices with their start and end apart: 4, of which 4 were waited for; matrix products, arithmetic and copies ran while one was open for 1% of the time, Pallas kernels for 7%

profile of v6, /device:TPU:8, one launch (start us, length us, event | category | flops | bytes accessed | tf_op | source)
XLA Modules:
  0.0 165.9 jit_solution(16085393169057726043)
XLA Ops:
  0.6 0.0 copy-start
  0.7 0.0 copy-start.4
  0.7 0.9 copy-done
  1.6 1.0 convolution_convert_fusion
  2.5 0.9 pad_maximum_fusion.1
  3.4 0.9 broadcast_in_dim.8
  4.3 8.5 %all-to-all-start = ((bf16[8,64,640]{2,1,0:T(8,128)(2,1)}), bf16[8,64,640]{2,1,0:T(8,128)(2,1)S(1)}, u32[]{:S(2)}, u32[]{:S(2)}) async-start(bf16[8,64,640]{2,1,0:T(8,128)(2,1)} %broadcast_in_dim.8), calls=%async_computation | async-start | bytes 1310720 | tf_op jit(solution)/shard_map/all_to_all | solution.py:23
  12.8 0.0 copy-done.4
  12.8 0.1 fusion.4
  12.8 0.1 reshape.54.place_ref
  12.9 20.2 %all-to-all-done = bf16[8,64,640]{2,1,0:T(8,128)(2,1)S(1)} async-done(((bf16[8,64,640]{2,1,0:T(8,128)(2,1)}), bf16[8,64,640]{2,1,0:T(8,128)(2,1)S(1)}, u32[]{:S(2)}, u32[]{:S(2)}) %all-to-all-start) | async-done | bytes 655392 | tf_op jit(solution)/shard_map/all_to_all | solution.py:23
  33.1 0.0 copy-start.1
  33.1 1.7 %broadcast_in_dim.9 = bf16[16,512,128]{2,1,0:T(8,128)(2,1)} broadcast(bf16[512,128]{1,0:T(8,128)(2,1)S(1)} %slice.9), dimensions={1,2} | broadcast | bytes 2228224 | tf_op jit(solution)/shard_map/broadcast_in_dim | solution.py:28
  34.8 0.0 copy-done.1
  34.8 7.4 %all-to-all-start.1 = ((bf16[16,512,128]{2,1,0:T(8,128)(2,1)}), bf16[16,512,128]{2,1,0:T(8,128)(2,1)S(1)}, u32[]{:S(2)}, u32[]{:S(2)}) async-start(bf16[16,512,128]{2,1,0:T(8,128)(2,1)} %broadcast_in_dim.9), calls=%async_computation.1 | async-start | bytes 4194304 | tf_op jit(solution)/shard_map/all_to_all | solution.py:23
  42.2 5.3 %edge_prep.1 = (f32[4096,128]{1,0:T(8,128)}, f32[4096,128]{1,0:T(8,128)}) custom-call(bf16[4096,128]{1,0:T(8,128)(2,1)} %bitcast.13, bf16[4096,128]{1,0:T(8,128)(2,1)} %bitcast.15, s32[64,64]{1,0:T(8,128)} %mask_ref.3, bf16[64,512]{1,0:T(8,128)(2,1)} %node_ref.3, bf16[64,512]{1,0:T(8,128)(2,1)} %node_cot_ref.3, bf16[512,128]{1,0:T(8,128)(2,1)} %w_src_ref.3, ...), custom_call_target="tpu_custom_call" | custom-call | flops 268435456 | bytes 12582912 | tf_op jit(solution)/shard_map/edge_prep/pallas_call | solution.py:124
  47.5 24.0 %all-to-all-done.1 = bf16[16,512,128]{2,1,0:T(8,128)(2,1)S(1)} async-done(((bf16[16,512,128]{2,1,0:T(8,128)(2,1)}), bf16[16,512,128]{2,1,0:T(8,128)(2,1)S(1)}, u32[]{:S(2)}, u32[]{:S(2)}) %all-to-all-start.1) | async-done | bytes 2097184 | tf_op jit(solution)/shard_map/all_to_all | solution.py:23
  71.5 15.2 %edge_chain.1 = (bf16[4096,128]{1,0:T(8,128)(2,1)}, bf16[4096,128]{1,0:T(8,128)(2,1)}, bf16[4096,128]{1,0:T(8,128)(2,1)}, bf16[4096,128]{1,0:T(8,128)(2,1)}, bf16[8192,128]{1,0:T(8,128)(2,1)}) custom-call(s32[4096]{0:T(1024)S(1)} %reshape.54.place_ref, bf16[8192,128]{1,0:T(8,128)(2,1)S(1)} %bitcast.11, f32[4096,128]{1,0:T(8,128)} %get-tuple-element.40.base_ref, ...), custom_call_target="tpu_custom_call" | custom-call | flops 536870912 | bytes 12582912 | tf_op jit(solution)/shard_map/edge_chain/pallas_call | solution.py:229
  86.8 5.0 %all-to-all-start.2 = ((bf16[16,512,128]{2,1,0:T(8,128)(2,1)}), bf16[16,512,128]{2,1,0:T(8,128)(2,1)S(1)}, u32[]{:S(2)}, u32[]{:S(2)}) async-start(bf16[16,512,128]{2,1,0:T(8,128)(2,1)} %bitcast.19), calls=%async_computation.2 | async-start | bytes 4194304 | tf_op jit(solution)/shard_map/all_to_all | solution.py:23
  91.8 7.0 %edge_side.1 = (bf16[4096,128]{1,0:T(8,128)(2,1)}, bf16[4096,128]{1,0:T(8,128)(2,1)}, bf16[1536,128]{1,0:T(8,128)(2,1)}, bf16[64,512]{1,0:T(8,128)(2,1)}, f32[64,512]{1,0:T(8,128)}) custom-call(bf16[4096,128]{1,0:T(8,128)(2,1)} %bitcast.14, bf16[4096,128]{1,0:T(8,128)(2,1)} %bitcast.16, s32[64,64]{1,0:T(8,128)} %mask_ref.3, ...), custom_call_target="tpu_custom_call" | custom-call | flops 671088640 | bytes 25165824 | tf_op jit(solution)/shard_map/edge_side/pallas_call | solution.py:335
  98.7 19.9 %all-to-all-done.2.arriving_ref = bf16[16,512,128]{2,1,0:T(8,128)(2,1)S(1)} async-done(((bf16[16,512,128]{2,1,0:T(8,128)(2,1)}), bf16[16,512,128]{2,1,0:T(8,128)(2,1)S(1)}, u32[]{:S(2)}, u32[]{:S(2)}) %all-to-all-start.2) | async-done | bytes 2097184 | tf_op jit(solution)/shard_map/all_to_all | solution.py:23
  118.7 1.7 %meet.1 = (bf16[512,128]{1,0:T(8,128)(2,1)S(1)}, bf16[16,128,128]{2,1,0:T(8,128)(2,1)S(1)}) custom-call(bf16[16,512,128]{2,1,0:T(8,128)(2,1)S(1)} %all-to-all-done.2.arriving_ref, bf16[512,640]{1,0:T(8,128)(2,1)} %bitcast.18, bf16[1536,128]{1,0:T(8,128)(2,1)} %get-tuple-element.50.early_ref), custom_call_target="tpu_custom_call" | custom-call | flops 67108864 | bytes 4194304 | tf_op jit(solution)/shard_map/meet/pallas_call | solution.py:373
  120.4 13.6 %all_to_all.30 = bf16[16,128,128]{2,1,0:T(8,128)(2,1)S(1)} all-to-all(bf16[16,128,128]{2,1,0:T(8,128)(2,1)S(1)} %get-tuple-element.52), channel_id=1, replica_groups=mesh['cplx'=2,'y'=4,'z'=8,'x'=4] {'x','y'}, dimensions={0} | all-to-all | bytes 1048576 | tf_op jit(solution)/shard_map/all_to_all | solution.py:23
  134.0 0.1 reduce_sum.24
  134.1 0.0 copy-start.3
  134.1 14.3 %all_to_all.31 = bf16[8,192,128]{2,1,0:T(8,128)(2,1)S(1)} all-to-all(bf16[8,192,128]{2,1,0:T(8,128)(2,1)S(1)} %pad_maximum_fusion), channel_id=1, replica_groups=mesh['cplx'=2,'y'=4,'z'=8,'x'=4] {'z'}, dimensions={0} | all-to-all | bytes 786432 | tf_op jit(solution)/shard_map/all_to_all | solution.py:23
  148.4 0.1 reduce_sum.25
  148.5 0.9 broadcast_in_dim.11
  149.4 4.8 %all-to-all-start.5 = ((bf16[16,128,128]{2,1,0:T(8,128)(2,1)}), bf16[16,128,128]{2,1,0:T(8,128)(2,1)S(1)}, u32[]{:S(2)}, u32[]{:S(2)}) async-start(bf16[16,128,128]{2,1,0:T(8,128)(2,1)} %broadcast_in_dim.11), calls=%async_computation.5 | async-start | bytes 1048576 | tf_op jit(solution)/shard_map/all_to_all | solution.py:23
  154.2 0.0 copy-done.3
  154.2 0.8 fusion
  155.0 8.0 %all-to-all-done.5.sums_ref = bf16[16,128,128]{2,1,0:T(8,128)(2,1)S(1)} async-done(((bf16[16,128,128]{2,1,0:T(8,128)(2,1)}), bf16[16,128,128]{2,1,0:T(8,128)(2,1)S(1)}, u32[]{:S(2)}, u32[]{:S(2)}) %all-to-all-start.5) | async-done | bytes 524320 | tf_op jit(solution)/shard_map/all_to_all | solution.py:23
  163.0 0.0 copy-start.2
  163.0 0.8 copy-done.2
  163.8 2.0 %finish.1 = (f32[512,128]{1,0:T(8,128)}, f32[512,128]{1,0:T(8,128)}, f32[128,128]{1,0:T(8,128)}, f32[128,128]{1,0:T(8,128)}, f32[128,128]{1,0:T(8,128)}, /*index=5*/f32[128,512]{1,0:T(8,128)}) custom-call(bf16[16,128,128]{2,1,0:T(8,128)(2,1)} %copy-done.2), custom_call_target="tpu_custom_call" | custom-call | tf_op jit(solution)/shard_map/finish/pallas_call | solution.py:415
  (4 shorter events, 0.1 us)
Async XLA Ops:
  0.6 0.9 copy-start
  0.7 12.1 %copy-start.4 = (s32[64,64]{1,0:T(8,128)S(1)}, s32[64,64]{1,0:T(8,128)}, u32[]{:S(2)}) copy-start(s32[64,64]{1,0:T(8,128)} %param.14) | copy-start | bytes 49156
  4.3 28.8 %all-to-all-start = ((bf16[8,64,640]{2,1,0:T(8,128)(2,1)}), bf16[8,64,640]{2,1,0:T(8,128)(2,1)S(1)}, u32[]{:S(2)}, u32[]{:S(2)}) async-start(bf16[8,64,640]{2,1,0:T(8,128)(2,1)} %broadcast_in_dim.8), calls=%async_computation | async-start | bytes 1310720 | tf_op jit(solution)/shard_map/all_to_all | solution.py:23
  33.1 1.7 %copy-start.1 = (bf16[8,64,640]{2,1,0:T(8,128)(2,1)}, bf16[8,64,640]{2,1,0:T(8,128)(2,1)S(1)}, u32[]{:S(2)}) copy-start(bf16[8,64,640]{2,1,0:T(8,128)(2,1)S(1)} %all-to-all-done) | copy-start | bytes 1966084
  34.8 36.7 %all-to-all-start.1 = ((bf16[16,512,128]{2,1,0:T(8,128)(2,1)}), bf16[16,512,128]{2,1,0:T(8,128)(2,1)S(1)}, u32[]{:S(2)}, u32[]{:S(2)}) async-start(bf16[16,512,128]{2,1,0:T(8,128)(2,1)} %broadcast_in_dim.9), calls=%async_computation.1 | async-start | bytes 4194304 | tf_op jit(solution)/shard_map/all_to_all | solution.py:23
  86.8 31.9 %all-to-all-start.2 = ((bf16[16,512,128]{2,1,0:T(8,128)(2,1)}), bf16[16,512,128]{2,1,0:T(8,128)(2,1)S(1)}, u32[]{:S(2)}, u32[]{:S(2)}) async-start(bf16[16,512,128]{2,1,0:T(8,128)(2,1)} %bitcast.19), calls=%async_computation.2 | async-start | bytes 4194304 | tf_op jit(solution)/shard_map/all_to_all | solution.py:23
  134.1 20.2 %copy-start.3 = (f32[64,512]{1,0:T(8,128)S(1)}, f32[64,512]{1,0:T(8,128)}, u32[]{:S(2)}) copy-start(f32[64,512]{1,0:T(8,128)} %get-tuple-element.48) | copy-start | bytes 393220
  149.4 13.6 %all-to-all-start.5 = ((bf16[16,128,128]{2,1,0:T(8,128)(2,1)}), bf16[16,128,128]{2,1,0:T(8,128)(2,1)S(1)}, u32[]{:S(2)}, u32[]{:S(2)}) async-start(bf16[16,128,128]{2,1,0:T(8,128)(2,1)} %broadcast_in_dim.11), calls=%async_computation.5 | async-start | bytes 1048576 | tf_op jit(solution)/shard_map/all_to_all | solution.py:23
  163.0 0.8 copy-start.2

commit v7 on v6

--- a/solution.py
+++ b/solution.py
@@ -231,7 +231,7 @@
         grid_spec=pltpu.PrefetchScalarGridSpec(
             num_scalar_prefetch=1,
             grid=(total // BLOCK,),
-            in_specs=[whole(count, width), rows, rows, whole(width, width)],
+            in_specs=[pl.BlockSpec(memory_space=pltpu.VMEM), rows, rows, whole(width, width)],
             out_specs=[rows] * 4 + [whole(count, width)],
             scratch_shapes=[held] + [held] * SUMS + [part] * (2 * CHUNKS),
         ),
@@ -350,31 +350,42 @@
     )(*map(in_hbm, (edges, cots)), in_hbm(mask), *map(in_hbm, chain), *rest)
 
 
-def meet_body(arriving_ref, node_ref, early_ref, partial_ref, message_ref):
+def meet_body(turn_ref, arriving_ref, early_ref, *rest):
+    *node_refs, partial_ref, message_ref = rest
     blocks, share, width = arriving_ref.shape
+    count = len(node_refs)
+    own = share // count
     bf16, f32 = jnp.bfloat16, jnp.float32
     value = arriving_ref[0].astype(f32)
     for at in range(1, blocks):
         value = value + arriving_ref[at].astype(f32)
-    partial = value.astype(bf16)
-    partial_ref[...] = partial
-    late = dot_rows(node_ref[...], partial).astype(bf16)
-    rest = late.shape[0] // blocks
+    partial_ref[...] = value.astype(bf16)
+    late = None
+    for shift, node_ref in enumerate(node_refs):
+        place = lax.rem(turn_ref[0] + (count - shift), count)
+        rows = pl.ds(pl.multiple_of(place * own, own), own)
+        term = dot_rows(node_ref[...], partial_ref[rows, :])
+        late = term if late is None else late + term
+    late = late.astype(bf16)
+    piece = late.shape[0] // blocks
     extra = early_ref.shape[0] // blocks
     for at in range(blocks):
         message_ref[at, pl.ds(0, extra), :] = early_ref[pl.ds(at * extra, extra), :]
-        message_ref[at, pl.ds(extra, rest), :] = late[at * rest : (at + 1) * rest]
-
-
-def meet(arriving, node_column, early, late_rows):
+        message_ref[at, pl.ds(extra, piece), :] = late[at * piece : (at + 1) * piece]
+
+
+def meet(turn, arriving, nodes, early):
     blocks, share, width = arriving.shape
-    deep = late_rows
+    own, deep = nodes[0].shape
     height = (early.shape[0] + deep) // blocks
     return pl.pallas_call(
         meet_body,
-        grid=(1,),
-        in_specs=[whole(*arriving.shape), whole(share, deep), whole(*early.shape)],
-        out_specs=[whole(share, width), whole(blocks, height, width)],
+        grid_spec=pltpu.PrefetchScalarGridSpec(
+            num_scalar_prefetch=1,
+            grid=(1,),
+            in_specs=[whole(*arriving.shape), whole(*early.shape)] + [whole(own, deep)] * len(nodes),
+            out_specs=[whole(share, width), whole(blocks, height, width)],
+        ),
         out_shape=[
             jax.ShapeDtypeStruct((share, width), jnp.bfloat16),
             jax.ShapeDtypeStruct((blocks, height, width), jnp.bfloat16),
@@ -384,7 +395,7 @@
             flops=2 * share * deep * width, bytes_accessed=4 * 2**20, transcendentals=0
         ),
         name="meet",
-    )(arriving, in_hbm(node_column), in_hbm(early))
+    )(turn, arriving, in_hbm(early), *map(in_hbm, nodes))
 
 
 def finish_body(node_scale, edge_scale, sums_ref, src_ref, dst_ref, one_ref, two_ref, three_ref, node_ref):
@@ -445,21 +456,24 @@
     node_scale = 1.0 / math.sqrt(total)
     edge_scale = 1.0 / math.sqrt(total * nbr_count)
 
-    proj = dot(node_in, w_dst).astype(bf16)
-    column = spread(jnp.concatenate([node_in, proj], axis=1), RING).reshape(-1, deep + width)
+    column = spread(dot(node_in, w_dst).astype(bf16), RING)
     own_row, rest = neighbours % row_count, neighbours // row_count
     at_x, rest = rest % wide, rest // wide
     places = ((at_x * (tall * long) + rest) * row_count + own_row).reshape(-1)
-    column, places = lax.optimization_barrier((column, places))
-    table = spread(column[:, deep:], PLANE).reshape(total, width)
+    column, places, node_late = lax.optimization_barrier((column, places, node_in))
+    table = spread(column.reshape(-1, width), PLANE).reshape(total, width)
+    turns = [[(at, (at + shift) % long) for at in range(long)] for shift in range(long)]
+    nodes = [node_in] + [lax.ppermute(node_late, "z", pairs) for pairs in turns[1 : long // 2]]
     edges = edge_in.reshape(row_count * nbr_count, width)
     cots = edge_cot.reshape(row_count * nbr_count, width)
     base, up = edge_prep(
         edges, cots, edge_mask, node_in, node_cot, w_src, w_edge_one, w_edge_three, w_node
     )
-    table, base, up = lax.optimization_barrier((table, base, up))
+    half = long // 2
+    table, base, up, *nodes = lax.optimization_barrier((table, base, up, *nodes))
     *chain, message = edge_chain(places, table, base, up, w_edge_two)
-    *chain, message = lax.optimization_barrier((*chain, message))
+    *chain, message, node_late = lax.optimization_barrier((*chain, message, node_late))
+    nodes += [lax.ppermute(node_late, "z", pairs) for pairs in turns[half:]]
     arriving = exchange(message.reshape(blocks, -1, width), PLANE)
     extra = -(-(2 * deep + 3 * width) // (blocks * 16)) * 16
     edge_out, grad_edge, early, node_out, grad_node = edge_side(
@@ -475,7 +489,9 @@
         w_node,
         blocks * extra,
     )
-    partial, message = meet(arriving, column, early, deep)
+    arriving, early, *nodes = lax.optimization_barrier((arriving, early, *nodes))
+    turn = jnp.full((1,), lax.axis_index("z"), jnp.int32)
+    partial, message = meet(turn, arriving, nodes, early)
     weights = sum_first(exchange(message, PLANE)).astype(bf16)
     weights = jnp.broadcast_to(weights[None], (long, *weights.shape))
     packed = jnp.concatenate([partial.reshape(long, row_count, width), weights], axis=1)

time: 167 us -> 153 us (0.916)
  waiting for transfers between devices: 72.1 us -> 45.7 us
  starting transfers between devices: 25.7 us -> 37.5 us
    all_to_all x4, waiting for transfers between devices: 72.1 us -> 44.8 us  [exchange(): return lax.all_to_all(value, axes, 0, 0, tiled=True)]
    ppermute x0 -> x7, starting transfers between devices: none -> 11.3 us  [the longest x4 7.96 us: shards(): nodes += [lax.ppermute(node_late, 'z', pairs) for pairs in turns[half:]]]
  transfers between devices with their start and end apart: 4 -> 11, of which waited for: 4 -> 6; matrix products, arithmetic and copies ran while one was open for 1% -> 1% of each run, Pallas kernels for 7% -> 8%
where the time goes in v7:
time: 153 us; the launch traced here: 152 us
  waiting for transfers between devices  45.7 us (30%)
  starting transfers between devices  37.5 us (25%)
  Pallas kernels  31.5 us (21%)
  blocking collectives  28.6 us (19%)
  local copies, waits for them, and re-layouts  5.19 us (3%)
  matrix products  1.79 us (1%)
    all_to_all x4, waiting for transfers between devices, exchange(): return lax.all_to_all(value, axes, 0, 0, tiled=True)  44.8 us
    all_to_all x2, blocking collectives, exchange(): return lax.all_to_all(value, axes, 0, 0, tiled=True)  28.6 us
    all_to_all x4, starting transfers between devices, exchange(): return lax.all_to_all(value, axes, 0, 0, tiled=True)  26.2 us
    pallas_call x1, Pallas kernels, edge_chain(): pl.pallas_call(chain_body, grid_spec=pltpu.PrefetchScalarGridSpec(num_sca...  15.2 us
    ppermute x4, starting transfers between devices, shards(): nodes += [lax.ppermute(node_late, 'z', pairs) for pairs in turns[half:]]  7.96 us
    pallas_call x1, Pallas kernels, edge_side(): pl.pallas_call(functools.partial(side_body, 1.0 / math.sqrt(nbrs)), grid=...  6.96 us
    pallas_call x1, Pallas kernels, edge_prep(): pl.pallas_call(functools.partial(prep_body, 1.0 / math.sqrt(nbrs)), grid=...  5.26 us
    ppermute x3, starting transfers between devices, shards(): lax.ppermute(node_late, 'z', pairs)  3.39 us
  transfers between devices with their start and end apart: 11, of which 6 were waited for; matrix products, arithmetic and copies ran while one was open for 1% of the time, Pallas kernels for 8%

profile of v7, /device:TPU:8, one launch (start us, length us, event | category | flops | bytes accessed | tf_op | source)
XLA Modules:
  0.0 152.1 jit_solution(2053036383270246334)
XLA Ops:
  0.6 0.0 copy-start
  0.7 0.9 copy-done
  1.6 1.0 convolution_convert_fusion
  2.5 0.7 broadcast_in_dim.12
  3.2 8.5 %all-to-all-start = ((bf16[8,64,128]{2,1,0:T(8,128)(2,1)}), bf16[8,64,128]{2,1,0:T(8,128)(2,1)S(1)}, u32[]{:S(2)}, u32[]{:S(2)}) async-start(bf16[8,64,128]{2,1,0:T(8,128)(2,1)} %broadcast_in_dim.12), calls=%async_computation | async-start | bytes 262144 | tf_op jit(solution)/shard_map/all_to_all | solution.py:23
  11.7 0.8 fusion.4
  12.5 0.1 reshape.50.place_ref
  12.6 8.2 %all-to-all-done = bf16[8,64,128]{2,1,0:T(8,128)(2,1)S(1)} async-done(((bf16[8,64,128]{2,1,0:T(8,128)(2,1)}), bf16[8,64,128]{2,1,0:T(8,128)(2,1)S(1)}, u32[]{:S(2)}, u32[]{:S(2)}) %all-to-all-start) | async-done | bytes 131104 | tf_op jit(solution)/shard_map/all_to_all | solution.py:23
  20.8 1.7 %broadcast_in_dim.14 = bf16[16,512,128]{2,1,0:T(8,128)(2,1)} broadcast(bf16[512,128]{1,0:T(8,128)(2,1)S(1)} %bitcast.19), dimensions={1,2} | broadcast | bytes 2228224 | tf_op jit(solution)/shard_map/broadcast_in_dim | solution.py:28
  22.5 7.5 %all-to-all-start.1 = ((bf16[16,512,128]{2,1,0:T(8,128)(2,1)}), bf16[16,512,128]{2,1,0:T(8,128)(2,1)S(1)}, u32[]{:S(2)}, u32[]{:S(2)}) async-start(bf16[16,512,128]{2,1,0:T(8,128)(2,1)} %broadcast_in_dim.14), calls=%async_computation.1 | async-start | bytes 4194304 | tf_op jit(solution)/shard_map/all_to_all | solution.py:23
  30.1 0.4 collective-permute-start
  30.5 0.7 collective-permute-start.1
  31.2 2.2 %collective-permute-start.2 = (bf16[64,512]{1,0:T(8,128)(2,1)S(1)}, bf16[64,512]{1,0:T(8,128)(2,1)S(1)}, u32[]{:S(2)}, u32[]{:S(2)}) collective-permute-start(bf16[64,512]{1,0:T(8,128)(2,1)S(1)} %copy-done.2), channel_id=1, source_target_pairs={{0,12},{4,16},{8,20},{12,24},{16,28},{20,0},{24,4},{28,8},{1,13},{... | collective-permute-start | bytes 196616 | tf_op jit(solution)/shard_map/ppermute | solution.py:466
  33.4 5.3 %edge_prep.1 = (f32[4096,128]{1,0:T(8,128)}, f32[4096,128]{1,0:T(8,128)}) custom-call(bf16[4096,128]{1,0:T(8,128)(2,1)} %bitcast.14, bf16[4096,128]{1,0:T(8,128)(2,1)} %bitcast.16, s32[64,64]{1,0:T(8,128)} %mask_ref.3, bf16[64,512]{1,0:T(8,128)(2,1)} %rest_0_, bf16[64,512]{1,0:T(8,128)(2,1)} %node_cot_ref.3, bf16[512,128]{1,0:T(8,128)(2,1)} %w_src_ref.3, ...), custom_call_target="tpu_custom_call" | custom-call | flops 268435456 | bytes 12582912 | tf_op jit(solution)/shard_map/edge_prep/pallas_call | solution.py:124
  38.7 0.0 collective-permute-done.rest_1_
  38.7 0.0 copy-start.5
  38.7 0.7 collective-permute-done.1.rest_2_
  39.5 0.2 collective-permute-done.2.rest_3_
  39.7 17.1 %all-to-all-done.1 = bf16[16,512,128]{2,1,0:T(8,128)(2,1)S(1)} async-done(((bf16[16,512,128]{2,1,0:T(8,128)(2,1)}), bf16[16,512,128]{2,1,0:T(8,128)(2,1)S(1)}, u32[]{:S(2)}, u32[]{:S(2)}) %all-to-all-start.1) | async-done | bytes 2097184 | tf_op jit(solution)/shard_map/all_to_all | solution.py:23
  56.8 15.2 %edge_chain.1 = (bf16[4096,128]{1,0:T(8,128)(2,1)}, bf16[4096,128]{1,0:T(8,128)(2,1)}, bf16[4096,128]{1,0:T(8,128)(2,1)}, bf16[4096,128]{1,0:T(8,128)(2,1)}, bf16[8192,128]{1,0:T(8,128)(2,1)}) custom-call(s32[4096]{0:T(1024)S(1)} %reshape.50.place_ref, bf16[8192,128]{1,0:T(8,128)(2,1)S(1)} %bitcast.12, f32[4096,128]{1,0:T(8,128)} %get-tuple-element.62.base_ref, ...), custom_call_target="tpu_custom_call" | custom-call | flops 536870912 | bytes 12582912 | tf_op jit(solution)/shard_map/edge_chain/pallas_call | solution.py:229
  72.1 0.0 copy-start.3
  72.1 5.4 %all-to-all-start.2 = ((bf16[16,512,128]{2,1,0:T(8,128)(2,1)}), bf16[16,512,128]{2,1,0:T(8,128)(2,1)S(1)}, u32[]{:S(2)}, u32[]{:S(2)}) async-start(bf16[16,512,128]{2,1,0:T(8,128)(2,1)} %bitcast.18), calls=%async_computation.2 | async-start | bytes 4194304 | tf_op jit(solution)/shard_map/all_to_all | solution.py:23
  77.5 0.9 collective-permute-start.3
  78.4 4.3 %collective-permute-start.4 = (bf16[64,512]{1,0:T(8,128)(2,1)S(1)}, bf16[64,512]{1,0:T(8,128)(2,1)S(1)}, u32[]{:S(2)}, u32[]{:S(2)}) collective-permute-start(bf16[64,512]{1,0:T(8,128)(2,1)S(1)} %copy-done.3), channel_id=1, source_target_pairs={{0,20},{4,24},{8,28},{12,0},{16,4},{20,8},{24,12},{28,16},{1,21},{... | collective-permute-start | bytes 196616 | tf_op jit(solution)/shard_map/ppermute | solution.py:476
  82.7 0.7 collective-permute-start.5
  83.4 2.0 %collective-permute-start.6 = (bf16[64,512]{1,0:T(8,128)(2,1)S(1)}, bf16[64,512]{1,0:T(8,128)(2,1)S(1)}, u32[]{:S(2)}, u32[]{:S(2)}) collective-permute-start(bf16[64,512]{1,0:T(8,128)(2,1)S(1)} %copy-done.3), channel_id=1, source_target_pairs={{0,28},{4,0},{8,4},{12,8},{16,12},{20,16},{24,20},{28,24},{1,29},{... | collective-permute-start | bytes 196616 | tf_op jit(solution)/shard_map/ppermute | solution.py:476
  85.4 7.0 %edge_side.1 = (bf16[4096,128]{1,0:T(8,128)(2,1)}, bf16[4096,128]{1,0:T(8,128)(2,1)}, bf16[1536,128]{1,0:T(8,128)(2,1)}, bf16[64,512]{1,0:T(8,128)(2,1)}, f32[64,512]{1,0:T(8,128)}) custom-call(bf16[4096,128]{1,0:T(8,128)(2,1)} %bitcast.15, bf16[4096,128]{1,0:T(8,128)(2,1)} %bitcast.17, s32[64,64]{1,0:T(8,128)} %mask_ref.3, ...), custom_call_target="tpu_custom_call" | custom-call | flops 671088640 | bytes 25165824 | tf_op jit(solution)/shard_map/edge_side/pallas_call | solution.py:335
  92.4 0.0 collective-permute-done.3.rest_4_
  92.4 0.0 copy-start.8
  92.4 0.0 collective-permute-done.4.rest_5_
  92.4 0.0 copy-start.9
  92.5 0.0 collective-permute-done.5.rest_6_
  92.5 0.0 copy-start.10
  92.5 0.0 collective-permute-done.6.rest_7_
  92.5 11.4 %all-to-all-done.2.arriving_ref = bf16[16,512,128]{2,1,0:T(8,128)(2,1)S(1)} async-done(((bf16[16,512,128]{2,1,0:T(8,128)(2,1)}), bf16[16,512,128]{2,1,0:T(8,128)(2,1)S(1)}, u32[]{:S(2)}, u32[]{:S(2)}) %all-to-all-start.2) | async-done | bytes 2097184 | tf_op jit(solution)/shard_map/all_to_all | solution.py:23
  103.9 0.0 copy-done.9
  103.9 2.0 %meet.1 = (bf16[512,128]{1,0:T(8,128)(2,1)S(1)}, bf16[16,128,128]{2,1,0:T(8,128)(2,1)S(1)}) custom-call(s32[1]{0:T(128)} %bitcast.5.turn_ref, bf16[16,512,128]{2,1,0:T(8,128)(2,1)S(1)} %all-to-all-done.2.arriving_ref, bf16[1536,128]{1,0:T(8,128)(2,1)} %get-tuple-element.84.early_ref, bf16[64,512]{1,0:T(8,128)(2,1)} %rest_0_, bf16[64,512]{1,0:T(8,128)(2,1)} %copy-done.5, ...), custom_call_target="tpu_custom_call" | custom-call | flops 67108864 | bytes 4194304 | tf_op jit(solution)/shard_map/meet/pallas_call | solution.py:381
  105.9 14.3 %all_to_all.30 = bf16[16,128,128]{2,1,0:T(8,128)(2,1)S(1)} all-to-all(bf16[16,128,128]{2,1,0:T(8,128)(2,1)S(1)} %get-tuple-element.94), channel_id=1, replica_groups=mesh['cplx'=2,'y'=4,'z'=8,'x'=4] {'x','y'}, dimensions={0} | all-to-all | bytes 1048576 | tf_op jit(solution)/shard_map/all_to_all | solution.py:23
  120.2 0.1 reduce_sum.24
  120.3 0.0 copy-start.4
  120.4 14.3 %all_to_all.31 = bf16[8,192,128]{2,1,0:T(8,128)(2,1)S(1)} all-to-all(bf16[8,192,128]{2,1,0:T(8,128)(2,1)S(1)} %pad_maximum_fusion), channel_id=1, replica_groups=mesh['cplx'=2,'y'=4,'z'=8,'x'=4] {'z'}, dimensions={0} | all-to-all | bytes 786432 | tf_op jit(solution)/shard_map/all_to_all | solution.py:23
  134.7 0.1 reduce_sum.25
  134.7 0.9 broadcast_in_dim.33
  135.6 4.8 %all-to-all-start.5 = ((bf16[16,128,128]{2,1,0:T(8,128)(2,1)}), bf16[16,128,128]{2,1,0:T(8,128)(2,1)S(1)}, u32[]{:S(2)}, u32[]{:S(2)}) async-start(bf16[16,128,128]{2,1,0:T(8,128)(2,1)} %broadcast_in_dim.33), calls=%async_computation.5 | async-start | bytes 1048576 | tf_op jit(solution)/shard_map/all_to_all | solution.py:23
  140.5 0.8 fusion
  141.3 8.0 %all-to-all-done.5.sums_ref = bf16[16,128,128]{2,1,0:T(8,128)(2,1)S(1)} async-done(((bf16[16,128,128]{2,1,0:T(8,128)(2,1)}), bf16[16,128,128]{2,1,0:T(8,128)(2,1)S(1)}, u32[]{:S(2)}, u32[]{:S(2)}) %all-to-all-start.5) | async-done | bytes 524320 | tf_op jit(solution)/shard_map/all_to_all | solution.py:23
  149.3 0.8 copy-done.1
  150.1 2.0 %finish.1 = (f32[512,128]{1,0:T(8,128)}, f32[512,128]{1,0:T(8,128)}, f32[128,128]{1,0:T(8,128)}, f32[128,128]{1,0:T(8,128)}, f32[128,128]{1,0:T(8,128)}, /*index=5*/f32[128,512]{1,0:T(8,128)}) custom-call(bf16[16,128,128]{2,1,0:T(8,128)(2,1)} %copy-done.1), custom_call_target="tpu_custom_call" | custom-call | tf_op jit(solution)/shard_map/finish/pallas_call | solution.py:426
  (17 shorter events, 0.1 us)
Async XLA Ops:
  0.6 0.9 copy-start
  3.2 17.6 %all-to-all-start = ((bf16[8,64,128]{2,1,0:T(8,128)(2,1)}), bf16[8,64,128]{2,1,0:T(8,128)(2,1)S(1)}, u32[]{:S(2)}, u32[]{:S(2)}) async-start(bf16[8,64,128]{2,1,0:T(8,128)(2,1)} %broadcast_in_dim.12), calls=%async_computation | async-start | bytes 262144 | tf_op jit(solution)/shard_map/all_to_all | solution.py:23
  22.5 7.5 %copy-start.2 = (bf16[64,512]{1,0:T(8,128)(2,1)S(1)}, bf16[64,512]{1,0:T(8,128)(2,1)}, u32[]{:S(2)}) copy-start(bf16[64,512]{1,0:T(8,128)(2,1)} %rest_0_) | copy-start | bytes 196612
  22.5 34.3 %all-to-all-start.1 = ((bf16[16,512,128]{2,1,0:T(8,128)(2,1)}), bf16[16,512,128]{2,1,0:T(8,128)(2,1)S(1)}, u32[]{:S(2)}, u32[]{:S(2)}) async-start(bf16[16,512,128]{2,1,0:T(8,128)(2,1)} %broadcast_in_dim.14), calls=%async_computation.1 | async-start | bytes 4194304 | tf_op jit(solution)/shard_map/all_to_all | solution.py:23
  30.1 8.7 %collective-permute-start = (bf16[64,512]{1,0:T(8,128)(2,1)S(1)}, bf16[64,512]{1,0:T(8,128)(2,1)S(1)}, u32[]{:S(2)}, u32[]{:S(2)}) collective-permute-start(bf16[64,512]{1,0:T(8,128)(2,1)S(1)} %copy-done.2), channel_id=1, source_target_pairs={{0,4},{4,8},{8,12},{12,16},{16,20},{20,24},{24,28},{28,0},{1,5},{5... | collective-permute-start | bytes 196616 | tf_op jit(solution)/shard_map/ppermute | solution.py:466
  30.5 9.0 %collective-permute-start.1 = (bf16[64,512]{1,0:T(8,128)(2,1)S(1)}, bf16[64,512]{1,0:T(8,128)(2,1)S(1)}, u32[]{:S(2)}, u32[]{:S(2)}) collective-permute-start(bf16[64,512]{1,0:T(8,128)(2,1)S(1)} %copy-done.2), channel_id=1, source_target_pairs={{0,8},{4,12},{8,16},{12,20},{16,24},{20,28},{24,0},{28,4},{1,9},{5... | collective-permute-start | bytes 196616 | tf_op jit(solution)/shard_map/ppermute | solution.py:466
  31.2 8.4 %collective-permute-start.2 = (bf16[64,512]{1,0:T(8,128)(2,1)S(1)}, bf16[64,512]{1,0:T(8,128)(2,1)S(1)}, u32[]{:S(2)}, u32[]{:S(2)}) collective-permute-start(bf16[64,512]{1,0:T(8,128)(2,1)S(1)} %copy-done.2), channel_id=1, source_target_pairs={{0,12},{4,16},{8,20},{12,24},{16,28},{20,0},{24,4},{28,8},{1,13},{... | collective-permute-start | bytes 196616 | tf_op jit(solution)/shard_map/ppermute | solution.py:466
  38.7 33.3 %copy-start.5 = (bf16[64,512]{1,0:T(8,128)(2,1)}, bf16[64,512]{1,0:T(8,128)(2,1)S(1)}, u32[]{:S(2)}) copy-start(bf16[64,512]{1,0:T(8,128)(2,1)S(1)} %collective-permute-done.rest_1_) | copy-start | bytes 196612
  39.5 32.6 %copy-start.6 = (bf16[64,512]{1,0:T(8,128)(2,1)}, bf16[64,512]{1,0:T(8,128)(2,1)S(1)}, u32[]{:S(2)}) copy-start(bf16[64,512]{1,0:T(8,128)(2,1)S(1)} %collective-permute-done.1.rest_2_) | copy-start | bytes 196612
  39.7 32.4 %copy-start.7 = (bf16[64,512]{1,0:T(8,128)(2,1)}, bf16[64,512]{1,0:T(8,128)(2,1)S(1)}, u32[]{:S(2)}) copy-start(bf16[64,512]{1,0:T(8,128)(2,1)S(1)} %collective-permute-done.2.rest_3_) | copy-start | bytes 196612
  72.1 5.4 %copy-start.3 = (bf16[64,512]{1,0:T(8,128)(2,1)S(1)}, bf16[64,512]{1,0:T(8,128)(2,1)}, u32[]{:S(2)}) copy-start(bf16[64,512]{1,0:T(8,128)(2,1)} %rest_0_) | copy-start | bytes 196612
  72.1 31.8 %all-to-all-start.2 = ((bf16[16,512,128]{2,1,0:T(8,128)(2,1)}), bf16[16,512,128]{2,1,0:T(8,128)(2,1)S(1)}, u32[]{:S(2)}, u32[]{:S(2)}) async-start(bf16[16,512,128]{2,1,0:T(8,128)(2,1)} %bitcast.18), calls=%async_computation.2 | async-start | bytes 4194304 | tf_op jit(solution)/shard_map/all_to_all | solution.py:23
  77.5 14.9 %collective-permute-start.3 = (bf16[64,512]{1,0:T(8,128)(2,1)S(1)}, bf16[64,512]{1,0:T(8,128)(2,1)S(1)}, u32[]{:S(2)}, u32[]{:S(2)}) collective-permute-start(bf16[64,512]{1,0:T(8,128)(2,1)S(1)} %copy-done.3), channel_id=1, source_target_pairs={{0,16},{4,20},{8,24},{12,28},{16,0},{20,4},{24,8},{28,12},{1,17},{... | collective-permute-start | bytes 196616 | tf_op jit(solution)/shard_map/ppermute | solution.py:476
  78.4 14.1 %collective-permute-start.4 = (bf16[64,512]{1,0:T(8,128)(2,1)S(1)}, bf16[64,512]{1,0:T(8,128)(2,1)S(1)}, u32[]{:S(2)}, u32[]{:S(2)}) collective-permute-start(bf16[64,512]{1,0:T(8,128)(2,1)S(1)} %copy-done.3), channel_id=1, source_target_pairs={{0,20},{4,24},{8,28},{12,0},{16,4},{20,8},{24,12},{28,16},{1,21},{... | collective-permute-start | bytes 196616 | tf_op jit(solution)/shard_map/ppermute | solution.py:476
  82.7 9.8 %collective-permute-start.5 = (bf16[64,512]{1,0:T(8,128)(2,1)S(1)}, bf16[64,512]{1,0:T(8,128)(2,1)S(1)}, u32[]{:S(2)}, u32[]{:S(2)}) collective-permute-start(bf16[64,512]{1,0:T(8,128)(2,1)S(1)} %copy-done.3), channel_id=1, source_target_pairs={{0,24},{4,28},{8,0},{12,4},{16,8},{20,12},{24,16},{28,20},{1,25},{... | collective-permute-start | bytes 196616 | tf_op jit(solution)/shard_map/ppermute | solution.py:476
  83.4 9.1 %collective-permute-start.6 = (bf16[64,512]{1,0:T(8,128)(2,1)S(1)}, bf16[64,512]{1,0:T(8,128)(2,1)S(1)}, u32[]{:S(2)}, u32[]{:S(2)}) collective-permute-start(bf16[64,512]{1,0:T(8,128)(2,1)S(1)} %copy-done.3), channel_id=1, source_target_pairs={{0,28},{4,0},{8,4},{12,8},{16,12},{20,16},{24,20},{28,24},{1,29},{... | collective-permute-start | bytes 196616 | tf_op jit(solution)/shard_map/ppermute | solution.py:476
  92.4 11.5 %copy-start.8 = (bf16[64,512]{1,0:T(8,128)(2,1)}, bf16[64,512]{1,0:T(8,128)(2,1)S(1)}, u32[]{:S(2)}) copy-start(bf16[64,512]{1,0:T(8,128)(2,1)S(1)} %collective-permute-done.3.rest_4_) | copy-start | bytes 196612
  92.4 11.5 %copy-start.9 = (bf16[64,512]{1,0:T(8,128)(2,1)}, bf16[64,512]{1,0:T(8,128)(2,1)S(1)}, u32[]{:S(2)}) copy-start(bf16[64,512]{1,0:T(8,128)(2,1)S(1)} %collective-permute-done.4.rest_5_) | copy-start | bytes 196612
  92.5 11.5 %copy-start.10 = (bf16[64,512]{1,0:T(8,128)(2,1)}, bf16[64,512]{1,0:T(8,128)(2,1)S(1)}, u32[]{:S(2)}) copy-start(bf16[64,512]{1,0:T(8,128)(2,1)S(1)} %collective-permute-done.5.rest_6_) | copy-start | bytes 196612
  92.5 11.4 %copy-start.11 = (bf16[64,512]{1,0:T(8,128)(2,1)}, bf16[64,512]{1,0:T(8,128)(2,1)S(1)}, u32[]{:S(2)}) copy-start(bf16[64,512]{1,0:T(8,128)(2,1)S(1)} %collective-permute-done.6.rest_7_) | copy-start | bytes 196612
  120.3 20.2 %copy-start.4 = (f32[64,512]{1,0:T(8,128)S(1)}, f32[64,512]{1,0:T(8,128)}, u32[]{:S(2)}) copy-start(f32[64,512]{1,0:T(8,128)} %get-tuple-element.75) | copy-start | bytes 393220
  135.6 13.6 %all-to-all-start.5 = ((bf16[16,128,128]{2,1,0:T(8,128)(2,1)}), bf16[16,128,128]{2,1,0:T(8,128)(2,1)S(1)}, u32[]{:S(2)}, u32[]{:S(2)}) async-start(bf16[16,128,128]{2,1,0:T(8,128)(2,1)} %broadcast_in_dim.33), calls=%async_computation.5 | async-start | bytes 1048576 | tf_op jit(solution)/shard_map/all_to_all | solution.py:23
  149.3 0.8 copy-start.1

commit v8 on v7

--- a/solution.py
+++ b/solution.py
@@ -14,7 +14,7 @@
 ALL = ("y", "z", "x")
 SUMS = 4
 BLOCK = 1024
-CHUNKS = 4
+CHUNKS = 8
 SIDE_BLOCK = 1024
 PIECE = 512
 
@@ -67,6 +67,33 @@
     count = turned.shape[0]
     columns = [jnp.broadcast_to(turned[:, j : j + 1], (count, width)) for j in range(mask.shape[0])]
     return jnp.concatenate(columns, axis=0)
+
+
+def project_body(node_ref, weight_ref, out_ref):
+    value = dot(node_ref[...], weight_ref[...]).astype(jnp.bfloat16)
+    for at in range(out_ref.shape[0]):
+        out_ref[at] = value
+
+
+def whole(*shape):
+    return pl.BlockSpec(shape, lambda i, *places: (0,) * len(shape))
+
+
+def in_hbm(value):
+    return pltpu.with_memory_space_constraint(value, pltpu.HBM)
+
+
+def project(node_in, weight, count):
+    nodes, width = node_in.shape[0], weight.shape[1]
+    return pl.pallas_call(
+        project_body,
+        grid=(1,),
+        in_specs=[whole(*node_in.shape), whole(*weight.shape)],
+        out_specs=whole(count, nodes, width),
+        out_shape=pltpu.HBM((count, nodes, width), jnp.bfloat16),
+        compiler_params=pltpu.CompilerParams(vmem_limit_bytes=8 * 1024 * 1024),
+        name="project",
+    )(in_hbm(node_in), in_hbm(weight))
 
 
 def prep_body(
@@ -102,14 +129,6 @@
     up_ref[...] = dot_turned(grad_upd, three_ref[...])
     src_rows = rows_of(src_proj[pl.ds(row, groups), :], nbrs)
     base_ref[...] = dot(edge_ref[...], one_ref[...]) + src_rows
-
-
-def in_hbm(value):
-    return pltpu.with_memory_space_constraint(value, pltpu.HBM)
-
-
-def whole(*shape):
-    return pl.BlockSpec(shape, lambda i, *places: (0,) * len(shape))
 
 
 def edge_prep(edges, cots, mask, node_in, node_cot, w_src, w_one, w_three, w_node):
@@ -426,9 +445,10 @@
     return pl.pallas_call(
         functools.partial(finish_body, node_scale, edge_scale),
         grid=(1,),
-        in_specs=[whole(*sums.shape)],
+        in_specs=[pl.BlockSpec(memory_space=pltpu.VMEM)],
         out_specs=[whole(*shape) for shape in shapes],
-        out_shape=[jax.ShapeDtypeStruct(shape, jnp.float32) for shape in shapes],
+        out_shape=[pltpu.HBM(shape, jnp.float32) for shape in shapes],
+        compiler_params=pltpu.CompilerParams(vmem_limit_bytes=8 * 1024 * 1024),
         name="finish",
     )(sums)
 
@@ -456,7 +476,7 @@
     node_scale = 1.0 / math.sqrt(total)
     edge_scale = 1.0 / math.sqrt(total * nbr_count)
 
-    column = spread(dot(node_in, w_dst).astype(bf16), RING)
+    column = exchange(project(node_in, w_dst, long), RING)
     own_row, rest = neighbours % row_count, neighbours // row_count
     at_x, rest = rest % wide, rest // wide
     places = ((at_x * (tall * long) + rest) * row_count + own_row).reshape(-1)

time: 153 us -> 150 us (0.980)
  local copies, waits for them, and re-layouts: 5.19 us -> 2.82 us
    pallas_call x0 -> x1, Pallas kernels: none -> 1.76 us  [project(): pl.pallas_call(project_body, grid=(1,), in_specs=[whole(*node_in.shape),...]
    unnamed x24 -> x22, local copies, waits for them, and re-layouts: 1.75 us -> 0.06 us
    broadcast_in_dim x3 -> x2, local copies, waits for them, and re-layouts: 3.32 us -> 2.65 us  [spread(): return exchange(jnp.broadcast_to(value[None], (count, *value.shape)), axes)]
where the time goes in v8:
time: 150 us; the launch traced here: 149 us
  waiting for transfers between devices  45.7 us (30%)
  starting transfers between devices  37.5 us (25%)
  Pallas kernels  31.8 us (21%)
  blocking collectives  28.7 us (19%)
  local copies, waits for them, and re-layouts  2.82 us (2%)
    all_to_all x4, waiting for transfers between devices, exchange(): return lax.all_to_all(value, axes, 0, 0, tiled=True)  44.8 us
    all_to_all x2, blocking collectives, exchange(): return lax.all_to_all(value, axes, 0, 0, tiled=True)  28.7 us
    all_to_all x4, starting transfers between devices, exchange(): return lax.all_to_all(value, axes, 0, 0, tiled=True)  26.2 us
    pallas_call x1, Pallas kernels, edge_chain(): pl.pallas_call(chain_body, grid_spec=pltpu.PrefetchScalarGridSpec(num_sca...  14.8 us
    ppermute x4, starting transfers between devices, shards(): nodes += [lax.ppermute(node_late, 'z', pairs) for pairs in turns[half:]]  7.95 us
    pallas_call x1, Pallas kernels, edge_side(): pl.pallas_call(functools.partial(side_body, 1.0 / math.sqrt(nbrs)), grid=...  6.95 us
    pallas_call x1, Pallas kernels, edge_prep(): pl.pallas_call(functools.partial(prep_body, 1.0 / math.sqrt(nbrs)), grid=...  5.27 us
    ppermute x3, starting transfers between devices, shards(): lax.ppermute(node_late, 'z', pairs)  3.39 us
  transfers between devices with their start and end apart: 11, of which 6 were waited for; matrix products, arithmetic and copies ran while one was open for 1% of the time, Pallas kernels for 8%

profile of v8, /device:TPU:8, one launch (start us, length us, event | category | flops | bytes accessed | tf_op | source)
XLA Modules:
  0.0 149.2 jit_solution(16199459180022847907)
XLA Ops:
  0.6 1.8 %project.1 = bf16[8,64,128]{2,1,0:T(8,128)(2,1)} custom-call(bf16[64,512]{1,0:T(8,128)(2,1)} %rest_0_, bf16[512,128]{1,0:T(8,128)(2,1)} %weight_ref.1), custom_call_target="tpu_custom_call" | custom-call | tf_op jit(solution)/shard_map/project/pallas_call | solution.py:88
  2.4 8.5 %all-to-all-start = ((bf16[8,64,128]{2,1,0:T(8,128)(2,1)}), bf16[8,64,128]{2,1,0:T(8,128)(2,1)S(1)}, u32[]{:S(2)}, u32[]{:S(2)}) async-start(bf16[8,64,128]{2,1,0:T(8,128)(2,1)} %project.1), calls=%async_computation | async-start | bytes 262144 | tf_op jit(solution)/shard_map/all_to_all | solution.py:23
  10.9 0.8 fusion.4
  11.7 0.1 reshape.49.place_ref
  11.8 8.2 %all-to-all-done = bf16[8,64,128]{2,1,0:T(8,128)(2,1)S(1)} async-done(((bf16[8,64,128]{2,1,0:T(8,128)(2,1)}), bf16[8,64,128]{2,1,0:T(8,128)(2,1)S(1)}, u32[]{:S(2)}, u32[]{:S(2)}) %all-to-all-start) | async-done | bytes 131104 | tf_op jit(solution)/shard_map/all_to_all | solution.py:23
  20.0 1.7 %broadcast_in_dim.11 = bf16[16,512,128]{2,1,0:T(8,128)(2,1)} broadcast(bf16[512,128]{1,0:T(8,128)(2,1)S(1)} %bitcast.17), dimensions={1,2} | broadcast | bytes 2228224 | tf_op jit(solution)/shard_map/broadcast_in_dim | solution.py:28
  21.7 7.5 %all-to-all-start.1 = ((bf16[16,512,128]{2,1,0:T(8,128)(2,1)}), bf16[16,512,128]{2,1,0:T(8,128)(2,1)S(1)}, u32[]{:S(2)}, u32[]{:S(2)}) async-start(bf16[16,512,128]{2,1,0:T(8,128)(2,1)} %broadcast_in_dim.11), calls=%async_computation.1 | async-start | bytes 4194304 | tf_op jit(solution)/shard_map/all_to_all | solution.py:23
  29.2 0.4 collective-permute-start
  29.7 0.7 collective-permute-start.1
  30.4 2.2 %collective-permute-start.2 = (bf16[64,512]{1,0:T(8,128)(2,1)S(1)}, bf16[64,512]{1,0:T(8,128)(2,1)S(1)}, u32[]{:S(2)}, u32[]{:S(2)}) collective-permute-start(bf16[64,512]{1,0:T(8,128)(2,1)S(1)} %copy-done), channel_id=1, source_target_pairs={{0,12},{4,16},{8,20},{12,24},{16,28},{20,0},{24,4},{28,8},{1,13},{... | collective-permute-start | bytes 196616 | tf_op jit(solution)/shard_map/ppermute | solution.py:486
  32.6 5.3 %edge_prep.1 = (f32[4096,128]{1,0:T(8,128)}, f32[4096,128]{1,0:T(8,128)}) custom-call(bf16[4096,128]{1,0:T(8,128)(2,1)} %bitcast.12, bf16[4096,128]{1,0:T(8,128)(2,1)} %bitcast.14, s32[64,64]{1,0:T(8,128)} %mask_ref.3, bf16[64,512]{1,0:T(8,128)(2,1)} %rest_0_, bf16[64,512]{1,0:T(8,128)(2,1)} %node_cot_ref.3, bf16[512,128]{1,0:T(8,128)(2,1)} %w_src_ref.3, ...), custom_call_target="tpu_custom_call" | custom-call | flops 268435456 | bytes 12582912 | tf_op jit(solution)/shard_map/edge_prep/pallas_call | solution.py:143
  37.9 0.0 collective-permute-done.rest_1_
  37.9 0.0 copy-start.4
  37.9 0.8 collective-permute-done.1.rest_2_
  38.7 0.1 collective-permute-done.2.rest_3_
  38.8 17.2 %all-to-all-done.1 = bf16[16,512,128]{2,1,0:T(8,128)(2,1)S(1)} async-done(((bf16[16,512,128]{2,1,0:T(8,128)(2,1)}), bf16[16,512,128]{2,1,0:T(8,128)(2,1)S(1)}, u32[]{:S(2)}, u32[]{:S(2)}) %all-to-all-start.1) | async-done | bytes 2097184 | tf_op jit(solution)/shard_map/all_to_all | solution.py:23
  56.0 14.8 %edge_chain.1 = (bf16[4096,128]{1,0:T(8,128)(2,1)}, bf16[4096,128]{1,0:T(8,128)(2,1)}, bf16[4096,128]{1,0:T(8,128)(2,1)}, bf16[4096,128]{1,0:T(8,128)(2,1)}, bf16[8192,128]{1,0:T(8,128)(2,1)}) custom-call(s32[4096]{0:T(1024)S(1)} %reshape.49.place_ref, bf16[8192,128]{1,0:T(8,128)(2,1)S(1)} %bitcast.10, f32[4096,128]{1,0:T(8,128)} %get-tuple-element.62.base_ref, ...), custom_call_target="tpu_custom_call" | custom-call | flops 536870912 | bytes 12582912 | tf_op jit(solution)/shard_map/edge_chain/pallas_call | solution.py:248
  70.8 0.0 copy-start.1
  70.9 5.4 %all-to-all-start.2 = ((bf16[16,512,128]{2,1,0:T(8,128)(2,1)}), bf16[16,512,128]{2,1,0:T(8,128)(2,1)S(1)}, u32[]{:S(2)}, u32[]{:S(2)}) async-start(bf16[16,512,128]{2,1,0:T(8,128)(2,1)} %bitcast.16), calls=%async_computation.2 | async-start | bytes 4194304 | tf_op jit(solution)/shard_map/all_to_all | solution.py:23
  76.3 0.0 copy-done.1
  76.3 0.9 collective-permute-start.3
  77.1 4.3 %collective-permute-start.4 = (bf16[64,512]{1,0:T(8,128)(2,1)S(1)}, bf16[64,512]{1,0:T(8,128)(2,1)S(1)}, u32[]{:S(2)}, u32[]{:S(2)}) collective-permute-start(bf16[64,512]{1,0:T(8,128)(2,1)S(1)} %copy-done.1), channel_id=1, source_target_pairs={{0,20},{4,24},{8,28},{12,0},{16,4},{20,8},{24,12},{28,16},{1,21},{... | collective-permute-start | bytes 196616 | tf_op jit(solution)/shard_map/ppermute | solution.py:496
  81.5 0.7 collective-permute-start.5
  82.2 2.0 %collective-permute-start.6 = (bf16[64,512]{1,0:T(8,128)(2,1)S(1)}, bf16[64,512]{1,0:T(8,128)(2,1)S(1)}, u32[]{:S(2)}, u32[]{:S(2)}) collective-permute-start(bf16[64,512]{1,0:T(8,128)(2,1)S(1)} %copy-done.1), channel_id=1, source_target_pairs={{0,28},{4,0},{8,4},{12,8},{16,12},{20,16},{24,20},{28,24},{1,29},{... | collective-permute-start | bytes 196616 | tf_op jit(solution)/shard_map/ppermute | solution.py:496
  84.2 7.0 %edge_side.1 = (bf16[4096,128]{1,0:T(8,128)(2,1)}, bf16[4096,128]{1,0:T(8,128)(2,1)}, bf16[1536,128]{1,0:T(8,128)(2,1)}, bf16[64,512]{1,0:T(8,128)(2,1)}, f32[64,512]{1,0:T(8,128)}) custom-call(bf16[4096,128]{1,0:T(8,128)(2,1)} %bitcast.13, bf16[4096,128]{1,0:T(8,128)(2,1)} %bitcast.15, s32[64,64]{1,0:T(8,128)} %mask_ref.3, ...), custom_call_target="tpu_custom_call" | custom-call | flops 671088640 | bytes 25165824 | tf_op jit(solution)/shard_map/edge_side/pallas_call | solution.py:354
  91.2 0.0 collective-permute-done.3.rest_4_
  91.2 0.0 copy-start.7
  91.2 0.0 collective-permute-done.4.rest_5_
  91.2 0.0 copy-start.8
  91.2 0.0 collective-permute-done.5.rest_6_
  91.2 0.0 copy-start.9
  91.2 0.0 collective-permute-done.6.rest_7_
  91.3 11.4 %all-to-all-done.2.arriving_ref = bf16[16,512,128]{2,1,0:T(8,128)(2,1)S(1)} async-done(((bf16[16,512,128]{2,1,0:T(8,128)(2,1)}), bf16[16,512,128]{2,1,0:T(8,128)(2,1)S(1)}, u32[]{:S(2)}, u32[]{:S(2)}) %all-to-all-start.2) | async-done | bytes 2097184 | tf_op jit(solution)/shard_map/all_to_all | solution.py:23
  102.7 0.0 copy-done.7
  102.7 2.0 %meet.1 = (bf16[512,128]{1,0:T(8,128)(2,1)S(1)}, bf16[16,128,128]{2,1,0:T(8,128)(2,1)S(1)}) custom-call(s32[1]{0:T(128)} %bitcast.5.turn_ref, bf16[16,512,128]{2,1,0:T(8,128)(2,1)S(1)} %all-to-all-done.2.arriving_ref, bf16[1536,128]{1,0:T(8,128)(2,1)} %get-tuple-element.84.early_ref, bf16[64,512]{1,0:T(8,128)(2,1)} %rest_0_, bf16[64,512]{1,0:T(8,128)(2,1)} %copy-done.4, ...), custom_call_target="tpu_custom_call" | custom-call | flops 67108864 | bytes 4194304 | tf_op jit(solution)/shard_map/meet/pallas_call | solution.py:400
  104.7 14.3 %all_to_all.30 = bf16[16,128,128]{2,1,0:T(8,128)(2,1)S(1)} all-to-all(bf16[16,128,128]{2,1,0:T(8,128)(2,1)S(1)} %get-tuple-element.94), channel_id=1, replica_groups=mesh['cplx'=2,'y'=4,'z'=8,'x'=4] {'x','y'}, dimensions={0} | all-to-all | bytes 1048576 | tf_op jit(solution)/shard_map/all_to_all | solution.py:23
  119.0 0.1 reduce_sum.24
  119.0 0.0 copy-start.2
  119.0 0.0 copy-start.3
  119.1 14.5 %all_to_all.31 = bf16[8,192,128]{2,1,0:T(8,128)(2,1)S(1)} all-to-all(bf16[8,192,128]{2,1,0:T(8,128)(2,1)S(1)} %pad_maximum_fusion), channel_id=1, replica_groups=mesh['cplx'=2,'y'=4,'z'=8,'x'=4] {'z'}, dimensions={0} | all-to-all | bytes 786432 | tf_op jit(solution)/shard_map/all_to_all | solution.py:23
  133.6 0.1 reduce_sum.25
  133.7 0.9 broadcast_in_dim.26
  134.6 4.8 %all-to-all-start.5 = ((bf16[16,128,128]{2,1,0:T(8,128)(2,1)}), bf16[16,128,128]{2,1,0:T(8,128)(2,1)S(1)}, u32[]{:S(2)}, u32[]{:S(2)}) async-start(bf16[16,128,128]{2,1,0:T(8,128)(2,1)} %broadcast_in_dim.26), calls=%async_computation.5 | async-start | bytes 1048576 | tf_op jit(solution)/shard_map/all_to_all | solution.py:23
  139.4 0.0 copy-done.2
  139.4 0.0 copy-done.3
  139.4 0.8 fusion
  140.2 8.0 %all-to-all-done.5.sums_ref = bf16[16,128,128]{2,1,0:T(8,128)(2,1)S(1)} async-done(((bf16[16,128,128]{2,1,0:T(8,128)(2,1)}), bf16[16,128,128]{2,1,0:T(8,128)(2,1)S(1)}, u32[]{:S(2)}, u32[]{:S(2)}) %all-to-all-start.5) | async-done | bytes 524320 | tf_op jit(solution)/shard_map/all_to_all | solution.py:23
  148.2 1.0 finish.1
  (14 shorter events, 0.1 us)
Async XLA Ops:
  2.4 17.6 %all-to-all-start = ((bf16[8,64,128]{2,1,0:T(8,128)(2,1)}), bf16[8,64,128]{2,1,0:T(8,128)(2,1)S(1)}, u32[]{:S(2)}, u32[]{:S(2)}) async-start(bf16[8,64,128]{2,1,0:T(8,128)(2,1)} %project.1), calls=%async_computation | async-start | bytes 262144 | tf_op jit(solution)/shard_map/all_to_all | solution.py:23
  21.7 7.5 %copy-start = (bf16[64,512]{1,0:T(8,128)(2,1)S(1)}, bf16[64,512]{1,0:T(8,128)(2,1)}, u32[]{:S(2)}) copy-start(bf16[64,512]{1,0:T(8,128)(2,1)} %rest_0_) | copy-start | bytes 196612
  21.7 34.3 %all-to-all-start.1 = ((bf16[16,512,128]{2,1,0:T(8,128)(2,1)}), bf16[16,512,128]{2,1,0:T(8,128)(2,1)S(1)}, u32[]{:S(2)}, u32[]{:S(2)}) async-start(bf16[16,512,128]{2,1,0:T(8,128)(2,1)} %broadcast_in_dim.11), calls=%async_computation.1 | async-start | bytes 4194304 | tf_op jit(solution)/shard_map/all_to_all | solution.py:23
  29.2 8.7 %collective-permute-start = (bf16[64,512]{1,0:T(8,128)(2,1)S(1)}, bf16[64,512]{1,0:T(8,128)(2,1)S(1)}, u32[]{:S(2)}, u32[]{:S(2)}) collective-permute-start(bf16[64,512]{1,0:T(8,128)(2,1)S(1)} %copy-done), channel_id=1, source_target_pairs={{0,4},{4,8},{8,12},{12,16},{16,20},{20,24},{24,28},{28,0},{1,5},{5... | collective-permute-start | bytes 196616 | tf_op jit(solution)/shard_map/ppermute | solution.py:486
  29.7 9.0 %collective-permute-start.1 = (bf16[64,512]{1,0:T(8,128)(2,1)S(1)}, bf16[64,512]{1,0:T(8,128)(2,1)S(1)}, u32[]{:S(2)}, u32[]{:S(2)}) collective-permute-start(bf16[64,512]{1,0:T(8,128)(2,1)S(1)} %copy-done), channel_id=1, source_target_pairs={{0,8},{4,12},{8,16},{12,20},{16,24},{20,28},{24,0},{28,4},{1,9},{5... | collective-permute-start | bytes 196616 | tf_op jit(solution)/shard_map/ppermute | solution.py:486
  30.4 8.4 %collective-permute-start.2 = (bf16[64,512]{1,0:T(8,128)(2,1)S(1)}, bf16[64,512]{1,0:T(8,128)(2,1)S(1)}, u32[]{:S(2)}, u32[]{:S(2)}) collective-permute-start(bf16[64,512]{1,0:T(8,128)(2,1)S(1)} %copy-done), channel_id=1, source_target_pairs={{0,12},{4,16},{8,20},{12,24},{16,28},{20,0},{24,4},{28,8},{1,13},{... | collective-permute-start | bytes 196616 | tf_op jit(solution)/shard_map/ppermute | solution.py:486
  37.9 32.9 %copy-start.4 = (bf16[64,512]{1,0:T(8,128)(2,1)}, bf16[64,512]{1,0:T(8,128)(2,1)S(1)}, u32[]{:S(2)}) copy-start(bf16[64,512]{1,0:T(8,128)(2,1)S(1)} %collective-permute-done.rest_1_) | copy-start | bytes 196612
  38.7 32.1 %copy-start.5 = (bf16[64,512]{1,0:T(8,128)(2,1)}, bf16[64,512]{1,0:T(8,128)(2,1)S(1)}, u32[]{:S(2)}) copy-start(bf16[64,512]{1,0:T(8,128)(2,1)S(1)} %collective-permute-done.1.rest_2_) | copy-start | bytes 196612
  38.8 32.0 %copy-start.6 = (bf16[64,512]{1,0:T(8,128)(2,1)}, bf16[64,512]{1,0:T(8,128)(2,1)S(1)}, u32[]{:S(2)}) copy-start(bf16[64,512]{1,0:T(8,128)(2,1)S(1)} %collective-permute-done.2.rest_3_) | copy-start | bytes 196612
  70.8 5.4 %copy-start.1 = (bf16[64,512]{1,0:T(8,128)(2,1)S(1)}, bf16[64,512]{1,0:T(8,128)(2,1)}, u32[]{:S(2)}) copy-start(bf16[64,512]{1,0:T(8,128)(2,1)} %rest_0_) | copy-start | bytes 196612
  70.9 31.8 %all-to-all-start.2 = ((bf16[16,512,128]{2,1,0:T(8,128)(2,1)}), bf16[16,512,128]{2,1,0:T(8,128)(2,1)S(1)}, u32[]{:S(2)}, u32[]{:S(2)}) async-start(bf16[16,512,128]{2,1,0:T(8,128)(2,1)} %bitcast.16), calls=%async_computation.2 | async-start | bytes 4194304 | tf_op jit(solution)/shard_map/all_to_all | solution.py:23
  76.3 14.9 %collective-permute-start.3 = (bf16[64,512]{1,0:T(8,128)(2,1)S(1)}, bf16[64,512]{1,0:T(8,128)(2,1)S(1)}, u32[]{:S(2)}, u32[]{:S(2)}) collective-permute-start(bf16[64,512]{1,0:T(8,128)(2,1)S(1)} %copy-done.1), channel_id=1, source_target_pairs={{0,16},{4,20},{8,24},{12,28},{16,0},{20,4},{24,8},{28,12},{1,17},{... | collective-permute-start | bytes 196616 | tf_op jit(solution)/shard_map/ppermute | solution.py:496
  77.1 14.1 %collective-permute-start.4 = (bf16[64,512]{1,0:T(8,128)(2,1)S(1)}, bf16[64,512]{1,0:T(8,128)(2,1)S(1)}, u32[]{:S(2)}, u32[]{:S(2)}) collective-permute-start(bf16[64,512]{1,0:T(8,128)(2,1)S(1)} %copy-done.1), channel_id=1, source_target_pairs={{0,20},{4,24},{8,28},{12,0},{16,4},{20,8},{24,12},{28,16},{1,21},{... | collective-permute-start | bytes 196616 | tf_op jit(solution)/shard_map/ppermute | solution.py:496
  81.5 9.8 %collective-permute-start.5 = (bf16[64,512]{1,0:T(8,128)(2,1)S(1)}, bf16[64,512]{1,0:T(8,128)(2,1)S(1)}, u32[]{:S(2)}, u32[]{:S(2)}) collective-permute-start(bf16[64,512]{1,0:T(8,128)(2,1)S(1)} %copy-done.1), channel_id=1, source_target_pairs={{0,24},{4,28},{8,0},{12,4},{16,8},{20,12},{24,16},{28,20},{1,25},{... | collective-permute-start | bytes 196616 | tf_op jit(solution)/shard_map/ppermute | solution.py:496
  82.2 9.1 %collective-permute-start.6 = (bf16[64,512]{1,0:T(8,128)(2,1)S(1)}, bf16[64,512]{1,0:T(8,128)(2,1)S(1)}, u32[]{:S(2)}, u32[]{:S(2)}) collective-permute-start(bf16[64,512]{1,0:T(8,128)(2,1)S(1)} %copy-done.1), channel_id=1, source_target_pairs={{0,28},{4,0},{8,4},{12,8},{16,12},{20,16},{24,20},{28,24},{1,29},{... | collective-permute-start | bytes 196616 | tf_op jit(solution)/shard_map/ppermute | solution.py:496
  91.2 11.5 %copy-start.7 = (bf16[64,512]{1,0:T(8,128)(2,1)}, bf16[64,512]{1,0:T(8,128)(2,1)S(1)}, u32[]{:S(2)}) copy-start(bf16[64,512]{1,0:T(8,128)(2,1)S(1)} %collective-permute-done.3.rest_4_) | copy-start | bytes 196612
  91.2 11.5 %copy-start.8 = (bf16[64,512]{1,0:T(8,128)(2,1)}, bf16[64,512]{1,0:T(8,128)(2,1)S(1)}, u32[]{:S(2)}) copy-start(bf16[64,512]{1,0:T(8,128)(2,1)S(1)} %collective-permute-done.4.rest_5_) | copy-start | bytes 196612
  91.2 11.5 %copy-start.9 = (bf16[64,512]{1,0:T(8,128)(2,1)}, bf16[64,512]{1,0:T(8,128)(2,1)S(1)}, u32[]{:S(2)}) copy-start(bf16[64,512]{1,0:T(8,128)(2,1)S(1)} %collective-permute-done.5.rest_6_) | copy-start | bytes 196612
  91.3 11.4 %copy-start.10 = (bf16[64,512]{1,0:T(8,128)(2,1)}, bf16[64,512]{1,0:T(8,128)(2,1)S(1)}, u32[]{:S(2)}) copy-start(bf16[64,512]{1,0:T(8,128)(2,1)S(1)} %collective-permute-done.6.rest_7_) | copy-start | bytes 196612
  119.0 20.4 %copy-start.2 = (bf16[512,128]{1,0:T(8,128)(2,1)S(1)}, bf16[512,128]{1,0:T(8,128)(2,1)}, u32[]{:S(2)}) copy-start(bf16[512,128]{1,0:T(8,128)(2,1)} %weight_ref.1) | copy-start | bytes 393220
  119.0 20.4 %copy-start.3 = (f32[64,512]{1,0:T(8,128)S(1)}, f32[64,512]{1,0:T(8,128)}, u32[]{:S(2)}) copy-start(f32[64,512]{1,0:T(8,128)} %get-tuple-element.75) | copy-start | bytes 393220
  134.6 13.6 %all-to-all-start.5 = ((bf16[16,128,128]{2,1,0:T(8,128)(2,1)}), bf16[16,128,128]{2,1,0:T(8,128)(2,1)S(1)}, u32[]{:S(2)}, u32[]{:S(2)}) async-start(bf16[16,128,128]{2,1,0:T(8,128)(2,1)} %broadcast_in_dim.26), calls=%async_computation.5 | async-start | bytes 1048576 | tf_op jit(solution)/shard_map/all_to_all | solution.py:23

commit v9 on v8

--- a/solution.py
+++ b/solution.py
@@ -402,14 +402,15 @@
         grid_spec=pltpu.PrefetchScalarGridSpec(
             num_scalar_prefetch=1,
             grid=(1,),
-            in_specs=[whole(*arriving.shape), whole(*early.shape)] + [whole(own, deep)] * len(nodes),
+            in_specs=[pl.BlockSpec(memory_space=pltpu.VMEM), whole(*early.shape)]
+            + [whole(own, deep)] * len(nodes),
             out_specs=[whole(share, width), whole(blocks, height, width)],
         ),
         out_shape=[
             jax.ShapeDtypeStruct((share, width), jnp.bfloat16),
             jax.ShapeDtypeStruct((blocks, height, width), jnp.bfloat16),
         ],
-        compiler_params=pltpu.CompilerParams(vmem_limit_bytes=24 * 1024 * 1024),
+        compiler_params=pltpu.CompilerParams(vmem_limit_bytes=16 * 1024 * 1024),
         cost_estimate=pl.CostEstimate(
             flops=2 * share * deep * width, bytes_accessed=4 * 2**20, transcendentals=0
         ),
@@ -417,11 +418,27 @@
     )(turn, arriving, in_hbm(early), *map(in_hbm, nodes))
 
 
-def finish_body(node_scale, edge_scale, sums_ref, src_ref, dst_ref, one_ref, two_ref, three_ref, node_ref):
+def finish_body(
+    node_scale,
+    edge_scale,
+    sums_ref,
+    grad_dst_ref,
+    base_ref,
+    w_dst_ref,
+    grad_node_ref,
+    src_ref,
+    dst_ref,
+    one_ref,
+    two_ref,
+    three_ref,
+    node_ref,
+):
     blocks, height, width = sums_ref.shape
     deep = src_ref.shape[0]
     piece = deep // blocks
     extra = height - piece
+    value = base_ref[...] + dot_turned(grad_dst_ref[...], w_dst_ref[...])
+    grad_node_ref[...] = value.astype(jnp.bfloat16)
     for at in range(blocks):
         late = sums_ref[at, pl.ds(extra, piece), :].astype(jnp.float32)
         dst_ref[pl.ds(at * piece, piece), :] = late * node_scale
@@ -439,18 +456,20 @@
             node_ref[pl.ds(row, piece), pl.ds(slab * width, width)] = value * node_scale
 
 
-def finish(sums, deep, node_scale, edge_scale):
-    width = sums.shape[2]
+def finish(sums, own, base, w_dst, node_scale, edge_scale):
+    deep, width = w_dst.shape
     shapes = [(deep, width)] * 2 + [(width, width)] * 3 + [(width, deep)]
     return pl.pallas_call(
         functools.partial(finish_body, node_scale, edge_scale),
         grid=(1,),
-        in_specs=[pl.BlockSpec(memory_space=pltpu.VMEM)],
-        out_specs=[whole(*shape) for shape in shapes],
-        out_shape=[pltpu.HBM(shape, jnp.float32) for shape in shapes],
+        in_specs=[pl.BlockSpec(memory_space=pltpu.VMEM), whole(base.shape[0], width)]
+        + [whole(*base.shape), whole(deep, width)],
+        out_specs=[whole(*base.shape)] + [whole(*shape) for shape in shapes],
+        out_shape=[pltpu.HBM(base.shape, jnp.bfloat16)]
+        + [pltpu.HBM(shape, jnp.float32) for shape in shapes],
         compiler_params=pltpu.CompilerParams(vmem_limit_bytes=8 * 1024 * 1024),
         name="finish",
-    )(sums)
+    )(sums, own, in_hbm(base), in_hbm(w_dst))
 
 
 def shards(
@@ -516,8 +535,8 @@
     weights = jnp.broadcast_to(weights[None], (long, *weights.shape))
     packed = jnp.concatenate([partial.reshape(long, row_count, width), weights], axis=1)
     own = sum_first(exchange(packed, RING)).astype(bf16)
-    grad_node = (grad_node + dot_turned(own[:row_count], w_dst)).astype(bf16)
-    weights = finish(spread(own[row_count:], PLANE), deep, node_scale, edge_scale)
+    sums = spread(own[row_count:], PLANE)
+    grad_node, *weights = finish(sums, own, grad_node, w_dst, node_scale, edge_scale)
     return (
         node_out,
         edge_out.reshape(edge_in.shape),

time: 150 us -> 150 us (level)
  blocking collectives: 28.7 us -> 41.9 us
  waiting for transfers between devices: 45.7 us -> 37.8 us
  starting transfers between devices: 37.5 us -> 32.7 us
    all_to_all x2 -> x3, blocking collectives: 28.7 us -> 41.9 us  [exchange(): return lax.all_to_all(value, axes, 0, 0, tiled=True)]
    all_to_all x4 -> x3, waiting for transfers between devices: 44.8 us -> 36.8 us  [exchange(): return lax.all_to_all(value, axes, 0, 0, tiled=True)]
    all_to_all x4 -> x3, starting transfers between devices: 26.2 us -> 21.4 us  [exchange(): return lax.all_to_all(value, axes, 0, 0, tiled=True)]
  transfers between devices with their start and end apart: 11 -> 10, of which waited for: 6 -> 5; matrix products, arithmetic and copies ran while one was open for 1% -> 1% of each run, Pallas kernels for 8% -> 8%
where the time goes in v9:
time: 150 us; the launch traced here: 149 us
  blocking collectives  41.9 us (28%)
  waiting for transfers between devices  37.8 us (25%)
  Pallas kernels  32.7 us (22%)
  starting transfers between devices  32.7 us (22%)
  local copies, waits for them, and re-layouts  2 us (1%)
    all_to_all x3, blocking collectives, exchange(): return lax.all_to_all(value, axes, 0, 0, tiled=True)  41.9 us
    all_to_all x3, waiting for transfers between devices, exchange(): return lax.all_to_all(value, axes, 0, 0, tiled=True)  36.8 us
    all_to_all x3, starting transfers between devices, exchange(): return lax.all_to_all(value, axes, 0, 0, tiled=True)  21.4 us
    pallas_call x1, Pallas kernels, edge_chain(): pl.pallas_call(chain_body, grid_spec=pltpu.PrefetchScalarGridSpec(num_sca...  14.8 us
    ppermute x4, starting transfers between devices, shards(): nodes += [lax.ppermute(node_late, 'z', pairs) for pairs in turns[half:]]  7.95 us
    pallas_call x1, Pallas kernels, edge_side(): pl.pallas_call(functools.partial(side_body, 1.0 / math.sqrt(nbrs)), grid=...  6.94 us
    pallas_call x1, Pallas kernels, edge_prep(): pl.pallas_call(functools.partial(prep_body, 1.0 / math.sqrt(nbrs)), grid=...  5.26 us
    ppermute x3, starting transfers between devices, shards(): lax.ppermute(node_late, 'z', pairs)  3.39 us
  transfers between devices with their start and end apart: 10, of which 5 were waited for; matrix products, arithmetic and copies ran while one was open for 1% of the time, Pallas kernels for 8%

profile of v9, /device:TPU:8, one launch (start us, length us, event | category | flops | bytes accessed | tf_op | source)
XLA Modules:
  0.0 148.9 jit_solution(6688961127810333072)
XLA Ops:
  0.6 1.8 %project.1 = bf16[8,64,128]{2,1,0:T(8,128)(2,1)} custom-call(bf16[64,512]{1,0:T(8,128)(2,1)} %rest_0_, bf16[512,128]{1,0:T(8,128)(2,1)} %w_dst_ref.1), custom_call_target="tpu_custom_call" | custom-call | tf_op jit(solution)/shard_map/project/pallas_call | solution.py:88
  2.4 8.5 %all-to-all-start = ((bf16[8,64,128]{2,1,0:T(8,128)(2,1)}), bf16[8,64,128]{2,1,0:T(8,128)(2,1)S(1)}, u32[]{:S(2)}, u32[]{:S(2)}) async-start(bf16[8,64,128]{2,1,0:T(8,128)(2,1)} %project.1), calls=%async_computation | async-start | bytes 262144 | tf_op jit(solution)/shard_map/all_to_all | solution.py:23
  10.9 0.8 fusion.3
  11.7 0.1 reshape.49.place_ref
  11.8 8.2 %all-to-all-done = bf16[8,64,128]{2,1,0:T(8,128)(2,1)S(1)} async-done(((bf16[8,64,128]{2,1,0:T(8,128)(2,1)}), bf16[8,64,128]{2,1,0:T(8,128)(2,1)S(1)}, u32[]{:S(2)}, u32[]{:S(2)}) %all-to-all-start) | async-done | bytes 131104 | tf_op jit(solution)/shard_map/all_to_all | solution.py:23
  20.0 1.7 %broadcast_in_dim.11 = bf16[16,512,128]{2,1,0:T(8,128)(2,1)} broadcast(bf16[512,128]{1,0:T(8,128)(2,1)S(1)} %bitcast.16), dimensions={1,2} | broadcast | bytes 2228224 | tf_op jit(solution)/shard_map/broadcast_in_dim | solution.py:28
  21.7 7.5 %all-to-all-start.1 = ((bf16[16,512,128]{2,1,0:T(8,128)(2,1)}), bf16[16,512,128]{2,1,0:T(8,128)(2,1)S(1)}, u32[]{:S(2)}, u32[]{:S(2)}) async-start(bf16[16,512,128]{2,1,0:T(8,128)(2,1)} %broadcast_in_dim.11), calls=%async_computation.1 | async-start | bytes 4194304 | tf_op jit(solution)/shard_map/all_to_all | solution.py:23
  29.2 0.0 copy-done
  29.2 0.4 collective-permute-start
  29.7 0.7 collective-permute-start.1
  30.4 2.2 %collective-permute-start.2 = (bf16[64,512]{1,0:T(8,128)(2,1)S(1)}, bf16[64,512]{1,0:T(8,128)(2,1)S(1)}, u32[]{:S(2)}, u32[]{:S(2)}) collective-permute-start(bf16[64,512]{1,0:T(8,128)(2,1)S(1)} %copy-done), channel_id=1, source_target_pairs={{0,12},{4,16},{8,20},{12,24},{16,28},{20,0},{24,4},{28,8},{1,13},{... | collective-permute-start | bytes 196616 | tf_op jit(solution)/shard_map/ppermute | solution.py:505
  32.6 5.3 %edge_prep.1 = (f32[4096,128]{1,0:T(8,128)}, f32[4096,128]{1,0:T(8,128)}) custom-call(bf16[4096,128]{1,0:T(8,128)(2,1)} %bitcast.11, bf16[4096,128]{1,0:T(8,128)(2,1)} %bitcast.13, s32[64,64]{1,0:T(8,128)} %mask_ref.3, bf16[64,512]{1,0:T(8,128)(2,1)} %rest_0_, bf16[64,512]{1,0:T(8,128)(2,1)} %node_cot_ref.3, bf16[512,128]{1,0:T(8,128)(2,1)} %w_src_ref.3, ...), custom_call_target="tpu_custom_call" | custom-call | flops 268435456 | bytes 12582912 | tf_op jit(solution)/shard_map/edge_prep/pallas_call | solution.py:143
  37.9 0.0 collective-permute-done.rest_1_
  37.9 0.0 copy-start.2
  37.9 0.8 collective-permute-done.1.rest_2_
  38.7 0.1 collective-permute-done.2.rest_3_
  38.8 17.2 %all-to-all-done.1 = bf16[16,512,128]{2,1,0:T(8,128)(2,1)S(1)} async-done(((bf16[16,512,128]{2,1,0:T(8,128)(2,1)}), bf16[16,512,128]{2,1,0:T(8,128)(2,1)S(1)}, u32[]{:S(2)}, u32[]{:S(2)}) %all-to-all-start.1) | async-done | bytes 2097184 | tf_op jit(solution)/shard_map/all_to_all | solution.py:23
  56.0 14.8 %edge_chain.1 = (bf16[4096,128]{1,0:T(8,128)(2,1)}, bf16[4096,128]{1,0:T(8,128)(2,1)}, bf16[4096,128]{1,0:T(8,128)(2,1)}, bf16[4096,128]{1,0:T(8,128)(2,1)}, bf16[8192,128]{1,0:T(8,128)(2,1)}) custom-call(s32[4096]{0:T(1024)S(1)} %reshape.49.place_ref, bf16[8192,128]{1,0:T(8,128)(2,1)S(1)} %bitcast.9, f32[4096,128]{1,0:T(8,128)} %get-tuple-element.63.base_ref, ...), custom_call_target="tpu_custom_call" | custom-call | flops 536870912 | bytes 12582912 | tf_op jit(solution)/shard_map/edge_chain/pallas_call | solution.py:248
  70.8 0.0 copy-done.2
  70.8 0.0 copy-done.3
  70.8 0.0 copy-done.4
  70.9 0.0 copy-start.1
  70.9 5.4 %all-to-all-start.2 = ((bf16[16,512,128]{2,1,0:T(8,128)(2,1)}), bf16[16,512,128]{2,1,0:T(8,128)(2,1)S(1)}, u32[]{:S(2)}, u32[]{:S(2)}) async-start(bf16[16,512,128]{2,1,0:T(8,128)(2,1)} %bitcast.15), calls=%async_computation.2 | async-start | bytes 4194304 | tf_op jit(solution)/shard_map/all_to_all | solution.py:23
  76.3 0.0 copy-done.1
  76.3 0.9 collective-permute-start.3
  77.1 4.3 %collective-permute-start.4 = (bf16[64,512]{1,0:T(8,128)(2,1)S(1)}, bf16[64,512]{1,0:T(8,128)(2,1)S(1)}, u32[]{:S(2)}, u32[]{:S(2)}) collective-permute-start(bf16[64,512]{1,0:T(8,128)(2,1)S(1)} %copy-done.1), channel_id=1, source_target_pairs={{0,20},{4,24},{8,28},{12,0},{16,4},{20,8},{24,12},{28,16},{1,21},{... | collective-permute-start | bytes 196616 | tf_op jit(solution)/shard_map/ppermute | solution.py:515
  81.4 0.8 collective-permute-start.5
  82.2 2.0 %collective-permute-start.6 = (bf16[64,512]{1,0:T(8,128)(2,1)S(1)}, bf16[64,512]{1,0:T(8,128)(2,1)S(1)}, u32[]{:S(2)}, u32[]{:S(2)}) collective-permute-start(bf16[64,512]{1,0:T(8,128)(2,1)S(1)} %copy-done.1), channel_id=1, source_target_pairs={{0,28},{4,0},{8,4},{12,8},{16,12},{20,16},{24,20},{28,24},{1,29},{... | collective-permute-start | bytes 196616 | tf_op jit(solution)/shard_map/ppermute | solution.py:515
  84.2 6.9 %edge_side.1 = (bf16[4096,128]{1,0:T(8,128)(2,1)}, bf16[4096,128]{1,0:T(8,128)(2,1)}, bf16[1536,128]{1,0:T(8,128)(2,1)}, bf16[64,512]{1,0:T(8,128)(2,1)}, f32[64,512]{1,0:T(8,128)}) custom-call(bf16[4096,128]{1,0:T(8,128)(2,1)} %bitcast.12, bf16[4096,128]{1,0:T(8,128)(2,1)} %bitcast.14, s32[64,64]{1,0:T(8,128)} %mask_ref.3, ...), custom_call_target="tpu_custom_call" | custom-call | flops 671088640 | bytes 25165824 | tf_op jit(solution)/shard_map/edge_side/pallas_call | solution.py:354
  91.2 0.0 collective-permute-done.3.rest_4_
  91.2 0.0 copy-start.5
  91.2 0.0 collective-permute-done.4.rest_5_
  91.2 0.0 copy-start.6
  91.2 0.0 collective-permute-done.5.rest_6_
  91.2 0.0 copy-start.7
  91.2 0.0 collective-permute-done.6.rest_7_
  91.2 0.0 copy-start.8
  91.2 11.4 %all-to-all-done.2.arriving_ref = bf16[16,512,128]{2,1,0:T(8,128)(2,1)S(1)} async-done(((bf16[16,512,128]{2,1,0:T(8,128)(2,1)}), bf16[16,512,128]{2,1,0:T(8,128)(2,1)S(1)}, u32[]{:S(2)}, u32[]{:S(2)}) %all-to-all-start.2) | async-done | bytes 2097184 | tf_op jit(solution)/shard_map/all_to_all | solution.py:23
  102.7 0.0 copy-done.5
  102.7 0.0 copy-done.6
  102.7 2.0 %meet.1 = (bf16[512,128]{1,0:T(8,128)(2,1)S(1)}, bf16[16,128,128]{2,1,0:T(8,128)(2,1)S(1)}) custom-call(s32[1]{0:T(128)} %bitcast.5.turn_ref, bf16[16,512,128]{2,1,0:T(8,128)(2,1)S(1)} %all-to-all-done.2.arriving_ref, bf16[1536,128]{1,0:T(8,128)(2,1)} %get-tuple-element.84.early_ref, bf16[64,512]{1,0:T(8,128)(2,1)} %rest_0_, bf16[64,512]{1,0:T(8,128)(2,1)} %copy-done.2, ...), custom_call_target="tpu_custom_call" | custom-call | flops 67108864 | bytes 4194304 | tf_op jit(solution)/shard_map/meet/pallas_call | solution.py:400
  104.7 14.3 %all_to_all.30 = bf16[16,128,128]{2,1,0:T(8,128)(2,1)S(1)} all-to-all(bf16[16,128,128]{2,1,0:T(8,128)(2,1)S(1)} %get-tuple-element.94), channel_id=1, replica_groups=mesh['cplx'=2,'y'=4,'z'=8,'x'=4] {'x','y'}, dimensions={0} | all-to-all | bytes 1048576 | tf_op jit(solution)/shard_map/all_to_all | solution.py:23
  119.0 0.1 reduce_sum.24
  119.1 14.3 %all_to_all.31 = bf16[8,192,128]{2,1,0:T(8,128)(2,1)S(1)} all-to-all(bf16[8,192,128]{2,1,0:T(8,128)(2,1)S(1)} %pad_maximum_fusion), channel_id=1, replica_groups=mesh['cplx'=2,'y'=4,'z'=8,'x'=4] {'z'}, dimensions={0} | all-to-all | bytes 786432 | tf_op jit(solution)/shard_map/all_to_all | solution.py:23
  133.4 0.1 reduce_sum.25.grad_dst_ref
  133.5 0.1 broadcast_in_dim.26
  133.6 13.3 %all_to_all.32.sums_ref = bf16[16,128,128]{2,1,0:T(8,128)(2,1)S(1)} all-to-all(bf16[16,128,128]{2,1,0:T(8,128)(2,1)S(1)} %broadcast_in_dim.26), channel_id=1, replica_groups=mesh['cplx'=2,'y'=4,'z'=8,'x'=4] {'x','y'}, dimensions={0} | all-to-all | bytes 1048576 | tf_op jit(solution)/shard_map/all_to_all | solution.py:23
  147.0 2.0 %finish.1 = (bf16[64,512]{1,0:T(8,128)(2,1)}, f32[512,128]{1,0:T(8,128)}, f32[512,128]{1,0:T(8,128)}, f32[128,128]{1,0:T(8,128)}, f32[128,128]{1,0:T(8,128)}, /*index=5*/f32[128,128]{1,0:T(8,128)}, f32[128,512]{1,0:T(8,128)}) custom-call(bf16[16,128,128]{2,1,0:T(8,128)(2,1)S(1)} %all_to_all.32.sums_ref, bf16[192,128]{1,0:T(8,128)(2,1)S(1)} %reduce_sum.25.grad_dst_ref, ...), custom_call_target="tpu_custom_call" | custom-call | tf_op jit(solution)/shard_map/finish/pallas_call | solution.py:462
  (8 shorter events, 0.1 us)
Async XLA Ops:
  2.4 17.6 %all-to-all-start = ((bf16[8,64,128]{2,1,0:T(8,128)(2,1)}), bf16[8,64,128]{2,1,0:T(8,128)(2,1)S(1)}, u32[]{:S(2)}, u32[]{:S(2)}) async-start(bf16[8,64,128]{2,1,0:T(8,128)(2,1)} %project.1), calls=%async_computation | async-start | bytes 262144 | tf_op jit(solution)/shard_map/all_to_all | solution.py:23
  21.7 7.5 %copy-start = (bf16[64,512]{1,0:T(8,128)(2,1)S(1)}, bf16[64,512]{1,0:T(8,128)(2,1)}, u32[]{:S(2)}) copy-start(bf16[64,512]{1,0:T(8,128)(2,1)} %rest_0_) | copy-start | bytes 196612
  21.7 34.3 %all-to-all-start.1 = ((bf16[16,512,128]{2,1,0:T(8,128)(2,1)}), bf16[16,512,128]{2,1,0:T(8,128)(2,1)S(1)}, u32[]{:S(2)}, u32[]{:S(2)}) async-start(bf16[16,512,128]{2,1,0:T(8,128)(2,1)} %broadcast_in_dim.11), calls=%async_computation.1 | async-start | bytes 4194304 | tf_op jit(solution)/shard_map/all_to_all | solution.py:23
  29.2 8.7 %collective-permute-start = (bf16[64,512]{1,0:T(8,128)(2,1)S(1)}, bf16[64,512]{1,0:T(8,128)(2,1)S(1)}, u32[]{:S(2)}, u32[]{:S(2)}) collective-permute-start(bf16[64,512]{1,0:T(8,128)(2,1)S(1)} %copy-done), channel_id=1, source_target_pairs={{0,4},{4,8},{8,12},{12,16},{16,20},{20,24},{24,28},{28,0},{1,5},{5... | collective-permute-start | bytes 196616 | tf_op jit(solution)/shard_map/ppermute | solution.py:505
  29.7 9.0 %collective-permute-start.1 = (bf16[64,512]{1,0:T(8,128)(2,1)S(1)}, bf16[64,512]{1,0:T(8,128)(2,1)S(1)}, u32[]{:S(2)}, u32[]{:S(2)}) collective-permute-start(bf16[64,512]{1,0:T(8,128)(2,1)S(1)} %copy-done), channel_id=1, source_target_pairs={{0,8},{4,12},{8,16},{12,20},{16,24},{20,28},{24,0},{28,4},{1,9},{5... | collective-permute-start | bytes 196616 | tf_op jit(solution)/shard_map/ppermute | solution.py:505
  30.4 8.4 %collective-permute-start.2 = (bf16[64,512]{1,0:T(8,128)(2,1)S(1)}, bf16[64,512]{1,0:T(8,128)(2,1)S(1)}, u32[]{:S(2)}, u32[]{:S(2)}) collective-permute-start(bf16[64,512]{1,0:T(8,128)(2,1)S(1)} %copy-done), channel_id=1, source_target_pairs={{0,12},{4,16},{8,20},{12,24},{16,28},{20,0},{24,4},{28,8},{1,13},{... | collective-permute-start | bytes 196616 | tf_op jit(solution)/shard_map/ppermute | solution.py:505
  37.9 32.9 %copy-start.2 = (bf16[64,512]{1,0:T(8,128)(2,1)}, bf16[64,512]{1,0:T(8,128)(2,1)S(1)}, u32[]{:S(2)}) copy-start(bf16[64,512]{1,0:T(8,128)(2,1)S(1)} %collective-permute-done.rest_1_) | copy-start | bytes 196612
  38.7 32.2 %copy-start.3 = (bf16[64,512]{1,0:T(8,128)(2,1)}, bf16[64,512]{1,0:T(8,128)(2,1)S(1)}, u32[]{:S(2)}) copy-start(bf16[64,512]{1,0:T(8,128)(2,1)S(1)} %collective-permute-done.1.rest_2_) | copy-start | bytes 196612
  38.8 32.0 %copy-start.4 = (bf16[64,512]{1,0:T(8,128)(2,1)}, bf16[64,512]{1,0:T(8,128)(2,1)S(1)}, u32[]{:S(2)}) copy-start(bf16[64,512]{1,0:T(8,128)(2,1)S(1)} %collective-permute-done.2.rest_3_) | copy-start | bytes 196612
  70.9 5.4 %copy-start.1 = (bf16[64,512]{1,0:T(8,128)(2,1)S(1)}, bf16[64,512]{1,0:T(8,128)(2,1)}, u32[]{:S(2)}) copy-start(bf16[64,512]{1,0:T(8,128)(2,1)} %rest_0_) | copy-start | bytes 196612
  70.9 31.8 %all-to-all-start.2 = ((bf16[16,512,128]{2,1,0:T(8,128)(2,1)}), bf16[16,512,128]{2,1,0:T(8,128)(2,1)S(1)}, u32[]{:S(2)}, u32[]{:S(2)}) async-start(bf16[16,512,128]{2,1,0:T(8,128)(2,1)} %bitcast.15), calls=%async_computation.2 | async-start | bytes 4194304 | tf_op jit(solution)/shard_map/all_to_all | solution.py:23
  76.3 14.9 %collective-permute-start.3 = (bf16[64,512]{1,0:T(8,128)(2,1)S(1)}, bf16[64,512]{1,0:T(8,128)(2,1)S(1)}, u32[]{:S(2)}, u32[]{:S(2)}) collective-permute-start(bf16[64,512]{1,0:T(8,128)(2,1)S(1)} %copy-done.1), channel_id=1, source_target_pairs={{0,16},{4,20},{8,24},{12,28},{16,0},{20,4},{24,8},{28,12},{1,17},{... | collective-permute-start | bytes 196616 | tf_op jit(solution)/shard_map/ppermute | solution.py:515
  77.1 14.0 %collective-permute-start.4 = (bf16[64,512]{1,0:T(8,128)(2,1)S(1)}, bf16[64,512]{1,0:T(8,128)(2,1)S(1)}, u32[]{:S(2)}, u32[]{:S(2)}) collective-permute-start(bf16[64,512]{1,0:T(8,128)(2,1)S(1)} %copy-done.1), channel_id=1, source_target_pairs={{0,20},{4,24},{8,28},{12,0},{16,4},{20,8},{24,12},{28,16},{1,21},{... | collective-permute-start | bytes 196616 | tf_op jit(solution)/shard_map/ppermute | solution.py:515
  81.4 9.8 %collective-permute-start.5 = (bf16[64,512]{1,0:T(8,128)(2,1)S(1)}, bf16[64,512]{1,0:T(8,128)(2,1)S(1)}, u32[]{:S(2)}, u32[]{:S(2)}) collective-permute-start(bf16[64,512]{1,0:T(8,128)(2,1)S(1)} %copy-done.1), channel_id=1, source_target_pairs={{0,24},{4,28},{8,0},{12,4},{16,8},{20,12},{24,16},{28,20},{1,25},{... | collective-permute-start | bytes 196616 | tf_op jit(solution)/shard_map/ppermute | solution.py:515
  82.2 9.0 %collective-permute-start.6 = (bf16[64,512]{1,0:T(8,128)(2,1)S(1)}, bf16[64,512]{1,0:T(8,128)(2,1)S(1)}, u32[]{:S(2)}, u32[]{:S(2)}) collective-permute-start(bf16[64,512]{1,0:T(8,128)(2,1)S(1)} %copy-done.1), channel_id=1, source_target_pairs={{0,28},{4,0},{8,4},{12,8},{16,12},{20,16},{24,20},{28,24},{1,29},{... | collective-permute-start | bytes 196616 | tf_op jit(solution)/shard_map/ppermute | solution.py:515
  91.2 11.5 %copy-start.5 = (bf16[64,512]{1,0:T(8,128)(2,1)}, bf16[64,512]{1,0:T(8,128)(2,1)S(1)}, u32[]{:S(2)}) copy-start(bf16[64,512]{1,0:T(8,128)(2,1)S(1)} %collective-permute-done.3.rest_4_) | copy-start | bytes 196612
  91.2 11.5 %copy-start.6 = (bf16[64,512]{1,0:T(8,128)(2,1)}, bf16[64,512]{1,0:T(8,128)(2,1)S(1)}, u32[]{:S(2)}) copy-start(bf16[64,512]{1,0:T(8,128)(2,1)S(1)} %collective-permute-done.4.rest_5_) | copy-start | bytes 196612
  91.2 11.5 %copy-start.7 = (bf16[64,512]{1,0:T(8,128)(2,1)}, bf16[64,512]{1,0:T(8,128)(2,1)S(1)}, u32[]{:S(2)}) copy-start(bf16[64,512]{1,0:T(8,128)(2,1)S(1)} %collective-permute-done.5.rest_6_) | copy-start | bytes 196612
  91.2 11.5 %copy-start.8 = (bf16[64,512]{1,0:T(8,128)(2,1)}, bf16[64,512]{1,0:T(8,128)(2,1)S(1)}, u32[]{:S(2)}) copy-start(bf16[64,512]{1,0:T(8,128)(2,1)S(1)} %collective-permute-done.6.rest_7_) | copy-start | bytes 196612

commit v10 on v8

--- a/solution.py
+++ b/solution.py
@@ -379,12 +379,12 @@
     for at in range(1, blocks):
         value = value + arriving_ref[at].astype(f32)
     partial_ref[...] = value.astype(bf16)
-    late = None
-    for shift, node_ref in enumerate(node_refs):
+    terms = []
+    for shift in range(count):
         place = lax.rem(turn_ref[0] + (count - shift), count)
-        rows = pl.ds(pl.multiple_of(place * own, own), own)
-        term = dot_rows(node_ref[...], partial_ref[rows, :])
-        late = term if late is None else late + term
+        terms.append(partial_ref[pl.ds(pl.multiple_of(place * own, own), own), :])
+    nodes = jnp.concatenate([node_ref[...] for node_ref in node_refs], axis=0)
+    late = dot_rows(nodes, jnp.concatenate(terms, axis=0))
     late = late.astype(bf16)
     piece = late.shape[0] // blocks
     extra = early_ref.shape[0] // blocks
@@ -402,14 +402,15 @@
         grid_spec=pltpu.PrefetchScalarGridSpec(
             num_scalar_prefetch=1,
             grid=(1,),
-            in_specs=[whole(*arriving.shape), whole(*early.shape)] + [whole(own, deep)] * len(nodes),
+            in_specs=[pl.BlockSpec(memory_space=pltpu.VMEM), whole(*early.shape)]
+            + [whole(own, deep)] * len(nodes),
             out_specs=[whole(share, width), whole(blocks, height, width)],
         ),
         out_shape=[
             jax.ShapeDtypeStruct((share, width), jnp.bfloat16),
             jax.ShapeDtypeStruct((blocks, height, width), jnp.bfloat16),
         ],
-        compiler_params=pltpu.CompilerParams(vmem_limit_bytes=24 * 1024 * 1024),
+        compiler_params=pltpu.CompilerParams(vmem_limit_bytes=16 * 1024 * 1024),
         cost_estimate=pl.CostEstimate(
             flops=2 * share * deep * width, bytes_accessed=4 * 2**20, transcendentals=0
         ),

time: 150 us -> 150 us (level)
  no operation moved by 1% of the time
where the time goes in v10:
time: 150 us; the launch traced here: 149 us
  waiting for transfers between devices  45.7 us (30%)
  starting transfers between devices  37.5 us (25%)
  Pallas kernels  31.7 us (21%)
  blocking collectives  28.7 us (19%)
  local copies, waits for them, and re-layouts  2.82 us (2%)
    all_to_all x4, waiting for transfers between devices, exchange(): return lax.all_to_all(value, axes, 0, 0, tiled=True)  44.8 us
    all_to_all x2, blocking collectives, exchange(): return lax.all_to_all(value, axes, 0, 0, tiled=True)  28.7 us
    all_to_all x4, starting transfers between devices, exchange(): return lax.all_to_all(value, axes, 0, 0, tiled=True)  26.2 us
    pallas_call x1, Pallas kernels, edge_chain(): pl.pallas_call(chain_body, grid_spec=pltpu.PrefetchScalarGridSpec(num_sca...  14.8 us
    ppermute x4, starting transfers between devices, shards(): nodes += [lax.ppermute(node_late, 'z', pairs) for pairs in turns[half:]]  7.95 us
    pallas_call x1, Pallas kernels, edge_side(): pl.pallas_call(functools.partial(side_body, 1.0 / math.sqrt(nbrs)), grid=...  6.95 us
    pallas_call x1, Pallas kernels, edge_prep(): pl.pallas_call(functools.partial(prep_body, 1.0 / math.sqrt(nbrs)), grid=...  5.27 us
    ppermute x3, starting transfers between devices, shards(): lax.ppermute(node_late, 'z', pairs)  3.39 us
  transfers between devices with their start and end apart: 11, of which 6 were waited for; matrix products, arithmetic and copies ran while one was open for 1% of the time, Pallas kernels for 8%

profile of v10, /device:TPU:8, one launch (start us, length us, event | category | flops | bytes accessed | tf_op | source)
XLA Modules:
  0.0 149.1 jit_solution(12049227760511512776)
XLA Ops:
  0.6 1.8 %project.1 = bf16[8,64,128]{2,1,0:T(8,128)(2,1)} custom-call(bf16[64,512]{1,0:T(8,128)(2,1)} %rest_0_, bf16[512,128]{1,0:T(8,128)(2,1)} %weight_ref.1), custom_call_target="tpu_custom_call" | custom-call | tf_op jit(solution)/shard_map/project/pallas_call | solution.py:88
  2.4 8.5 %all-to-all-start = ((bf16[8,64,128]{2,1,0:T(8,128)(2,1)}), bf16[8,64,128]{2,1,0:T(8,128)(2,1)S(1)}, u32[]{:S(2)}, u32[]{:S(2)}) async-start(bf16[8,64,128]{2,1,0:T(8,128)(2,1)} %project.1), calls=%async_computation | async-start | bytes 262144 | tf_op jit(solution)/shard_map/all_to_all | solution.py:23
  10.9 0.8 fusion.4
  11.7 0.1 reshape.49.place_ref
  11.8 8.2 %all-to-all-done = bf16[8,64,128]{2,1,0:T(8,128)(2,1)S(1)} async-done(((bf16[8,64,128]{2,1,0:T(8,128)(2,1)}), bf16[8,64,128]{2,1,0:T(8,128)(2,1)S(1)}, u32[]{:S(2)}, u32[]{:S(2)}) %all-to-all-start) | async-done | bytes 131104 | tf_op jit(solution)/shard_map/all_to_all | solution.py:23
  20.0 1.7 %broadcast_in_dim.11 = bf16[16,512,128]{2,1,0:T(8,128)(2,1)} broadcast(bf16[512,128]{1,0:T(8,128)(2,1)S(1)} %bitcast.17), dimensions={1,2} | broadcast | bytes 2228224 | tf_op jit(solution)/shard_map/broadcast_in_dim | solution.py:28
  21.7 7.5 %all-to-all-start.1 = ((bf16[16,512,128]{2,1,0:T(8,128)(2,1)}), bf16[16,512,128]{2,1,0:T(8,128)(2,1)S(1)}, u32[]{:S(2)}, u32[]{:S(2)}) async-start(bf16[16,512,128]{2,1,0:T(8,128)(2,1)} %broadcast_in_dim.11), calls=%async_computation.1 | async-start | bytes 4194304 | tf_op jit(solution)/shard_map/all_to_all | solution.py:23
  29.2 0.4 collective-permute-start
  29.7 0.7 collective-permute-start.1
  30.4 2.2 %collective-permute-start.2 = (bf16[64,512]{1,0:T(8,128)(2,1)S(1)}, bf16[64,512]{1,0:T(8,128)(2,1)S(1)}, u32[]{:S(2)}, u32[]{:S(2)}) collective-permute-start(bf16[64,512]{1,0:T(8,128)(2,1)S(1)} %copy-done), channel_id=1, source_target_pairs={{0,12},{4,16},{8,20},{12,24},{16,28},{20,0},{24,4},{28,8},{1,13},{... | collective-permute-start | bytes 196616 | tf_op jit(solution)/shard_map/ppermute | solution.py:487
  32.6 5.3 %edge_prep.1 = (f32[4096,128]{1,0:T(8,128)}, f32[4096,128]{1,0:T(8,128)}) custom-call(bf16[4096,128]{1,0:T(8,128)(2,1)} %bitcast.12, bf16[4096,128]{1,0:T(8,128)(2,1)} %bitcast.14, s32[64,64]{1,0:T(8,128)} %mask_ref.3, bf16[64,512]{1,0:T(8,128)(2,1)} %rest_0_, bf16[64,512]{1,0:T(8,128)(2,1)} %node_cot_ref.3, bf16[512,128]{1,0:T(8,128)(2,1)} %w_src_ref.3, ...), custom_call_target="tpu_custom_call" | custom-call | flops 268435456 | bytes 12582912 | tf_op jit(solution)/shard_map/edge_prep/pallas_call | solution.py:143
  37.9 0.0 collective-permute-done.rest_1_
  37.9 0.0 copy-start.4
  37.9 0.8 collective-permute-done.1.rest_2_
  38.7 0.1 collective-permute-done.2.rest_3_
  38.8 17.2 %all-to-all-done.1 = bf16[16,512,128]{2,1,0:T(8,128)(2,1)S(1)} async-done(((bf16[16,512,128]{2,1,0:T(8,128)(2,1)}), bf16[16,512,128]{2,1,0:T(8,128)(2,1)S(1)}, u32[]{:S(2)}, u32[]{:S(2)}) %all-to-all-start.1) | async-done | bytes 2097184 | tf_op jit(solution)/shard_map/all_to_all | solution.py:23
  56.0 14.8 %edge_chain.1 = (bf16[4096,128]{1,0:T(8,128)(2,1)}, bf16[4096,128]{1,0:T(8,128)(2,1)}, bf16[4096,128]{1,0:T(8,128)(2,1)}, bf16[4096,128]{1,0:T(8,128)(2,1)}, bf16[8192,128]{1,0:T(8,128)(2,1)}) custom-call(s32[4096]{0:T(1024)S(1)} %reshape.49.place_ref, bf16[8192,128]{1,0:T(8,128)(2,1)S(1)} %bitcast.10, f32[4096,128]{1,0:T(8,128)} %get-tuple-element.62.base_ref, ...), custom_call_target="tpu_custom_call" | custom-call | flops 536870912 | bytes 12582912 | tf_op jit(solution)/shard_map/edge_chain/pallas_call | solution.py:248
  70.8 0.0 copy-done.4
  70.8 0.0 copy-done.5
  70.8 0.0 copy-done.6
  70.8 0.0 copy-start.1
  70.9 5.4 %all-to-all-start.2 = ((bf16[16,512,128]{2,1,0:T(8,128)(2,1)}), bf16[16,512,128]{2,1,0:T(8,128)(2,1)S(1)}, u32[]{:S(2)}, u32[]{:S(2)}) async-start(bf16[16,512,128]{2,1,0:T(8,128)(2,1)} %bitcast.16), calls=%async_computation.2 | async-start | bytes 4194304 | tf_op jit(solution)/shard_map/all_to_all | solution.py:23
  76.3 0.9 collective-permute-start.3
  77.1 4.3 %collective-permute-start.4 = (bf16[64,512]{1,0:T(8,128)(2,1)S(1)}, bf16[64,512]{1,0:T(8,128)(2,1)S(1)}, u32[]{:S(2)}, u32[]{:S(2)}) collective-permute-start(bf16[64,512]{1,0:T(8,128)(2,1)S(1)} %copy-done.1), channel_id=1, source_target_pairs={{0,20},{4,24},{8,28},{12,0},{16,4},{20,8},{24,12},{28,16},{1,21},{... | collective-permute-start | bytes 196616 | tf_op jit(solution)/shard_map/ppermute | solution.py:497
  81.5 0.7 collective-permute-start.5
  82.2 2.0 %collective-permute-start.6 = (bf16[64,512]{1,0:T(8,128)(2,1)S(1)}, bf16[64,512]{1,0:T(8,128)(2,1)S(1)}, u32[]{:S(2)}, u32[]{:S(2)}) collective-permute-start(bf16[64,512]{1,0:T(8,128)(2,1)S(1)} %copy-done.1), channel_id=1, source_target_pairs={{0,28},{4,0},{8,4},{12,8},{16,12},{20,16},{24,20},{28,24},{1,29},{... | collective-permute-start | bytes 196616 | tf_op jit(solution)/shard_map/ppermute | solution.py:497
  84.2 7.0 %edge_side.1 = (bf16[4096,128]{1,0:T(8,128)(2,1)}, bf16[4096,128]{1,0:T(8,128)(2,1)}, bf16[1536,128]{1,0:T(8,128)(2,1)}, bf16[64,512]{1,0:T(8,128)(2,1)}, f32[64,512]{1,0:T(8,128)}) custom-call(bf16[4096,128]{1,0:T(8,128)(2,1)} %bitcast.13, bf16[4096,128]{1,0:T(8,128)(2,1)} %bitcast.15, s32[64,64]{1,0:T(8,128)} %mask_ref.3, ...), custom_call_target="tpu_custom_call" | custom-call | flops 671088640 | bytes 25165824 | tf_op jit(solution)/shard_map/edge_side/pallas_call | solution.py:354
  91.2 0.0 collective-permute-done.3.rest_4_
  91.2 0.0 copy-start.7
  91.2 0.0 collective-permute-done.4.rest_5_
  91.2 0.0 copy-start.8
  91.2 0.0 collective-permute-done.5.rest_6_
  91.2 0.0 copy-start.9
  91.2 0.0 collective-permute-done.6.rest_7_
  91.3 0.0 copy-start.10
  91.3 11.4 %all-to-all-done.2.arriving_ref = bf16[16,512,128]{2,1,0:T(8,128)(2,1)S(1)} async-done(((bf16[16,512,128]{2,1,0:T(8,128)(2,1)}), bf16[16,512,128]{2,1,0:T(8,128)(2,1)S(1)}, u32[]{:S(2)}, u32[]{:S(2)}) %all-to-all-start.2) | async-done | bytes 2097184 | tf_op jit(solution)/shard_map/all_to_all | solution.py:23
  102.7 1.9 %meet.1 = (bf16[512,128]{1,0:T(8,128)(2,1)S(1)}, bf16[16,128,128]{2,1,0:T(8,128)(2,1)S(1)}) custom-call(s32[1]{0:T(128)} %bitcast.5.turn_ref, bf16[16,512,128]{2,1,0:T(8,128)(2,1)S(1)} %all-to-all-done.2.arriving_ref, bf16[1536,128]{1,0:T(8,128)(2,1)} %get-tuple-element.84.early_ref, bf16[64,512]{1,0:T(8,128)(2,1)} %rest_0_, bf16[64,512]{1,0:T(8,128)(2,1)} %copy-done.4, ...), custom_call_target="tpu_custom_call" | custom-call | flops 67108864 | bytes 4194304 | tf_op jit(solution)/shard_map/meet/pallas_call | solution.py:400
  104.6 14.3 %all_to_all.30 = bf16[16,128,128]{2,1,0:T(8,128)(2,1)S(1)} all-to-all(bf16[16,128,128]{2,1,0:T(8,128)(2,1)S(1)} %get-tuple-element.94), channel_id=1, replica_groups=mesh['cplx'=2,'y'=4,'z'=8,'x'=4] {'x','y'}, dimensions={0} | all-to-all | bytes 1048576 | tf_op jit(solution)/shard_map/all_to_all | solution.py:23
  118.9 0.1 reduce_sum.24
  118.9 0.0 copy-start.2
  118.9 0.0 copy-start.3
  119.0 14.5 %all_to_all.31 = bf16[8,192,128]{2,1,0:T(8,128)(2,1)S(1)} all-to-all(bf16[8,192,128]{2,1,0:T(8,128)(2,1)S(1)} %pad_maximum_fusion), channel_id=1, replica_groups=mesh['cplx'=2,'y'=4,'z'=8,'x'=4] {'z'}, dimensions={0} | all-to-all | bytes 786432 | tf_op jit(solution)/shard_map/all_to_all | solution.py:23
  133.5 0.1 reduce_sum.25
  133.6 0.9 broadcast_in_dim.26
  134.5 4.8 %all-to-all-start.5 = ((bf16[16,128,128]{2,1,0:T(8,128)(2,1)}), bf16[16,128,128]{2,1,0:T(8,128)(2,1)S(1)}, u32[]{:S(2)}, u32[]{:S(2)}) async-start(bf16[16,128,128]{2,1,0:T(8,128)(2,1)} %broadcast_in_dim.26), calls=%async_computation.5 | async-start | bytes 1048576 | tf_op jit(solution)/shard_map/all_to_all | solution.py:23
  139.3 0.8 fusion
  140.1 8.0 %all-to-all-done.5.sums_ref = bf16[16,128,128]{2,1,0:T(8,128)(2,1)S(1)} async-done(((bf16[16,128,128]{2,1,0:T(8,128)(2,1)}), bf16[16,128,128]{2,1,0:T(8,128)(2,1)S(1)}, u32[]{:S(2)}, u32[]{:S(2)}) %all-to-all-start.5) | async-done | bytes 524320 | tf_op jit(solution)/shard_map/all_to_all | solution.py:23
  148.1 1.0 finish.1
  (14 shorter events, 0.1 us)
Async XLA Ops:
  2.4 17.6 %all-to-all-start = ((bf16[8,64,128]{2,1,0:T(8,128)(2,1)}), bf16[8,64,128]{2,1,0:T(8,128)(2,1)S(1)}, u32[]{:S(2)}, u32[]{:S(2)}) async-start(bf16[8,64,128]{2,1,0:T(8,128)(2,1)} %project.1), calls=%async_computation | async-start | bytes 262144 | tf_op jit(solution)/shard_map/all_to_all | solution.py:23
  21.7 7.5 %copy-start = (bf16[64,512]{1,0:T(8,128)(2,1)S(1)}, bf16[64,512]{1,0:T(8,128)(2,1)}, u32[]{:S(2)}) copy-start(bf16[64,512]{1,0:T(8,128)(2,1)} %rest_0_) | copy-start | bytes 196612
  21.7 34.3 %all-to-all-start.1 = ((bf16[16,512,128]{2,1,0:T(8,128)(2,1)}), bf16[16,512,128]{2,1,0:T(8,128)(2,1)S(1)}, u32[]{:S(2)}, u32[]{:S(2)}) async-start(bf16[16,512,128]{2,1,0:T(8,128)(2,1)} %broadcast_in_dim.11), calls=%async_computation.1 | async-start | bytes 4194304 | tf_op jit(solution)/shard_map/all_to_all | solution.py:23
  29.2 8.7 %collective-permute-start = (bf16[64,512]{1,0:T(8,128)(2,1)S(1)}, bf16[64,512]{1,0:T(8,128)(2,1)S(1)}, u32[]{:S(2)}, u32[]{:S(2)}) collective-permute-start(bf16[64,512]{1,0:T(8,128)(2,1)S(1)} %copy-done), channel_id=1, source_target_pairs={{0,4},{4,8},{8,12},{12,16},{16,20},{20,24},{24,28},{28,0},{1,5},{5... | collective-permute-start | bytes 196616 | tf_op jit(solution)/shard_map/ppermute | solution.py:487
  29.7 9.0 %collective-permute-start.1 = (bf16[64,512]{1,0:T(8,128)(2,1)S(1)}, bf16[64,512]{1,0:T(8,128)(2,1)S(1)}, u32[]{:S(2)}, u32[]{:S(2)}) collective-permute-start(bf16[64,512]{1,0:T(8,128)(2,1)S(1)} %copy-done), channel_id=1, source_target_pairs={{0,8},{4,12},{8,16},{12,20},{16,24},{20,28},{24,0},{28,4},{1,9},{5... | collective-permute-start | bytes 196616 | tf_op jit(solution)/shard_map/ppermute | solution.py:487
  30.4 8.4 %collective-permute-start.2 = (bf16[64,512]{1,0:T(8,128)(2,1)S(1)}, bf16[64,512]{1,0:T(8,128)(2,1)S(1)}, u32[]{:S(2)}, u32[]{:S(2)}) collective-permute-start(bf16[64,512]{1,0:T(8,128)(2,1)S(1)} %copy-done), channel_id=1, source_target_pairs={{0,12},{4,16},{8,20},{12,24},{16,28},{20,0},{24,4},{28,8},{1,13},{... | collective-permute-start | bytes 196616 | tf_op jit(solution)/shard_map/ppermute | solution.py:487
  37.9 32.9 %copy-start.4 = (bf16[64,512]{1,0:T(8,128)(2,1)}, bf16[64,512]{1,0:T(8,128)(2,1)S(1)}, u32[]{:S(2)}) copy-start(bf16[64,512]{1,0:T(8,128)(2,1)S(1)} %collective-permute-done.rest_1_) | copy-start | bytes 196612
  38.7 32.1 %copy-start.5 = (bf16[64,512]{1,0:T(8,128)(2,1)}, bf16[64,512]{1,0:T(8,128)(2,1)S(1)}, u32[]{:S(2)}) copy-start(bf16[64,512]{1,0:T(8,128)(2,1)S(1)} %collective-permute-done.1.rest_2_) | copy-start | bytes 196612
  38.8 32.0 %copy-start.6 = (bf16[64,512]{1,0:T(8,128)(2,1)}, bf16[64,512]{1,0:T(8,128)(2,1)S(1)}, u32[]{:S(2)}) copy-start(bf16[64,512]{1,0:T(8,128)(2,1)S(1)} %collective-permute-done.2.rest_3_) | copy-start | bytes 196612
  70.8 5.4 %copy-start.1 = (bf16[64,512]{1,0:T(8,128)(2,1)S(1)}, bf16[64,512]{1,0:T(8,128)(2,1)}, u32[]{:S(2)}) copy-start(bf16[64,512]{1,0:T(8,128)(2,1)} %rest_0_) | copy-start | bytes 196612
  70.9 31.8 %all-to-all-start.2 = ((bf16[16,512,128]{2,1,0:T(8,128)(2,1)}), bf16[16,512,128]{2,1,0:T(8,128)(2,1)S(1)}, u32[]{:S(2)}, u32[]{:S(2)}) async-start(bf16[16,512,128]{2,1,0:T(8,128)(2,1)} %bitcast.16), calls=%async_computation.2 | async-start | bytes 4194304 | tf_op jit(solution)/shard_map/all_to_all | solution.py:23
  76.3 14.9 %collective-permute-start.3 = (bf16[64,512]{1,0:T(8,128)(2,1)S(1)}, bf16[64,512]{1,0:T(8,128)(2,1)S(1)}, u32[]{:S(2)}, u32[]{:S(2)}) collective-permute-start(bf16[64,512]{1,0:T(8,128)(2,1)S(1)} %copy-done.1), channel_id=1, source_target_pairs={{0,16},{4,20},{8,24},{12,28},{16,0},{20,4},{24,8},{28,12},{1,17},{... | collective-permute-start | bytes 196616 | tf_op jit(solution)/shard_map/ppermute | solution.py:497
  77.1 14.1 %collective-permute-start.4 = (bf16[64,512]{1,0:T(8,128)(2,1)S(1)}, bf16[64,512]{1,0:T(8,128)(2,1)S(1)}, u32[]{:S(2)}, u32[]{:S(2)}) collective-permute-start(bf16[64,512]{1,0:T(8,128)(2,1)S(1)} %copy-done.1), channel_id=1, source_target_pairs={{0,20},{4,24},{8,28},{12,0},{16,4},{20,8},{24,12},{28,16},{1,21},{... | collective-permute-start | bytes 196616 | tf_op jit(solution)/shard_map/ppermute | solution.py:497
  81.5 9.8 %collective-permute-start.5 = (bf16[64,512]{1,0:T(8,128)(2,1)S(1)}, bf16[64,512]{1,0:T(8,128)(2,1)S(1)}, u32[]{:S(2)}, u32[]{:S(2)}) collective-permute-start(bf16[64,512]{1,0:T(8,128)(2,1)S(1)} %copy-done.1), channel_id=1, source_target_pairs={{0,24},{4,28},{8,0},{12,4},{16,8},{20,12},{24,16},{28,20},{1,25},{... | collective-permute-start | bytes 196616 | tf_op jit(solution)/shard_map/ppermute | solution.py:497
  82.2 9.1 %collective-permute-start.6 = (bf16[64,512]{1,0:T(8,128)(2,1)S(1)}, bf16[64,512]{1,0:T(8,128)(2,1)S(1)}, u32[]{:S(2)}, u32[]{:S(2)}) collective-permute-start(bf16[64,512]{1,0:T(8,128)(2,1)S(1)} %copy-done.1), channel_id=1, source_target_pairs={{0,28},{4,0},{8,4},{12,8},{16,12},{20,16},{24,20},{28,24},{1,29},{... | collective-permute-start | bytes 196616 | tf_op jit(solution)/shard_map/ppermute | solution.py:497
  91.2 11.5 %copy-start.7 = (bf16[64,512]{1,0:T(8,128)(2,1)}, bf16[64,512]{1,0:T(8,128)(2,1)S(1)}, u32[]{:S(2)}) copy-start(bf16[64,512]{1,0:T(8,128)(2,1)S(1)} %collective-permute-done.3.rest_4_) | copy-start | bytes 196612
  91.2 11.5 %copy-start.8 = (bf16[64,512]{1,0:T(8,128)(2,1)}, bf16[64,512]{1,0:T(8,128)(2,1)S(1)}, u32[]{:S(2)}) copy-start(bf16[64,512]{1,0:T(8,128)(2,1)S(1)} %collective-permute-done.4.rest_5_) | copy-start | bytes 196612
  91.2 11.5 %copy-start.9 = (bf16[64,512]{1,0:T(8,128)(2,1)}, bf16[64,512]{1,0:T(8,128)(2,1)S(1)}, u32[]{:S(2)}) copy-start(bf16[64,512]{1,0:T(8,128)(2,1)S(1)} %collective-permute-done.5.rest_6_) | copy-start | bytes 196612
  91.3 11.4 %copy-start.10 = (bf16[64,512]{1,0:T(8,128)(2,1)}, bf16[64,512]{1,0:T(8,128)(2,1)S(1)}, u32[]{:S(2)}) copy-start(bf16[64,512]{1,0:T(8,128)(2,1)S(1)} %collective-permute-done.6.rest_7_) | copy-start | bytes 196612
  118.9 20.4 %copy-start.2 = (bf16[512,128]{1,0:T(8,128)(2,1)S(1)}, bf16[512,128]{1,0:T(8,128)(2,1)}, u32[]{:S(2)}) copy-start(bf16[512,128]{1,0:T(8,128)(2,1)} %weight_ref.1) | copy-start | bytes 393220
  118.9 20.4 %copy-start.3 = (f32[64,512]{1,0:T(8,128)S(1)}, f32[64,512]{1,0:T(8,128)}, u32[]{:S(2)}) copy-start(f32[64,512]{1,0:T(8,128)} %get-tuple-element.75) | copy-start | bytes 393220
  134.5 13.6 %all-to-all-start.5 = ((bf16[16,128,128]{2,1,0:T(8,128)(2,1)}), bf16[16,128,128]{2,1,0:T(8,128)(2,1)S(1)}, u32[]{:S(2)}, u32[]{:S(2)}) async-start(bf16[16,128,128]{2,1,0:T(8,128)(2,1)} %broadcast_in_dim.26), calls=%async_computation.5 | async-start | bytes 1048576 | tf_op jit(solution)/shard_map/all_to_all | solution.py:23
